TPU v7x, 128 devices: a whole 4x4x4 slice. The times are simulated.
128 devices in a mesh: dp: 4 (over x_hi, core), fsdp: 32 (over z, y, x_lo).
Axes of the slice: x: 4 (x_hi: 2, x_lo: 2; x = x_hi * 2 + x_lo), y: 4, z: 4, core: 2. Of those that a mesh axis runs over, the one named last changes fastest.
Arguments:
- xbc: bfloat16 [16384, 10240], P(('dp', 'fsdp')), may hold values from -6 to 6
- zgate: bfloat16 [16384, 8192], P(('dp', 'fsdp')), may hold values from -6 to 6
- dt_raw: float32 [16384, 128], P(('dp', 'fsdp')), may hold values from -5 to 5
- prompt_states: bfloat16 [32, 128, 64, 128], P(None, ('dp', 'fsdp')), may hold values from -3 to 3
- conv_tails: bfloat16 [32, 3, 10240], P(None, None, ('dp', 'fsdp')), may hold values from -6 to 6
- resp_prompt: int32 [512], replicated, may hold values from 0 to 31, as said below
- resp_lengths: int32 [128, 4], P(('dp', 'fsdp')), may hold values from 1 to 80, 128 in all within a row
- rewards: float32 [512], replicated, may hold values from -4 to 4
- upstream: bfloat16 [16384, 8192], P(('dp', 'fsdp')), may hold values from -6 to 6
- conv_weight: float32 [4, 10240], P(None, 'fsdp'), may hold values from -3 to 3
- conv_bias: float32 [10240], P('fsdp'), may hold values from -3 to 3
- dt_bias: float32 [128], P('fsdp'), may hold values from -3 to -1
- a_log: float32 [128], P('fsdp'), may hold values from -5 to -0.7
- d_skip: float32 [128], P('fsdp'), may hold values from 0.5 to 1.5
- norm_gain: float32 [8192], P('fsdp'), may hold values from 0.5 to 1.5
Outputs:
- grad_xbc: bfloat16 [16384, 10240], P(('dp', 'fsdp'))
- grad_zgate: bfloat16 [16384, 8192], P(('dp', 'fsdp'))
- grad_dt_raw: float32 [16384, 128], P(('dp', 'fsdp'))
- grad_prompt_states: float32 [32, 128, 64, 128], P(None, ('dp', 'fsdp'))
- grad_conv_tails: float32 [32, 3, 10240], P(None, None, ('dp', 'fsdp'))
- grad_conv_weight: float32 [4, 10240], P(None, 'fsdp')
- grad_conv_bias: float32 [10240], P('fsdp')
- grad_dt_bias: float32 [128], P('fsdp')
- grad_a_log: float32 [128], P('fsdp')
- grad_d_skip: float32 [128], P('fsdp')
- grad_norm_gain: float32 [8192], P('fsdp')
Inputs may be any that keep to these rules, and one draw needn't show every extreme that they name: `resp_prompt`: each of the 32 prompts is named by exactly 16 responses. `resp_lengths`: the 4 lengths of one device sum to 128.
All inputs are finite; a program needn't handle non-finite values.
Results may differ from a plain program's by a relative error of at most 0.0011.
Values may be sent and summed in bfloat16 or wider, within the bound.
No kernel may reach another device: no remote copies, remote signals or barrier semaphores. Data moves between devices by JAX's collectives and lax.ppermute only.
A program may use at most 192 MiB of HBM per device.

v0:
```python
import jax
import jax.numpy as jnp
from jax import lax
from jax.sharding import PartitionSpec as P

GROUP = 16
H = 128
P_SIZE = 64
N = 128
G = 8
GS = 2048


def advantages(rewards, resp_prompt, prompt_count):
    member = (resp_prompt[:, None] == jnp.arange(prompt_count, dtype=jnp.int32)[None, :]).astype(
        jnp.float32
    )
    group_mean = jnp.dot(rewards, member, precision=lax.Precision.HIGHEST) / GROUP
    centred = rewards - jnp.dot(member, group_mean, precision=lax.Precision.HIGHEST)
    spread = jnp.sqrt(jnp.dot(centred * centred, member, precision=lax.Precision.HIGHEST) / GROUP)
    return centred / jnp.dot(member, jnp.maximum(spread, 0.8), precision=lax.Precision.HIGHEST)


def token_layout(lengths, row_count):
    places = jnp.arange(row_count, dtype=jnp.int32)
    doc_ends = jnp.cumsum(lengths)
    doc_starts = doc_ends - lengths
    member = (places[:, None] >= doc_starts[None, :]) & (places[:, None] < doc_ends[None, :])
    start_tok = jnp.sum(jnp.where(member, doc_starts[None, :], 0), axis=1)
    return (member, start_tok, places - start_tok)


def conv_branch(signal, tail_rows, conv_w, conv_b, member, offset):
    row_count = signal.shape[0]
    summed = conv_w[3][None, :] * signal
    for delay_step in (1, 2, 3):
        lagged = jnp.concatenate(
            [jnp.zeros((delay_step, signal.shape[1]), jnp.float32), signal[:-delay_step]], axis=0
        )
        summed = (
            summed
            + jnp.where((offset >= delay_step)[:, None], lagged, 0.0)
            * conv_w[3 - delay_step][None, :]
        )
    tail_a = tail_rows[:, 0, :]
    tail_b = tail_rows[:, 1, :]
    tail_c = tail_rows[:, 2, :]
    w_zero = conv_w[0][None, :]
    w_one = conv_w[1][None, :]
    w_two = conv_w[2][None, :]
    lead_in = jnp.stack(
        [
            w_two * tail_c + w_one * tail_b + w_zero * tail_a,
            w_one * tail_c + w_zero * tail_b,
            w_zero * tail_c,
        ],
        axis=1,
    )
    select = (
        member[:, :, None]
        & (offset[:, None, None] == jnp.arange(3, dtype=jnp.int32)[None, None, :])
    ).astype(jnp.float32)
    summed = summed + jnp.dot(
        select.reshape(row_count, -1),
        lead_in.reshape(-1, signal.shape[1]),
        precision=lax.Precision.HIGHEST,
    )
    return jax.nn.silu(summed + conv_b[None, :])


def mixer_forward(signal, gate_in, dt_in, states, tail_rows, params, member, start_tok, offset):
    conv_w, conv_b, bias_dt, log_rate, skip_all, gain = params
    row_count = signal.shape[0]
    doc_count = states.shape[0]
    inner = H * P_SIZE
    per_group = H // G
    conv_out = conv_branch(signal, tail_rows, conv_w, conv_b, member, offset)
    x_heads = conv_out[:, :inner].reshape(row_count, G, per_group, P_SIZE).transpose(1, 0, 2, 3)
    b_all = conv_out[:, inner : inner + G * N].reshape(row_count, G, N).transpose(1, 0, 2)
    c_all = conv_out[:, inner + G * N :].reshape(row_count, G, N).transpose(1, 0, 2)
    step_size = jax.nn.softplus(dt_in + bias_dt[None, :])
    decay_log = -step_size * jnp.exp(log_rate)[None, :]
    cum_log = jnp.cumsum(decay_log, axis=0)
    base_log = jnp.take(cum_log - decay_log, start_tok, axis=0)
    rel_log = cum_log - base_log
    places = jnp.arange(row_count, dtype=jnp.int32)
    causal = (start_tok[:, None] == start_tok[None, :]) & (places[:, None] >= places[None, :])
    member_f = member.astype(jnp.float32)

    def by_group(table):
        return table.reshape(row_count, G, per_group).transpose(1, 0, 2)

    start_all = states.reshape(doc_count, G, per_group, P_SIZE, N).transpose(1, 0, 2, 3, 4)

    def group_mix(items):
        c_rows, b_rows, x_rows, steps_g, cum_g, rel_g, start_state, skip_gain = items
        scores = jnp.dot(c_rows, b_rows.T, precision=lax.Precision.HIGHEST)
        log_gaps = cum_g.T[:, :, None] - cum_g.T[:, None, :]
        decays = jnp.exp(jnp.where(causal[None], log_gaps, -jnp.inf))
        weights = decays * scores[None] * steps_g.T[:, None, :]
        within = jnp.einsum("kts,skp->tkp", weights, x_rows, precision=lax.Precision.HIGHEST)
        c_masked = member_f[:, :, None] * c_rows[:, None, :]
        carried = jnp.einsum(
            "tdn,dkpn->tkp", c_masked, start_state, precision=lax.Precision.HIGHEST
        )
        carried = carried * jnp.exp(rel_g)[:, :, None]
        return within + carried + skip_gain[None, :, None] * x_rows

    mixed_out = lax.map(
        jax.checkpoint(group_mix),
        (
            c_all,
            b_all,
            x_heads,
            by_group(step_size),
            by_group(cum_log),
            by_group(rel_log),
            start_all,
            skip_all.reshape(G, per_group),
        ),
    )
    mixed_out = mixed_out.transpose(1, 0, 2, 3).reshape(row_count, inner)
    gated_out = mixed_out * jax.nn.silu(gate_in)
    grouped = gated_out.reshape(row_count, inner // GS, GS)
    inv_rms = lax.rsqrt(jnp.mean(grouped * grouped, axis=-1, keepdims=True) + 1e-05)
    return (grouped * inv_rms).reshape(row_count, inner) * gain[None, :]


def local_grads(
    signal_in, gate_in, dt_in, states, tail_rows, params, lengths, upstream, doc_weight
):
    member, start_tok, offset = token_layout(lengths, signal_in.shape[0])
    tok_weight = jnp.sum(jnp.where(member, doc_weight[None, :], 0.0), axis=1)

    def forward(signal, gate_vals, dt_vals, state_vals, tail_vals, weight_vals):
        return mixer_forward(
            signal,
            gate_vals,
            dt_vals,
            state_vals,
            tail_vals,
            weight_vals,
            member,
            start_tok,
            offset,
        )

    primal_out, pullback = jax.vjp(
        forward,
        signal_in.astype(jnp.float32),
        gate_in.astype(jnp.float32),
        dt_in,
        states.astype(jnp.float32),
        tail_rows.astype(jnp.float32),
        params,
    )
    return pullback(upstream.astype(jnp.float32) * tok_weight[:, None])


def shards(
    xbc,
    zgate,
    dt_raw,
    prompt_states,
    conv_tails,
    resp_prompt,
    resp_lengths,
    rewards,
    upstream,
    conv_weight,
    conv_bias,
    dt_bias,
    a_log,
    d_skip,
    norm_gain,
):
    dp_count = lax.axis_size("dp")
    fsdp_count = lax.axis_size("fsdp")
    holders = dp_count * fsdp_count
    holder = lax.axis_index(("dp", "fsdp"))
    params = (
        lax.all_gather(conv_weight, "fsdp", axis=1, tiled=True),
        lax.all_gather(conv_bias, "fsdp", axis=0, tiled=True),
        lax.all_gather(dt_bias, "fsdp", axis=0, tiled=True),
        lax.all_gather(a_log, "fsdp", axis=0, tiled=True),
        lax.all_gather(d_skip, "fsdp", axis=0, tiled=True),
        lax.all_gather(norm_gain, "fsdp", axis=0, tiled=True),
    )
    doc_count = resp_lengths.shape[1]
    lengths = resp_lengths[0]
    prompt_count = prompt_states.shape[0]
    head_share = prompt_states.shape[1]
    chan_share = conv_tails.shape[2]
    responses = holders * doc_count
    state_rows = prompt_states[resp_prompt]
    tail_sent = conv_tails[resp_prompt]
    got_states, got_tails = (
        lax.all_to_all(
            state_rows.reshape(holders, doc_count, 1, head_share, P_SIZE, N),
            ("dp", "fsdp"),
            split_axis=0,
            concat_axis=2,
            tiled=True,
        ),
        lax.all_to_all(
            tail_sent.reshape(holders, doc_count, 1, 3, chan_share),
            ("dp", "fsdp"),
            split_axis=0,
            concat_axis=2,
            tiled=True,
        ),
    )
    states = got_states.reshape(doc_count, holders * head_share, P_SIZE, N)
    tail_rows = (
        got_tails.reshape(doc_count, holders, 3, chan_share)
        .transpose(0, 2, 1, 3)
        .reshape(doc_count, 3, holders * chan_share)
    )
    advantage = advantages(rewards, resp_prompt, prompt_count)
    row_count = xbc.shape[0]
    doc_weight = lax.dynamic_slice_in_dim(advantage, holder * doc_count, doc_count) * (
        row_count / (doc_count * lengths.astype(jnp.float32))
    )
    gradients = local_grads(
        xbc, zgate, dt_raw, states, tail_rows, params, lengths, upstream, doc_weight
    )
    grad_x, grad_z, grad_dt, grad_state, grad_tail, grad_param = gradients
    tail_back = grad_tail.reshape(doc_count, 3, holders, chan_share).transpose(0, 2, 1, 3)
    back_state, back_tail = (
        lax.all_to_all(
            grad_state.reshape(1, doc_count, holders, head_share, P_SIZE, N),
            ("dp", "fsdp"),
            split_axis=2,
            concat_axis=0,
            tiled=True,
        ),
        lax.all_to_all(
            tail_back.reshape(1, doc_count, holders, 3, chan_share),
            ("dp", "fsdp"),
            split_axis=2,
            concat_axis=0,
            tiled=True,
        ),
    )
    prompt_onehot = (
        jnp.arange(prompt_count, dtype=jnp.int32)[:, None] == resp_prompt[None, :]
    ).astype(jnp.float32)
    grad_states_out = jnp.dot(
        prompt_onehot,
        back_state.reshape(responses, head_share * P_SIZE * N),
        precision=lax.Precision.HIGHEST,
    ).reshape(prompt_count, head_share, P_SIZE, N)
    grad_tails_out = jnp.dot(
        prompt_onehot, back_tail.reshape(responses, 3 * chan_share), precision=lax.Precision.HIGHEST
    ).reshape(prompt_count, 3, chan_share)
    shares = (
        lax.psum_scatter(grad_param[0], "fsdp", scatter_dimension=1, tiled=True),
        lax.psum_scatter(grad_param[1], "fsdp", scatter_dimension=0, tiled=True),
        lax.psum_scatter(grad_param[2], "fsdp", scatter_dimension=0, tiled=True),
        lax.psum_scatter(grad_param[3], "fsdp", scatter_dimension=0, tiled=True),
        lax.psum_scatter(grad_param[4], "fsdp", scatter_dimension=0, tiled=True),
        lax.psum_scatter(grad_param[5], "fsdp", scatter_dimension=0, tiled=True),
    )
    totals = lax.psum(shares, "dp")
    return (
        grad_x.astype(jnp.bfloat16),
        grad_z.astype(jnp.bfloat16),
        grad_dt,
        grad_states_out,
        grad_tails_out,
        totals[0],
        totals[1],
        totals[2],
        totals[3],
        totals[4],
        totals[5],
    )


def solution(mesh):
    return jax.shard_map(
        shards,
        mesh=mesh,
        in_specs=(
            P(("dp", "fsdp"), None),
            P(("dp", "fsdp"), None),
            P(("dp", "fsdp"), None),
            P(None, ("dp", "fsdp"), None, None),
            P(None, None, ("dp", "fsdp")),
            P(),
            P(("dp", "fsdp"), None),
            P(),
            P(("dp", "fsdp"), None),
            P(None, "fsdp"),
            P("fsdp"),
            P("fsdp"),
            P("fsdp"),
            P("fsdp"),
            P("fsdp"),
        ),
        out_specs=(
            P(("dp", "fsdp"), None),
            P(("dp", "fsdp"), None),
            P(("dp", "fsdp"), None),
            P(None, ("dp", "fsdp"), None, None),
            P(None, None, ("dp", "fsdp")),
            P(None, "fsdp"),
            P("fsdp"),
            P("fsdp"),
            P("fsdp"),
            P("fsdp"),
            P("fsdp"),
        ),
        check_vma=False,
    )
```

profile of v0, /device:TPU:1, one launch (start us, length us, event | category | flops | bytes accessed | tf_op | source)
XLA Modules:
  0.0 1460.1 jit_solution(7315456346505911198)
XLA Ops:
  8.1 3.6 gather_fusion
  12.5 11.9 all-to-all-start
  34.3 131.6 %all-reduce.29 = (f32[10240]{0:T(1024)}, f32[128]{0:T(128)S(1)}, f32[128]{0:T(128)S(1)}, f32[128]{0:T(128)}) all-reduce(f32[10240]{0:T(1024)S(1)} %dynamic-update-slice, f32[128]{0:T(128)S(1)} %dynamic-update-slice.1, f32[128]{0:T(128)S(1)} %dynamic-update-slice.2, f32[128]{0:T(128)S(1)} %dynamic-update-slice.3), channel_id=1, replica_groups=mesh['dp'=4,'fsdp'=32] {'fsdp'}, use_global_device_ids=true, to_apply=%add.19 | all-reduce | flops 10624 | bytes 84992
  179.1 13.5 gather_fusion.2
  193.3 32.9 %all-to-all-start.1 = ((bf16[128,4,1,1,64,128]{5,4,1,3,2,0:T(8,128)(2,1)}), bf16[128,4,1,1,64,128]{5,4,1,3,2,0:T(8,128)(2,1)}, u32[]{:S(2)}, u32[]{:S(2)}) async-start(bf16[128,4,1,1,64,128]{5,4,1,3,2,0:T(8,128)(2,1)} %bitcast.488), calls=%async_computation.1 | async-start | bytes 16777216 | tf_op jit(solution)/shard_map/all_to_all | solution.py:198
  226.2 156.9 %all-gather = f32[32,320,4]{1,2,0:T(4,128)S(1)} all-gather(f32[1,320,4]{1,2,0:T(4,128)S(1)} %bitcast.536), channel_id=1, replica_groups=mesh['dp'=4,'fsdp'=32] {'fsdp'}, dimensions={0}, use_global_device_ids=true | all-gather | bytes 168960 | tf_op jit(solution)/shard_map/all_gather | solution.py:182
  384.8 4.1 copy.83
  388.9 4.1 copy.82
  394.3 63.0 %all-gather.1 = f32[32,1,256]{2,1,0:T(1,128)S(1)} all-gather(f32[1,1,256]{2,1,0:T(1,128)S(1)} %bitcast.541), channel_id=1, replica_groups=mesh['dp'=4,'fsdp'=32] {'fsdp'}, dimensions={0}, use_global_device_ids=true | all-gather | bytes 33792 | tf_op jit(solution)/shard_map/all_gather | solution.py:187
  465.9 12.7 fusion.99
  483.4 5.6 copy.78
  491.3 11.4 bitcast_convert_fusion
  505.2 88.9 %while.41 = (s32[]{:T(128)}, f32[8,128,16,64]{1,3,2,0:T(8,128)}, f32[8,128,16,64]{1,3,2,0:T(8,128)}, f32[8,128,16]{1,2,0:T(8,128)S(1)}, f32[8,128,128]{2,1,0:T(8...) while((s32[]{:T(128)}, f32[8,128,16,64]{1,3,2,0:T(8,128)}, ...), condition=%wide.region_5.6_spmd.clone, body=%wide.region_4.5_spmd.clone.sunk | while | flops 1033439232 | bytes 5282625 | solution.py:109
  506.8 3.5 fusion.212
  512.1 4.2 fusion.215
  517.8 3.5 fusion.212
  523.2 4.2 fusion.215
  529.0 3.5 fusion.212
  534.3 4.2 fusion.215
  540.1 3.5 fusion.212
  545.4 4.2 fusion.215
  551.2 3.5 fusion.212
  556.5 4.2 fusion.215
  562.3 3.5 fusion.212
  567.6 4.3 fusion.215
  573.5 3.5 fusion.212
  578.8 4.2 fusion.215
  584.6 3.5 fusion.212
  589.9 4.2 fusion.215
  594.1 4.6 bitcast_reduce_fusion.1
  600.0 7.0 fusion.105
  612.4 7.9 broadcast_in_dim.266
  620.9 177.1 %while.42 = (s32[]{:T(128)}, f32[8,128,128]{2,1,0:T(8,128)}, f32[8,128,128]{2,1,0:T(8,128)}, f32[8,128,16,64]{1,3,2,0:T(8,128)}, f32[8,128,16]{1,2,0:T(8,128)S(1...) while((s32[]{:T(128)}, f32[8,128,128]{2,1,0:T(8,128)}, ...), condition=%wide.region_16.17_spmd.clone, body=%wide.region_8.16_spmd.clone.sunk | while | flops 2899869696 | bytes 19416704 | solution.py:109
  660.4 3.2 bitcast_dynamic-update-slice_fusion.11
  704.6 3.3 bitcast_dynamic-update-slice_fusion.11
  797.9 5.6 copy.86
  805.8 12.1 fusion.145
  825.8 49.9 %all_to_all.51 = f32[1,4,128,3,80]{4,1,3,0,2:T(4,128)S(1)} all-to-all(f32[1,4,128,3,80]{4,1,3,0,2:T(4,128)S(1)} %copy.96), channel_id=1, replica_groups=mesh['dp'=4,'fsdp'=32] {'dp','fsdp'}, dimensions={2} | all-to-all | bytes 983040 | tf_op jit(solution)/shard_map/all_to_all | solution.py:237
  875.8 5.8 all-to-all-start.2
  889.7 3.3 copy.107
  893.1 3.6 fusion.94
  901.6 4.1 copy.99
  905.7 288.3 %all-reduce.33.cloned.1.call-done = (f32[10240]{0:T(1024)}, f32[128]{0:T(128)}, f32[128]{0:T(128)}, f32[128]{0:T(128)}, f32[8192]{0:T(1024)}) async-done(((f32[10240]{0:T(1024)}, f32[128]{0:T(128)}, f32[128]{0:T(128)}, f32[128]{0:T(128)}, f32[8192]{0:T(1024)}), (f32[10240]{0:T(1024)}, f32[128]{0:T(128)}, f32[128]{0:T(128)}, f32[128]{0:T(128)}, f32[8192]{0:T(1024)})) %all-reduce.33.cloned.1.call-update) | async-done | bytes 75280
  1197.6 166.5 %reduce-scatter.4.cloned.1.call-done = f32[320,4]{1,0:T(8,128)} async-done(((f32[10240,4]{1,0:T(8,128)}), f32[320,4]{1,0:T(8,128)}) %reduce-scatter.4.cloned.1.call-update) | async-done | bytes 5136
  1365.1 34.9 %all-reduce.30 = (f32[4,320]{1,0:T(4,128)}, f32[320]{0:T(512)}, f32[4]{0:T(128)}, f32[4]{0:T(128)}, f32[4]{0:T(128)}, /*index=5*/f32[256]{0:T(256)}) all-reduce(f32[4,320]{1,0:T(4,128)S(1)} %copy.108, f32[320]{0:T(512)S(1)} %dynamic-slice.5, f32[4]{0:T(128)S(1)} %dynamic-slice.7, ...), channel_id=1, replica_groups=mesh['dp'=4,'fsdp'=32] {'dp'}, use_global_device_ids=true, to_apply=%region_30.31 | all-reduce | flops 1868 | bytes 14944 | tf_op jit(solution)/shard_map/psum | solution.py:264
  1401.8 20.1 %copy.121 = f32[64,8,64,128]{3,1,2,0:T(8,128)} copy(f32[64,8,64,128]{3,2,1,0:T(8,128)} %bitcast.181) | data formatting | bytes 33554432
  1421.9 17.5 %copy.90 = f32[8192,512]{1,0:T(8,128)} copy(f32[8192,512]{0,1:T(8,128)} %bitcast.486) | data formatting | bytes 33554432 | tf_op jit(solution)/shard_map/dot_general | solution.py:248
  1439.4 11.9 convolution_bitcast_fusion.6
  (426 shorter events, 279.1 us)
Async XLA Ops:
  7.2 171.9 %copy-start = (bf16[32,1,64,128]{3,2,1,0:T(8,128)(2,1)S(1)}, bf16[32,1,64,128]{3,2,1,0:T(8,128)(2,1)}, u32[]{:S(2)}) copy-start(bf16[32,1,64,128]{3,2,1,0:T(8,128)(2,1)} %param.22) | copy-start | bytes 1572868
  7.2 22.4 %copy-start.35 = (u32[128]{0:T(128)S(1)}, u32[128]{0:T(128)}, u32[]{:S(2)}) copy-start(u32[128]{0:T(128)} %constant.238) | copy-start | bytes 1540
  7.2 17.3 %copy-start.17 = (s32[512]{0:T(512)S(1)}, s32[512]{0:T(512)}, u32[]{:S(2)}) copy-start(s32[512]{0:T(512)} %param.24) | copy-start | bytes 6148
  7.2 26.8 %copy-start.36 = (f32[320]{0:T(512)S(1)}, f32[320]{0:T(512)}, u32[]{:S(2)}) copy-start(f32[320]{0:T(512)} %param.29) | copy-start | bytes 3844
  7.2 162.9 %copy-start.3 = (bf16[128,10240]{1,0:T(8,128)(2,1)S(1)}, bf16[128,10240]{1,0:T(8,128)(2,1)}, u32[]{:S(2)}) copy-start(bf16[128,10240]{1,0:T(8,128)(2,1)} %param.19) | copy-start | bytes 7864324
  8.1 159.9 %copy-start.19 = (s32[1024]{0:T(1024)}, s32[1024]{0:T(1024)S(1)}, u32[]{:S(2)}) copy-start(s32[1024]{0:T(1024)S(1)} %pad_clamp_fusion.1) | copy-start | bytes 12292
  12.5 180.7 %all-to-all-start = ((bf16[128,4,1,3,80]{4,1,3,2,0:T(4,128)(2,1)}), bf16[128,4,1,3,80]{4,1,3,2,0:T(4,128)(2,1)}, u32[]{:S(2)}, u32[]{:S(2)}) async-start(bf16[128,4,1,3,80]{4,1,3,2,0:T(4,128)(2,1)} %copy.71), calls=%async_computation | async-start | bytes 786432 | tf_op jit(solution)/shard_map/all_to_all | solution.py:205
  166.0 7.1 copy-start.25
  166.0 7.1 copy-start.43
  166.0 7.1 copy-start.27
  168.0 225.6 %copy-start.37 = (pred[128,4]{0,1:T(4,128)(4,1)}, pred[128,4]{0,1:T(4,128)(4,1)S(1)}, u32[]{:S(2)}) copy-start(pred[128,4]{0,1:T(4,128)(4,1)S(1)} %get-tuple-element.757) | copy-start | bytes 1540
  193.2 190.1 %copy-start.40 = (s32[128]{0:T(128)}, s32[128]{0:T(128)S(1)}, u32[]{:S(2)}) copy-start(s32[128]{0:T(128)S(1)} %fusion.142) | copy-start | bytes 1540
  193.2 33.0 %copy-start.23 = (f32[4,320]{1,0:T(4,128)S(1)}, f32[4,320]{1,0:T(4,128)}, u32[]{:S(2)}) copy-start(f32[4,320]{1,0:T(4,128)} %param.28) | copy-start | bytes 15364
  193.2 190.9 %copy-start.41 = (f32[128]{0:T(128)S(1)}, f32[128]{0:T(128)}, u32[]{:S(2)}) copy-start(f32[128]{0:T(128)} %get-tuple-element.746) | copy-start | bytes 1540
  193.3 298.1 %all-to-all-start.1 = ((bf16[128,4,1,1,64,128]{5,4,1,3,2,0:T(8,128)(2,1)}), bf16[128,4,1,1,64,128]{5,4,1,3,2,0:T(8,128)(2,1)}, u32[]{:S(2)}, u32[]{:S(2)}) async-start(bf16[128,4,1,1,64,128]{5,4,1,3,2,0:T(8,128)(2,1)} %bitcast.488), calls=%async_computation.1 | async-start | bytes 16777216 | tf_op jit(solution)/shard_map/all_to_all | solution.py:198
  226.2 168.1 %copy-start.39 = (f32[256]{0:T(256)S(1)}, f32[256]{0:T(256)}, u32[]{:S(2)}) copy-start(f32[256]{0:T(256)} %param.33) | copy-start | bytes 3076
  388.9 77.0 %copy-start.42 = (f32[10240]{0:T(1024)S(1)}, f32[10240]{0:T(1024)}, u32[]{:S(2)}) copy-start(f32[10240]{0:T(1024)} %get-tuple-element.743) | copy-start | bytes 122884
  393.6 72.2 %copy-start.38 = (pred[128,4]{0,1:T(4,128)(4,1)S(1)}, pred[128,4]{0,1:T(4,128)(4,1)}, u32[]{:S(2)}) copy-start(pred[128,4]{0,1:T(4,128)(4,1)} %copy-done.37) | copy-start | bytes 1540
  457.9 20.7 %copy-start.29 = (pred[128]{0:T(512)(128)(4,1)}, pred[128]{0:T(512)(128)(4,1)S(1)}, u32[]{:S(2)}) copy-start(pred[128]{0:T(512)(128)(4,1)S(1)} %get-tuple-element.796) | copy-start | bytes 388
  457.9 20.7 %copy-start.31 = (pred[128]{0:T(512)(128)(4,1)}, pred[128]{0:T(512)(128)(4,1)S(1)}, u32[]{:S(2)}) copy-start(pred[128]{0:T(512)(128)(4,1)S(1)} %get-tuple-element.798) | copy-start | bytes 388
  457.9 20.7 %copy-start.33 = (pred[128]{0:T(512)(128)(4,1)}, pred[128]{0:T(512)(128)(4,1)S(1)}, u32[]{:S(2)}) copy-start(pred[128]{0:T(512)(128)(4,1)S(1)} %get-tuple-element.797) | copy-start | bytes 388
  458.9 19.7 %copy-start.12 = (f32[1,10240]{1,0:T(1,128)}, f32[1,10240]{1,0:T(1,128)S(1)}, u32[]{:S(2)}) copy-start(f32[1,10240]{1,0:T(1,128)S(1)} %get-tuple-element.783) | copy-start | bytes 122884
  505.2 88.9 %copy-start.24 = (f32[128]{0:T(128)S(1)}, f32[128]{0:T(128)}, u32[]{:S(2)}) copy-start(f32[128]{0:T(128)} %get-tuple-element.756) | copy-start | bytes 1540
  594.1 4.6 copy-start.4
  594.1 5.3 copy-start.5
  594.1 5.9 copy-start.6
  797.9 7.8 copy-start.30
  797.9 7.8 copy-start.32
  797.9 7.8 copy-start.34
  805.8 14.5 copy-start.22
  817.9 4.3 copy-start.8
  875.8 8.2 copy-start.10
  875.8 8.2 copy-start.11
  875.8 8.4 copy-start.21
  875.8 11.8 copy-start.9
  875.8 11.8 copy-start.26
  875.8 11.8 copy-start.28
  875.8 13.0 copy-start.44
  875.8 13.6 copy-start.14
  875.8 13.6 copy-start.15
  875.8 13.6 copy-start.16
  875.8 526.0 %all-to-all-start.2 = ((f32[1,4,128,1,64,128]{5,4,1,3,0,2:T(8,128)}), f32[1,4,128,1,64,128]{5,4,1,3,0,2:T(8,128)}, u32[]{:S(2)}, u32[]{:S(2)}) async-start(f32[1,4,128,1,64,128]{5,4,1,3,0,2:T(8,128)} %bitcast.75), calls=%async_computation.2 | async-start | bytes 33554432 | tf_op jit(solution)/shard_map/all_to_all | solution.py:230
  881.7 312.3 %all-reduce.33.cloned.1.call-start = ((), (), s32[]{:S(2)}) async-start(), calls=%async_computation.6 | async-start | bytes 150528
  889.3 474.8 %reduce-scatter.4.cloned.1.call-start = ((), (), s32[]{:S(2)}) async-start(), calls=%async_computation.5 | async-start | bytes 5406720
  893.0 3.6 slice-start
  893.1 4.0 slice-start.1
  901.6 499.2 %copy-start.18 = (s32[512]{0:T(512)S(1)}, s32[512]{0:T(512)}, u32[]{:S(2)}) copy-start(s32[512]{0:T(512)} %param.24) | copy-start | bytes 6148
  1439.4 13.5 copy-start.1
  (4 other events, 8.8 us)
Sparse Core Ops, SparseCore 0:
  889.5 304.4 all-reduce.32
  1196.5 167.5 reduce-scatter.3
where the time goes:
time: 1470 us; the launch traced here: 1460 us
  waiting for transfers between devices  455 us (31%)
  blocking collectives  436 us (30%)
  matrix products  205 us (14%)
  local copies, waits for them, and re-layouts  200 us (14%)
  other arithmetic  94.4 us (6%)
  starting transfers between devices  50.7 us (3%)
  between operations  18.4 us (1%)
    unnamed x4, waiting for transfers between devices  455 us
    all_gather x1, blocking collectives, shards(): lax.all_gather(conv_weight, 'fsdp', axis=1, tiled=True)  157 us
    unnamed x1, blocking collectives  132 us
    dot_general x32, matrix products, group_mix(): jnp.einsum('tdn,dkpn->tkp', c_masked, start_state, precision=lax.Precisio...  79.9 us
    dot_general x24, matrix products, group_mix(): jnp.einsum('kts,skp->tkp', weights, x_rows, precision=lax.Precision.HIGHEST)  70.7 us
    all_gather x1, blocking collectives, shards(): lax.all_gather(norm_gain, 'fsdp', axis=0, tiled=True)  63 us
    unnamed x117, local copies, waits for them, and re-layouts  53.5 us
    all_to_all x1, blocking collectives, shards(): lax.all_to_all(tail_back.reshape(1, doc_count, holders, 3, chan_share), (...  49.9 us
  transfers between devices with their start and end apart: 5, of which 2 were waited for; matrix products, arithmetic and copies ran while one was open for 7% of the time, Pallas kernels for 0%

commit v1 on v0

v1 whole, which is shorter than its diff:
```python
import functools

import jax
import jax.numpy as jnp
from jax import lax
from jax.experimental import pallas as pl
from jax.experimental.pallas import tpu as pltpu
from jax.sharding import PartitionSpec as P

GROUP = 16
T = 128
DOCS = 4
H = 128
P_SIZE = 64
N = 128
G = 8
HG = H // G
GC = HG * P_SIZE
GS = 2048
DI = 8192
CONV = 10240
PROMPTS = 32
SRC = 8

F32 = jnp.float32
BF16 = jnp.bfloat16
NN = (((1,), (0,)), ((), ()))
NT = (((1,), (1,)), ((), ()))
TN = (((0,), (0,)), ((), ()))
AXES = ("dp", "fsdp")


def mm(a, b, dims=NN):
    return lax.dot_general(a, b, dims, preferred_element_type=F32)


def split(a):
    hi = a.astype(BF16)
    return hi, (a - hi.astype(F32)).astype(BF16)


def mm3(a, b, dims=NN):
    ah, al = split(a)
    bh, bl = split(b)
    return mm(ah, bh, dims) + (mm(ah, bl, dims) + mm(al, bh, dims))


def cat(parts, axis):
    return jnp.concatenate(parts, axis=axis)


def sigmoid(a):
    return 1.0 / (1.0 + jnp.exp(-a))


def lanes(rows=T):
    return lax.broadcasted_iota(jnp.int32, (rows, 128), 1)


def head_sum_matrix(first):
    row = lax.broadcasted_iota(jnp.int32, (128, 128), 0)
    col = lax.broadcasted_iota(jnp.int32, (128, 128), 1)
    return (col == first + row // P_SIZE).astype(BF16)


def lagged(u, tails, sel, off):
    led = mm(sel, tails.astype(BF16))
    out = []
    for k in (1, 2, 3):
        back = jnp.where(off >= k, pltpu.roll(u, k, axis=0), 0.0)
        out.append(back + led[(k - 1) * T : k * T])
    return out


def conv_forward(raw, tails, w, bias, sel, off):
    u = raw.astype(F32)
    l1, l2, l3 = lagged(u, tails, sel, off)
    a = bias + w[3:4] * u + w[2:3] * l1 + w[1:2] * l2 + w[0:1] * l3
    sig = sigmoid(a)
    return a * sig, sig * (1.0 + a * (1.0 - sig))


def conv_backward(dout, sp, raw, tails, w, sel, sel_t, off):
    u = raw.astype(F32)
    l1, l2, l3 = lagged(u, tails, sel, off)
    da = dout * sp
    width = da.shape[1]
    sums = [jnp.sum(da * f, axis=0, keepdims=True) for f in (l3, l2, l1, u)]
    sums.append(jnp.sum(da, axis=0, keepdims=True))
    sums.append(jnp.zeros((3, width), F32))
    du = w[3:4] * da
    parts = []
    for k in (1, 2, 3):
        term = w[3 - k : 4 - k] * da
        parts.append(term)
        du = du + pltpu.roll(jnp.where(off >= k, term, 0.0), T - k, axis=0)
    hi, lo = split(cat(parts, 0))
    return du, cat(sums, 0), mm(sel_t, hi) + mm(sel_t, lo)


def local_kernel(
    xr, br, cr, tx, tb, tc, wx, wb, wc, bx, bb, bc, off_ref, sel_ref,
    caus_ref, rel_ref, relt_ref, stept_ref, dsk_ref,
    x_o, b_o, c_o, spx_o, spb_o, spc_o, m0_o, lw_o, exr_o, cq_o, sc_o, score_o,
):
    off = off_ref[...]
    sel = sel_ref[...]
    b, spb = conv_forward(br[...], tb[...], wb[...], bb[...], sel, off)
    c, spc = conv_forward(cr[...], tc[...], wc[...], bc[...], sel, off)
    b_o[...] = b
    c_o[...] = c
    spb_o[...] = spb
    spc_o[...] = spc
    scores = mm3(c, b, NT)
    score_o[0] = scores
    ceil = jnp.maximum(jnp.max(jnp.abs(c), axis=1, keepdims=True), 1e-30)
    cq = jnp.round(c * (32767.0 / ceil)).astype(jnp.int32).astype(jnp.int16)
    for h in range(HG):
        cq_o[h] = cq
    ceil_t = jnp.max(jnp.abs(c.T), axis=0, keepdims=True)
    sc_o[0] = jnp.maximum(ceil_t, 1e-30) * (1.0 / 32767.0)
    caus = caus_ref[...] > 0.0
    first = lanes() < P_SIZE
    for i in range(HG // 2):
        at = slice(128 * i, 128 * (i + 1))
        x, spx = conv_forward(xr[:, at], tx[:, at], wx[:, at], bx[:, at], sel, off)
        x_o[:, at] = x
        spx_o[:, at] = spx
        cols, weights = [], []
        for j in (2 * i, 2 * i + 1):
            col = jnp.broadcast_to(rel_ref[0, :, j : j + 1], (T, T))
            gap = jnp.where(caus, col - relt_ref[j : j + 1, :], -1e30)
            lw = jnp.exp(gap) * stept_ref[j : j + 1, :]
            lw_o[j] = lw
            cols.append(col)
            weights.append(lw * scores)
        exr_o[:, at] = jnp.exp(jnp.where(first, cols[0], cols[1]))
        wide = cat([jnp.where(first, x, 0.0), jnp.where(first, 0.0, x)], 0)
        m0_o[:, at] = mm3(cat(weights, 1), wide) + dsk_ref[:, at] * x


def norm_kernel(
    st_ref, c_ref, m0_ref, exr_ref, z_ref, up_ref, gain_ref, tokw_ref, memb_ref, sc_ref,
    dz_o, dm_o, q_o, s_o, dg_o, rs_o,
    mix_s,
):
    memb = memb_ref[...]
    tokw = tokw_ref[...]
    for gg in range(2):
        cg = c_ref[:, 128 * gg : 128 * (gg + 1)]
        hi, lo = split(cat([cg * memb[:, d : d + 1] for d in range(DOCS)], 1))
        rhs = cat(
            [st_ref[HG * gg : HG * (gg + 1), d].reshape(GC, N) for d in range(DOCS)], 1
        )
        both = mm(cat([hi, lo], 0), rhs, NT)
        at = slice(GC * gg, GC * (gg + 1))
        mix_s[:, at] = m0_ref[:, at] + (both[:T] + both[T:]) * exr_ref[:, at]
    squares = jnp.zeros((T, 128), F32)
    crossed = jnp.zeros((T, 128), F32)
    for i in range(GS // 128):
        at = slice(128 * i, 128 * (i + 1))
        z = z_ref[:, at].astype(F32)
        v = mix_s[:, at] * (z * sigmoid(z))
        dn = up_ref[:, at].astype(F32) * tokw * gain_ref[:, at]
        squares = squares + v * v
        crossed = crossed + dn * v
    r = lax.rsqrt(jnp.sum(squares, axis=1, keepdims=True) * (1.0 / GS) + 1e-05)
    k = r * r * r * (jnp.sum(crossed, axis=1, keepdims=True) * (1.0 / GS))
    r = jnp.broadcast_to(r, (T, 128))
    k = jnp.broadcast_to(k, (T, 128))
    rs = jnp.zeros((2 * T, 128), F32)
    for i in range(GS // 128):
        at = slice(128 * i, 128 * (i + 1))
        z = z_ref[:, at].astype(F32)
        sig = sigmoid(z)
        sz = z * sig
        mixed = mix_s[:, at]
        v = mixed * sz
        go = up_ref[:, at].astype(F32) * tokw
        dg_o[:, at] = jnp.sum(go * v * r, axis=0, keepdims=True)
        dv = r * (go * gain_ref[:, at]) - v * k
        dm = dv * sz
        dm_o[:, at] = dm
        dz_o[:, at] = (dv * mixed * (sig * (1.0 + z * (1.0 - sig)))).astype(BF16)
        hi, lo = split(dm * mixed)
        rs = rs + mm(cat([hi, lo], 0), head_sum_matrix(2 * i))
        turned = (dm * exr_ref[:, at]).T
        for j in range(2):
            h = 2 * i + j
            e = turned[P_SIZE * j : P_SIZE * (j + 1)]
            top = jnp.maximum(jnp.max(jnp.abs(e), axis=0, keepdims=True), 1e-30)
            q_o[h] = jnp.round(e * (32767.0 / top)).astype(jnp.int32).astype(jnp.int16)
            s_o[h : h + 1, :] = top * (1.0 / 32767.0) * sc_ref[h // HG]
    rs_o[0] = rs[:T] + rs[T:]


def back_kernel(
    st_ref, dm_ref, exr_ref, lw_ref, score_ref, x_ref, b_ref, c_ref,
    spx, spb, spc, xr, br, cr, tx, tb, tc, wx, wb, wc, off_ref, sel_ref, selt_ref,
    memb_ref, dsk_ref,
    gx_o, gb_o, gc_o, px_o, pb_o, pc_o, ttx_o, ttb_o, ttc_o, rx_o, cq_o,
):
    off = off_ref[...]
    sel = sel_ref[...]
    sel_t = selt_ref[...]
    memb = memb_ref[...]
    b = b_ref[...]
    c = c_ref[...]
    scores = score_ref[0]
    hi, lo = split(dm_ref[...] * exr_ref[...])
    rhs = cat([st_ref[:, d].reshape(GC, N) for d in range(DOCS)], 1)
    both = mm(cat([hi, lo], 0), rhs)
    both = both[:T] + both[T:]
    dc = jnp.zeros((T, N), F32)
    for d in range(DOCS):
        dc = dc + both[:, N * d : N * (d + 1)] * memb[:, d : d + 1]
    first = lanes() < P_SIZE
    dscores = jnp.zeros((T, T), F32)
    rx = jnp.zeros((2 * T, 128), F32)
    for i in range(HG // 2):
        at = slice(128 * i, 128 * (i + 1))
        dm = dm_ref[:, at]
        x = x_ref[:, at]
        wide = cat([jnp.where(first, dm, 0.0), jnp.where(first, 0.0, dm)], 0)
        dweights = mm3(wide, x, NT)
        weights = []
        for j in range(2):
            lw = lw_ref[2 * i + j]
            g1 = dweights[T * j : T * (j + 1)] * lw
            dscores = dscores + g1
            cq_o[2 * i + j : 2 * i + j + 1, :] = jnp.sum(g1 * scores, axis=0, keepdims=True)
            weights.append(lw * scores)
        turned = wide_t(dm, first)
        dx = mm3(turned, cat(weights, 0)).T + dsk_ref[:, at] * dm
        hi, lo = split(dm * x)
        rx = rx + mm(cat([hi, lo], 0), head_sum_matrix(2 * i))
        du, sums, dt = conv_backward(
            dx, spx[:, at], xr[:, at], tx[:, at], wx[:, at], sel, sel_t, off
        )
        gx_o[:, at] = du.astype(BF16)
        px_o[:, at] = sums
        ttx_o[:, at] = dt
    rx_o[0] = rx[:T] + rx[T:]
    dc = dc + mm3(dscores, b)
    db = mm3(dscores.T, c)
    du, sums, dt = conv_backward(db, spb[...], br[...], tb[...], wb[...], sel, sel_t, off)
    gb_o[...] = du.astype(BF16)
    pb_o[...] = sums
    ttb_o[...] = dt
    du, sums, dt = conv_backward(dc, spc[...], cr[...], tc[...], wc[...], sel, sel_t, off)
    gc_o[...] = du.astype(BF16)
    pc_o[...] = sums
    ttc_o[...] = dt


def wide_t(dm, first):
    t = dm.T
    z = jnp.zeros((P_SIZE, T), F32)
    return cat([cat([t[:P_SIZE], z], 1), cat([z, t[P_SIZE:]], 1)], 0)


def state_kernel(prompt_ref, q_ref, c_ref, s_ref, mask_ref, out_ref):
    step = pl.program_id(0)

    @pl.when(step == 0)
    def _():
        out_ref[...] = jnp.zeros_like(out_ref)

    for i in range(SRC):
        q = q_ref[i].astype(jnp.int32).astype(F32) * s_ref[i : i + 1, :]
        hi, lo = split(q)
        ci = c_ref[i].astype(jnp.int32)
        low = ci & 255
        high = (ci - low).astype(F32).astype(BF16)
        low = low.astype(F32).astype(BF16)
        rhs = cat([high, high, low, low], 0)
        rows = []
        for d in range(DOCS):
            m = jnp.broadcast_to(mask_ref[i, d : d + 1, :], (P_SIZE, T)).astype(BF16)
            rows.append(cat([hi * m, lo * m] * 2, 1))
        got = mm(cat(rows, 0), rhs)
        for d in range(DOCS):
            p = prompt_ref[(step * SRC + i) * DOCS + d]
            out_ref[p] = out_ref[p] + got[P_SIZE * d : P_SIZE * (d + 1)]


def whole(shape):
    return pl.BlockSpec(shape, lambda g, *_: (0,) * len(shape))


def cols(rows, width, first=0):
    return pl.BlockSpec((rows, width), lambda g, *_: (0, first + g))


def lead(*shape):
    return pl.BlockSpec(shape, lambda g, *_: (g,) + (0,) * (len(shape) - 1))


def shape(dims, dtype=F32):
    return jax.ShapeDtypeStruct(dims, dtype)


def call(body, grid, in_specs, out_specs, out_shape, name, flops, nbytes, scratch=()):
    return pl.pallas_call(
        body,
        grid=grid,
        in_specs=in_specs,
        out_specs=out_specs,
        out_shape=out_shape,
        scratch_shapes=list(scratch),
        compiler_params=pltpu.CompilerParams(vmem_limit_bytes=56 * 1024 * 1024),
        cost_estimate=pl.CostEstimate(flops=flops, bytes_accessed=nbytes, transcendentals=0),
        name=name,
    )


def advantages(rewards, resp_prompt, prompt_count):
    member = (resp_prompt[:, None] == jnp.arange(prompt_count, dtype=jnp.int32)[None, :]).astype(F32)
    group_mean = jnp.dot(rewards, member, precision=lax.Precision.HIGHEST) / GROUP
    centred = rewards - jnp.dot(member, group_mean, precision=lax.Precision.HIGHEST)
    spread = jnp.sqrt(jnp.dot(centred * centred, member, precision=lax.Precision.HIGHEST) / GROUP)
    return centred / jnp.dot(member, jnp.maximum(spread, 0.8), precision=lax.Precision.HIGHEST)


def shards(
    xbc, zgate, dt_raw, prompt_states, conv_tails, resp_prompt, resp_lengths, rewards, upstream,
    conv_weight, conv_bias, dt_bias, a_log, d_skip, norm_gain,
):
    devices = lax.axis_size("dp") * lax.axis_size("fsdp")
    n_dp, n_fsdp = lax.axis_size("dp"), lax.axis_size("fsdp")
    dp = lax.axis_index("dp")
    holder = lax.axis_index(AXES)
    exchange = functools.partial(
        lax.all_to_all, axis_name=AXES, split_axis=0, concat_axis=0, tiled=True
    )

    weights = cat(
        [conv_weight.reshape(-1), conv_bias, dt_bias, a_log, d_skip, norm_gain], 0
    )
    count = weights.shape[0]
    weights = jnp.pad(weights, (0, 2048 - count))
    quarter = lax.dynamic_slice_in_dim(weights, dp * 512, 512)
    onehot = resp_prompt[:, None] == jnp.arange(PROMPTS, dtype=jnp.int32)[None, :]
    tails_sent = jnp.dot(
        onehot.astype(BF16), conv_tails.reshape(PROMPTS, 240), preferred_element_type=F32
    )
    lengths_f = jnp.broadcast_to(resp_lengths.astype(F32), (devices, DOCS))
    sent = cat(
        [
            tails_sent.reshape(devices, 960),
            lengths_f,
            jnp.zeros((devices, 60), F32),
            jnp.broadcast_to(quarter[None], (devices, 512)),
        ],
        1,
    )
    got = exchange(sent.reshape(devices, 12, 128)).reshape(devices, 1536)
    states = exchange(
        prompt_states[resp_prompt].reshape(devices, DOCS, P_SIZE, N)
    )

    tails = got[:, :960].reshape(devices, 12, 80).transpose(1, 0, 2).reshape(12, CONV)
    tails = jnp.pad(tails, ((0, 4), (0, 0)))
    all_lengths = got[:, 960:964].astype(jnp.int32)
    full = got[:, 1024:].reshape(n_dp, n_fsdp, 512).transpose(1, 0, 2).reshape(n_fsdp, 2048)
    conv_w = full[:, :1280].reshape(n_fsdp, 4, 320).transpose(1, 0, 2).reshape(4, CONV)
    conv_b = full[:, 1280:1600].reshape(1, CONV)
    bias_dt = full[:, 1600:1604].reshape(1, H)
    rate = jnp.exp(full[:, 1604:1608].reshape(1, H))
    skip = full[:, 1608:1612].reshape(1, H)
    gain = full[:, 1612:1868].reshape(1, DI)

    lengths = resp_lengths[0]
    places = jnp.arange(T, dtype=jnp.int32)
    ends = jnp.cumsum(lengths)
    starts = ends - lengths
    member = (places[:, None] >= starts[None, :]) & (places[:, None] < ends[None, :])
    start = jnp.sum(jnp.where(member, starts[None, :], 0), axis=1)
    offset = (places - start)[:, None]
    causal = ((start[:, None] == start[None, :]) & (places[:, None] >= places[None, :])).astype(F32)
    member_f = member.astype(F32)
    lag = jnp.arange(1, 4, dtype=jnp.int32)[:, None, None, None]
    row = jnp.arange(3, dtype=jnp.int32)[None, None, None, :]
    sel = member[None, :, :, None] & (offset[None, :, :, None] - lag + 3 == row)
    sel = jnp.pad(sel.reshape(3 * T, 12).astype(BF16), ((0, 0), (0, 4)))
    all_ends = jnp.cumsum(all_lengths, axis=1)
    all_starts = all_ends - all_lengths
    mask_rows = (
        (places[None, None, :] >= all_starts[:, :, None])
        & (places[None, None, :] < all_ends[:, :, None])
    ).astype(F32)
    advantage = advantages(rewards, resp_prompt, PROMPTS)
    doc_weight = lax.dynamic_slice_in_dim(advantage, holder * DOCS, DOCS) * (
        T / (DOCS * lengths.astype(F32))
    )
    tokw = jnp.sum(jnp.where(member, doc_weight[None, :], 0.0), axis=1)[:, None]

    raw_step = dt_raw + bias_dt
    step = jax.nn.softplus(raw_step)
    decay = -step * rate
    rel = jnp.dot(causal, decay, precision=lax.Precision.HIGHEST)
    rel_g = rel.reshape(T, G, HG).transpose(1, 0, 2)
    skip_wide = jnp.repeat(skip, P_SIZE, axis=1)

    conv_specs = [cols(T, GC), cols(T, N, 64), cols(T, N, 72)]
    tail_specs = [cols(16, GC), cols(16, N, 64), cols(16, N, 72)]
    tap_specs = [cols(4, GC), cols(4, N, 64), cols(4, N, 72)]
    bias_specs = [cols(1, GC), cols(1, N, 64), cols(1, N, 72)]
    x, b, c, spx, spb, spc, mixed0, lw, exr, cq, sc, scores = call(
        local_kernel,
        (G,),
        conv_specs + tail_specs + tap_specs + bias_specs
        + [whole((T, 1)), whole((3 * T, 16)), whole((T, T)), lead(1, T, HG), lead(HG, T), lead(HG, T),
           cols(1, GC)],
        [cols(T, GC), cols(T, N), cols(T, N), cols(T, GC), cols(T, N), cols(T, N), cols(T, GC),
         lead(HG, T, T), cols(T, GC), lead(HG, T, N), lead(1, 1, T), lead(1, T, T)],
        [shape((T, DI)), shape((T, G * N)), shape((T, G * N)), shape((T, DI)), shape((T, G * N)),
         shape((T, G * N)), shape((T, DI)), shape((H, T, T)), shape((T, DI)),
         shape((H, T, N), jnp.int16), shape((G, 1, T)), shape((G, T, T))],
        "local_forward", 2 * 10**9, 40 * 10**6,
    )(xbc, xbc, xbc, tails, tails, tails, conv_w, conv_w, conv_w, conv_b, conv_b, conv_b,
      offset, sel, causal, rel_g, rel.T, step.T, skip_wide)

    states, cq = lax.optimization_barrier((states, cq))
    got_c = exchange(cq)
    grad_z, dm, q, scale, d_gain, rs = call(
        norm_kernel,
        (4,),
        [lead(32, DOCS, P_SIZE, N), cols(T, 2 * N), cols(T, GS), cols(T, GS), cols(T, GS), cols(T, GS),
         cols(1, GS), whole((T, 1)), whole((T, DOCS)), lead(2, 1, T)],
        [cols(T, GS), cols(T, GS), lead(32, P_SIZE, T), lead(32, T), cols(1, GS), lead(1, T, 128)],
        [shape((T, DI), BF16), shape((T, DI)), shape((H, P_SIZE, T), jnp.int16), shape((H, T)),
         shape((1, DI)), shape((4, T, 128))],
        "norm_both_ways", 3 * 10**9, 35 * 10**6,
        [pltpu.VMEM((T, GS), F32)],
    )(states, c, mixed0, exr, zgate, upstream, gain, tokw, member_f, sc)
    got_q = exchange(q)
    got_s = exchange(scale.reshape(devices, 1, T)).reshape(devices, T)

    gx, gb, gc, px, pb, pc, ttx, ttb, ttc, rx, col_q = call(
        back_kernel,
        (G,),
        [lead(HG, DOCS, P_SIZE, N), cols(T, GC), cols(T, GC), lead(HG, T, T), lead(1, T, T),
         cols(T, GC), cols(T, N), cols(T, N), cols(T, GC), cols(T, N), cols(T, N)]
        + conv_specs + tail_specs + tap_specs
        + [whole((T, 1)), whole((3 * T, 16)), whole((16, 3 * T)), whole((T, DOCS)), cols(1, GC)],
        [cols(T, GC), cols(T, N), cols(T, N), cols(8, GC), cols(8, N), cols(8, N), cols(16, GC),
         cols(16, N), cols(16, N), lead(1, T, 128), lead(HG, T)],
        [shape((T, DI), BF16), shape((T, G * N), BF16), shape((T, G * N), BF16), shape((8, DI)),
         shape((8, G * N)), shape((8, G * N)), shape((16, DI)), shape((16, G * N)), shape((16, G * N)),
         shape((G, T, 128)), shape((H, T))],
        "local_backward", 4 * 10**9, 45 * 10**6,
    )(states, dm, exr, lw, scores, x, b, c, spx, spb, spc, xbc, xbc, xbc, tails, tails, tails,
      conv_w, conv_w, conv_w, offset, sel, sel.T, member_f, skip_wide)
    grad_x = cat([gx, gb, gc], 1)

    rs = rs[:, :, :32].transpose(1, 0, 2).reshape(T, H)
    rx = rx[:, :, :HG].transpose(1, 0, 2).reshape(T, H)
    col_q = col_q.T
    d_rel = rs - skip * rx - col_q
    d_decay = jnp.dot(causal.T, d_rel, precision=lax.Precision.HIGHEST)
    grad_dt = (col_q / step - rate * d_decay) * jax.nn.sigmoid(raw_step)
    d_alog = jnp.sum(decay * d_decay, axis=0)
    d_bias_dt = jnp.sum(grad_dt, axis=0)
    d_skip_out = jnp.sum(rx, axis=0)

    tails_back = cat([ttx, ttb, ttc], 1)[:12].reshape(12, devices, 80).transpose(1, 0, 2)
    taps = cat([px, pb, pc], 1)
    owned = cat(
        [
            taps[:4].reshape(4, n_fsdp, 320).transpose(1, 0, 2).reshape(n_fsdp, 1280),
            taps[4].reshape(n_fsdp, 320),
            d_bias_dt.reshape(n_fsdp, 4),
            d_alog.reshape(n_fsdp, 4),
            d_skip_out.reshape(n_fsdp, 4),
            d_gain.reshape(n_fsdp, 256),
        ],
        1,
    )
    back = cat(
        [
            tails_back.reshape(devices, 960),
            jnp.tile(owned, (n_dp, 1)),
            jnp.zeros((devices, 2944 - 960 - count), F32),
        ],
        1,
    )
    back = exchange(back.reshape(devices, 23, 128)).reshape(devices, 2944)

    grad_states = pl.pallas_call(
        state_kernel,
        grid_spec=pltpu.PrefetchScalarGridSpec(
            num_scalar_prefetch=1,
            grid=(devices // SRC,),
            in_specs=[lead(SRC, P_SIZE, T), lead(SRC, T, N), lead(SRC, T), lead(SRC, DOCS, T)],
            out_specs=whole((PROMPTS, P_SIZE, N)),
        ),
        out_shape=shape((PROMPTS, P_SIZE, N)),
        compiler_params=pltpu.CompilerParams(vmem_limit_bytes=56 * 1024 * 1024),
        cost_estimate=pl.CostEstimate(flops=4 * 10**9, bytes_accessed=8 * 10**6, transcendentals=0),
        name="state_gradients",
    )(resp_prompt, got_q, got_c, got_s, mask_rows)

    grad_tails = jnp.dot(
        onehot.astype(F32).T,
        back[:, :960].reshape(devices * DOCS, 240),
        precision=lax.Precision.HIGHEST,
    ).reshape(PROMPTS, 3, 80)
    total = jnp.sum(back[:, 960 : 960 + count], axis=0)
    return (
        grad_x,
        grad_z,
        grad_dt,
        grad_states.reshape(PROMPTS, 1, P_SIZE, N),
        grad_tails,
        total[:1280].reshape(4, 320),
        total[1280:1600],
        total[1600:1604],
        total[1604:1608],
        total[1608:1612],
        total[1612:1868],
    )


def solution(mesh):
    whole_axis = P(AXES, None)
    weight = P("fsdp")
    return jax.shard_map(
        shards,
        mesh=mesh,
        in_specs=(
            whole_axis, whole_axis, whole_axis, P(None, AXES, None, None), P(None, None, AXES),
            P(), whole_axis, P(), whole_axis, P(None, "fsdp"), weight, weight, weight, weight, weight,
        ),
        out_specs=(
            whole_axis, whole_axis, whole_axis, P(None, AXES, None, None), P(None, None, AXES),
            P(None, "fsdp"), weight, weight, weight, weight, weight,
        ),
        check_vma=False,
    )
```

time: 1470 us -> 362 us (0.25)
  blocking collectives: 436 us -> 67.7 us
  waiting for transfers between devices: 455 us -> 113 us
  matrix products: 205 us -> 3.72 us
  local copies, waits for them, and re-layouts: 200 us -> 40.4 us
  Pallas kernels: 0 us -> 91.9 us
  other arithmetic: 94.4 us -> 13.6 us
  starting transfers between devices: 50.7 us -> 29.6 us
  between operations: 18.4 us -> 1.32 us
    unnamed x4 -> x0, waiting for transfers between devices: 455 us -> none
    all_gather x2 -> x0, blocking collectives: 220 us -> none  [the longest x1 157 us: shards(): lax.all_gather(conv_weight, 'fsdp', axis=1, tiled=True)]
    dot_general x92 -> x4, matrix products: 203 us -> 3.12 us  [the longest x1 1 us: shards(): jnp.dot(onehot.astype(F32).T, back[:, :960].reshape(devices * DOCS, 240),...]
    unnamed x1 -> x0, blocking collectives: 132 us -> none
    all_to_all x3 -> x4, waiting for transfers between devices: 0.01 us -> 113 us  [the longest x1 67.3 us: shards(): exchange(prompt_states[resp_prompt].reshape(devices, DOCS, P_SIZE, N))]
    pallas_call x0 -> x4, Pallas kernels: none -> 91.9 us  [the longest x1 36 us: shards(): call(back_kernel, (G,), [lead(HG, DOCS, P_SIZE, N), cols(T, GC), cols(T,...]
    unnamed x117 -> x53, local copies, waits for them, and re-layouts: 53.5 us -> 2.43 us
    squeeze x56 -> x0, local copies, waits for them, and re-layouts: 43.7 us -> none  [mixer_forward(): lax.map(jax.checkpoint(group_mix), (c_all, b_all, x_heads, by_group(step_...]
  transfers between devices with their start and end apart: 5 -> 4, of which waited for: 2 -> 4; matrix products, arithmetic and copies ran while one was open for 7% -> 14% of each run, Pallas kernels for 0% -> 7%
where the time goes in v1:
time: 362 us; the launch traced here: 361 us
  waiting for transfers between devices  113 us (31%)
  Pallas kernels  91.9 us (25%)
  blocking collectives  67.7 us (19%)
  local copies, waits for them, and re-layouts  40.4 us (11%)
  starting transfers between devices  29.6 us (8%)
  other arithmetic  13.6 us (4%)
  matrix products  3.72 us (1%)
    all_to_all x1, waiting for transfers between devices, shards(): exchange(prompt_states[resp_prompt].reshape(devices, DOCS, P_SIZE, N))  67.3 us
    all_to_all x1, waiting for transfers between devices, shards(): got_c = exchange(cq)  38 us
    pallas_call x1, Pallas kernels, shards(): call(back_kernel, (G,), [lead(HG, DOCS, P_SIZE, N), cols(T, GC), cols(T,...  36 us
    all_to_all x1, blocking collectives, shards(): got_q = exchange(q)  35.1 us
    all_to_all x1, blocking collectives, shards(): back = exchange(back.reshape(devices, 23, 128)).reshape(devices, 2944)  32.7 us
    pallas_call x1, Pallas kernels, shards(): call(local_kernel, (G,), conv_specs + tail_specs + tap_specs + bias_specs...  25.6 us
    pallas_call x1, Pallas kernels, shards(): pl.pallas_call(state_kernel, grid_spec=pltpu.PrefetchScalarGridSpec(num_s...  16.4 us
    pallas_call x1, Pallas kernels, shards(): call(norm_kernel, (4,), [lead(32, DOCS, P_SIZE, N), cols(T, 2 * N), cols(...  13.9 us
  transfers between devices with their start and end apart: 4, of which 4 were waited for; matrix products, arithmetic and copies ran while one was open for 14% of the time, Pallas kernels for 7%

profile of v1, /device:TPU:1, one launch (start us, length us, event | category | flops | bytes accessed | tf_op | source)
XLA Modules:
  0.0 361.3 jit_solution(13381160534931916284)
XLA Ops:
  0.7 0.9 reduce-window.4
  1.5 0.7 fusion.37
  2.3 0.8 reshape.286
  3.1 0.8 copy.122
  3.9 1.0 fusion.15
  5.2 0.8 concatenate.21
  6.5 1.4 copy.125
  7.9 11.5 %all-to-all-start.1 = ((f32[128,12,128]{2,1,0:T(8,128)}), f32[128,12,128]{2,1,0:T(8,128)S(1)}, u32[]{:S(2)}, u32[]{:S(2)}) async-start(f32[128,12,128]{2,1,0:T(8,128)} %copy.125), calls=%async_computation.1 | async-start | bytes 2097152 | tf_op jit(solution)/shard_map/all_to_all | solution.py:357
  19.4 13.5 %gather_fusion = bf16[512,64,128]{2,1,0:T(8,128)(2,1)} fusion(bf16[32,64,128]{2,1,0:T(8,128)(2,1)S(1)} %bitcast.120, s32[1024]{0:T(1024)S(1)} %pad_clamp_fusion), kind=kCustom, calls=%fused_computation | custom fusion | bytes 16779264 | tf_op jit(solution)/shard_map/gather | solution.py:359
  32.9 5.8 %all-to-all-done.1 = f32[128,12,128]{2,1,0:T(8,128)S(1)} async-done(((f32[128,12,128]{2,1,0:T(8,128)}), f32[128,12,128]{2,1,0:T(8,128)S(1)}, u32[]{:S(2)}, u32[]{:S(2)}) %all-to-all-start.1) | async-done | bytes 786464 | tf_op jit(solution)/shard_map/all_to_all | solution.py:357
  38.7 5.8 %all-to-all-start = ((bf16[128,4,64,128]{3,2,1,0:T(8,128)(2,1)}), bf16[128,4,64,128]{3,2,1,0:T(8,128)(2,1)}, u32[]{:S(2)}, u32[]{:S(2)}) async-start(bf16[128,4,64,128]{3,2,1,0:T(8,128)(2,1)} %bitcast.121), calls=%async_computation | async-start | bytes 16777216 | tf_op jit(solution)/shard_map/all_to_all | solution.py:358
  45.3 0.8 copy.136.tokw_ref
  47.9 0.7 copy.135.sel_ref
  48.6 0.7 fusion.24.caus_ref
  50.7 0.6 copy.159
  51.3 0.7 reshape.295.bx.bb.bc
  52.6 0.8 reshape.294.wx.wb.wc
  53.5 0.7 broadcast_in_dim.43.dsk_ref
  55.0 0.9 pad.15.tx.tb.tc
  56.2 1.0 copy.134
  57.2 0.7 fusion.41.stept_ref
  58.0 25.6 %local_forward.1 = (f32[128,8192]{1,0:T(8,128)}, f32[128,1024]{1,0:T(8,128)}, f32[128,1024]{1,0:T(8,128)}, f32[128,8192]{1,0:T(8,128)}, f32[128,1024]{1,0:T(8,12...) custom-call(bf16[128,10240]{1,0:T(8,128)(2,1)} %cr.3, ...), custom_call_target="tpu_custom_call" | custom-call | flops 2000000000 | bytes 40000000 | tf_op jit(solution)/shard_map/local_forward/pallas_call | solution.py:409
  83.6 67.3 %all-to-all-done.st_ref = bf16[128,4,64,128]{3,2,1,0:T(8,128)(2,1)} async-done(((bf16[128,4,64,128]{3,2,1,0:T(8,128)(2,1)}), bf16[128,4,64,128]{3,2,1,0:T(8,128)(2,1)}, u32[]{:S(2)}, u32[]{:S(2)}) %all-to-all-start) | async-done | bytes 8388640 | tf_op jit(solution)/shard_map/all_to_all | solution.py:358
  150.9 13.9 %norm_both_ways.1 = (bf16[128,8192]{1,0:T(8,128)(2,1)}, f32[128,8192]{1,0:T(8,128)}, s16[128,64,128]{2,1,0:T(8,128)(2,1)}, f32[128,128]{1,0:T(8,128)}, f32[1,8192]{1,0:T(1,128)}, /*index=5*/f32[4,128,128]{2,1,0:T(8,128)}) custom-call(bf16[128,4,64,128]{3,2,1,0:T(8,128)(2,1)} %all-to-all-done.st_ref, f32[128,1024]{1,0:T(8,128)} %get-tuple-element.44.c_ref, ...), custom_call_target="tpu_custom_call" | custom-call | flops 3000000000 | bytes 35000000 | tf_op jit(solution)/shard_map/norm_both_ways/pallas_call | solution.py:426
  164.7 36.0 %local_backward.1 = (bf16[128,8192]{1,0:T(8,128)(2,1)}, bf16[128,1024]{1,0:T(8,128)(2,1)}, bf16[128,1024]{1,0:T(8,128)(2,1)}, f32[8,8192]{1,0:T(8,128)}, f32[8,1...) custom-call(bf16[128,4,64,128]{3,2,1,0:T(8,128)(2,1)} %all-to-all-do, ...), custom_call_target="tpu_custom_call" | custom-call | flops 4000000000 | bytes 45000000 | tf_op jit(solution)/shard_map/local_backward/pallas_call | solution.py:440
  200.8 1.2 slice_bitcast_fusion
  202.1 6.7 %all-to-all-start.4 = ((f32[128,1,128]{2,1,0:T(1,128)}), f32[128,1,128]{2,1,0:T(1,128)}, u32[]{:S(2)}, u32[]{:S(2)}) async-start(f32[128,1,128]{2,1,0:T(1,128)} %bitcast.36), calls=%async_computation.4 | async-start | bytes 131072 | tf_op jit(solution)/shard_map/all_to_all | solution.py:438
  209.0 0.9 fusion.42
  210.9 0.7 reduce.8
  213.4 0.8 concatenate.27
  214.7 1.6 copy.149
  216.3 2.1 all-to-all-done.4
  218.4 32.7 %all_to_all.30 = f32[128,23,128]{2,1,0:T(8,128)S(1)} all-to-all(f32[128,23,128]{2,1,0:T(8,128)} %copy.149), channel_id=1, replica_groups=mesh['dp'=4,'fsdp'=32] {'dp','fsdp'}, dimensions={0} | all-to-all | bytes 3014656 | tf_op jit(solution)/shard_map/all_to_all | solution.py:488
  251.1 35.1 %all_to_all.31.q_ref = s16[128,64,128]{2,1,0:T(8,128)(2,1)} all-to-all(s16[128,64,128]{2,1,0:T(8,128)(2,1)S(1)} %copy-done.3), channel_id=1, replica_groups=mesh['dp'=4,'fsdp'=32] {'dp','fsdp'}, dimensions={0} | all-to-all | bytes 4194304 | tf_op jit(solution)/shard_map/all_to_all | solution.py:437
  286.1 5.6 %all-to-all-start.3 = ((s16[128,128,128]{2,1,0:T(8,128)(2,1)}), s16[128,128,128]{2,1,0:T(8,128)(2,1)}, u32[]{:S(2)}, u32[]{:S(2)}) async-start(s16[128,128,128]{2,1,0:T(8,128)(2,1)} %get-tuple-element.64), calls=%async_computation.3 | async-start | bytes 8388608 | tf_op jit(solution)/shard_map/all_to_all | solution.py:425
  291.7 0.7 slice_convert_fusion
  292.6 0.7 fusion.38
  293.4 1.0 fusion.7.mask_ref
  294.4 0.7 copy.153
  295.1 3.3 pad_maximum_fusion
  298.4 1.6 copy.150
  300.1 1.1 slice.101
  301.2 1.5 slice_reduce_fusion
  302.7 0.6 slice.108
  303.9 0.7 reshape.317
  305.8 1.0 fusion.16
  306.8 38.0 %all-to-all-done.3.c_ref = s16[128,128,128]{2,1,0:T(8,128)(2,1)} async-done(((s16[128,128,128]{2,1,0:T(8,128)(2,1)}), s16[128,128,128]{2,1,0:T(8,128)(2,1)}, u32[]{:S(2)}, u32[]{:S(2)}) %all-to-all-start.3) | async-done | bytes 4194336 | tf_op jit(solution)/shard_map/all_to_all | solution.py:425
  344.9 16.4 %state_gradients.1 = f32[32,64,128]{2,1,0:T(8,128)} custom-call(s32[512]{0:T(512)} %prompt_ref.1, s16[128,64,128]{2,1,0:T(8,128)(2,1)} %all_to_all.31.q_ref, s16[128,128,128]{2,1,0:T(8,128)(2,1)} %all-to-all-done.3.c_ref, f32[128,128]{1,0:T(8,128)} %bitcast.37.s_ref, f32[128,4,128]{2,1,0:T(4,128)} %fusion.7.mask_ref), custom_call_target="tpu_custom_call" | custom-call | flops 4000000000 | bytes 8000000 | tf_op jit(solution)/shard_map/state_gradients/pallas_call | solution.py:490
  (129 shorter events, 12.0 us)
Async XLA Ops:
  0.6 18.8 %copy-start = (bf16[32,1,64,128]{3,2,1,0:T(8,128)(2,1)S(1)}, bf16[32,1,64,128]{3,2,1,0:T(8,128)(2,1)}, u32[]{:S(2)}) copy-start(bf16[32,1,64,128]{3,2,1,0:T(8,128)(2,1)} %param.18) | copy-start | bytes 1572868
  6.2 13.2 %copy-start.19 = (s32[512]{0:T(512)S(1)}, s32[512]{0:T(512)}, u32[]{:S(2)}) copy-start(s32[512]{0:T(512)} %prompt_ref.1) | copy-start | bytes 6148
  7.9 30.8 %all-to-all-start.1 = ((f32[128,12,128]{2,1,0:T(8,128)}), f32[128,12,128]{2,1,0:T(8,128)S(1)}, u32[]{:S(2)}, u32[]{:S(2)}) async-start(f32[128,12,128]{2,1,0:T(8,128)} %copy.125), calls=%async_computation.1 | async-start | bytes 2097152 | tf_op jit(solution)/shard_map/all_to_all | solution.py:357
  38.7 5.9 %copy-start.20 = (f32[512]{0:T(512)S(1)}, f32[512]{0:T(512)}, u32[]{:S(2)}) copy-start(f32[512]{0:T(512)} %param.22) | copy-start | bytes 6148
  38.7 6.5 %copy-start.21 = (s32[1,4]{1,0:T(1,128)S(1)}, s32[1,4]{1,0:T(1,128)}, u32[]{:S(2)}) copy-start(s32[1,4]{1,0:T(1,128)} %param.21) | copy-start | bytes 52
  38.7 7.4 %copy-start.13 = (f32[128,128]{1,0:T(8,128)S(1)}, f32[128,128]{1,0:T(8,128)}, u32[]{:S(2)}) copy-start(f32[128,128]{1,0:T(8,128)} %param.17) | copy-start | bytes 196612
  38.7 112.2 %all-to-all-start = ((bf16[128,4,64,128]{3,2,1,0:T(8,128)(2,1)}), bf16[128,4,64,128]{3,2,1,0:T(8,128)(2,1)}, u32[]{:S(2)}, u32[]{:S(2)}) async-start(bf16[128,4,64,128]{3,2,1,0:T(8,128)(2,1)} %bitcast.121), calls=%async_computation | async-start | bytes 16777216 | tf_op jit(solution)/shard_map/all_to_all | solution.py:358
  50.3 4.2 %copy-start.2 = (f32[128,12,128]{0,2,1:T(8,128)}, f32[128,12,128]{0,2,1:T(8,128)S(1)}, u32[]{:S(2)}) copy-start(f32[128,12,128]{0,2,1:T(8,128)S(1)} %copy.126) | copy-start | bytes 2359300
  56.2 1.7 copy-start.6
  164.7 44.1 %copy-start.10 = (f32[4,128,128]{2,1,0:T(8,128)S(1)}, f32[4,128,128]{2,1,0:T(8,128)}, u32[]{:S(2)}) copy-start(f32[4,128,128]{2,1,0:T(8,128)} %get-tuple-element.61) | copy-start | bytes 786436
  200.7 8.2 %copy-start.15 = (f32[128,128]{1,0:T(8,128)S(1)}, f32[128,128]{1,0:T(8,128)}, u32[]{:S(2)}) copy-start(f32[128,128]{1,0:T(8,128)} %get-tuple-element.60) | copy-start | bytes 196612
  200.7 9.2 %copy-start.9 = (f32[8,8192]{1,0:T(8,128)S(1)}, f32[8,8192]{1,0:T(8,128)}, u32[]{:S(2)}) copy-start(f32[8,8192]{1,0:T(8,128)} %get-tuple-element.69) | copy-start | bytes 786436
  200.7 9.2 %copy-start.18 = (f32[8,1024]{1,0:T(8,128)S(1)}, f32[8,1024]{1,0:T(8,128)}, u32[]{:S(2)}) copy-start(f32[8,1024]{1,0:T(8,128)} %get-tuple-element.70) | copy-start | bytes 98308
  200.7 9.2 %copy-start.17 = (f32[8,1024]{1,0:T(8,128)S(1)}, f32[8,1024]{1,0:T(8,128)}, u32[]{:S(2)}) copy-start(f32[8,1024]{1,0:T(8,128)} %get-tuple-element.71) | copy-start | bytes 98308
  200.8 9.4 %copy-start.5 = (f32[16,8192]{1,0:T(8,128)S(1)}, f32[16,8192]{1,0:T(8,128)}, u32[]{:S(2)}) copy-start(f32[16,8192]{1,0:T(8,128)} %get-tuple-element.66) | copy-start | bytes 1572868
  200.8 9.4 %copy-start.11 = (f32[16,1024]{1,0:T(8,128)S(1)}, f32[16,1024]{1,0:T(8,128)}, u32[]{:S(2)}) copy-start(f32[16,1024]{1,0:T(8,128)} %get-tuple-element.67) | copy-start | bytes 196612
  200.8 9.4 %copy-start.12 = (f32[16,1024]{1,0:T(8,128)S(1)}, f32[16,1024]{1,0:T(8,128)}, u32[]{:S(2)}) copy-start(f32[16,1024]{1,0:T(8,128)} %get-tuple-element.68) | copy-start | bytes 196612
  201.9 8.3 %copy-start.4 = (f32[8,128,128]{2,1,0:T(8,128)S(1)}, f32[8,128,128]{2,1,0:T(8,128)}, u32[]{:S(2)}) copy-start(f32[8,128,128]{2,1,0:T(8,128)} %get-tuple-element.62) | copy-start | bytes 1572868
  202.1 8.8 %copy-start.16 = (f32[1,8192]{1,0:T(1,128)S(1)}, f32[1,8192]{1,0:T(1,128)}, u32[]{:S(2)}) copy-start(f32[1,8192]{1,0:T(1,128)} %get-tuple-element.72) | copy-start | bytes 98308
  202.1 16.3 %all-to-all-start.4 = ((f32[128,1,128]{2,1,0:T(1,128)}), f32[128,1,128]{2,1,0:T(1,128)}, u32[]{:S(2)}, u32[]{:S(2)}) async-start(f32[128,1,128]{2,1,0:T(1,128)} %bitcast.36), calls=%async_computation.4 | async-start | bytes 131072 | tf_op jit(solution)/shard_map/all_to_all | solution.py:438
  218.4 32.7 %copy-start.3 = (s16[128,64,128]{2,1,0:T(8,128)(2,1)S(1)}, s16[128,64,128]{2,1,0:T(8,128)(2,1)}, u32[]{:S(2)}) copy-start(s16[128,64,128]{2,1,0:T(8,128)(2,1)} %get-tuple-element.63) | copy-start | bytes 6291460
  286.1 8.3 %copy-start.14 = (f32[128,128]{0,1:T(8,128)S(1)}, f32[128,128]{0,1:T(8,128)}, u32[]{:S(2)}) copy-start(f32[128,128]{0,1:T(8,128)} %get-tuple-element.129) | copy-start | bytes 196612
  286.1 9.0 %copy-start.7 = (bf16[128,1024]{1,0:T(8,128)(2,1)S(1)}, bf16[128,1024]{1,0:T(8,128)(2,1)}, u32[]{:S(2)}) copy-start(bf16[128,1024]{1,0:T(8,128)(2,1)} %get-tuple-element.57) | copy-start | bytes 786436
  286.1 9.0 %copy-start.8 = (bf16[128,1024]{1,0:T(8,128)(2,1)S(1)}, bf16[128,1024]{1,0:T(8,128)(2,1)}, u32[]{:S(2)}) copy-start(bf16[128,1024]{1,0:T(8,128)(2,1)} %get-tuple-element.58) | copy-start | bytes 786436
  286.1 58.7 %all-to-all-start.3 = ((s16[128,128,128]{2,1,0:T(8,128)(2,1)}), s16[128,128,128]{2,1,0:T(8,128)(2,1)}, u32[]{:S(2)}, u32[]{:S(2)}) async-start(s16[128,128,128]{2,1,0:T(8,128)(2,1)} %get-tuple-element.64), calls=%async_computation.3 | async-start | bytes 8388608 | tf_op jit(solution)/shard_map/all_to_all | solution.py:425
  344.9 16.4 %copy-start.1 = (bf16[32,1,64,128]{3,2,1,0:T(8,128)(2,1)S(1)}, bf16[32,1,64,128]{3,2,1,0:T(8,128)(2,1)}, u32[]{:S(2)}) copy-start(bf16[32,1,64,128]{3,2,1,0:T(8,128)(2,1)} %param.18) | copy-start | bytes 1572868

commit v2 on v1

v2 whole, which is shorter than its diff:
```python
import functools

import jax
import jax.numpy as jnp
from jax import lax
from jax.experimental import pallas as pl
from jax.experimental.pallas import tpu as pltpu
from jax.sharding import PartitionSpec as P

GROUP = 16
T = 128
DOCS = 4
H = 128
P_SIZE = 64
N = 128
G = 8
HG = H // G
GC = HG * P_SIZE
GS = 2048
DI = 8192
CONV = 10240
PROMPTS = 32
AHEAD = 128
STEPS = 32752.0
Q_ROWS = 72

F32 = jnp.float32
BF16 = jnp.bfloat16
NN = (((1,), (0,)), ((), ()))
NT = (((1,), (1,)), ((), ()))
TN = (((0,), (0,)), ((), ()))
AXES = ("dp", "fsdp")


def mm(a, b, dims=NN):
    return lax.dot_general(a, b, dims, preferred_element_type=F32)


def split(a):
    hi = a.astype(BF16)
    return hi, (a - hi.astype(F32)).astype(BF16)


def mm3(a, b, dims=NN):
    ah, al = split(a)
    bh, bl = split(b)
    along, out = (1, 0) if dims == NT else (0, 1)
    n = b.shape[out]
    got = mm(cat([ah, al], 1), cat([cat([bh, bh], along), cat([bl, bl], along)], out), dims)
    return got[:, :n] + got[:, n:]


def mm3_wide(a, b):
    m, n = a.shape[0], b.shape[1]
    got = mm(cat(split(a), 0), cat(split(b), 1))
    return got[:m, :n] + (got[:m, n:] + got[m:, :n])


def cat(parts, axis):
    return jnp.concatenate(parts, axis=axis)


def sigmoid(a):
    return 1.0 / (1.0 + jnp.exp(-a))


def level(top):
    return jnp.ceil(jnp.log2(jnp.maximum(top, 1e-30)) + 0.001)


def coded(a, rung):
    return jnp.round(a * (jnp.exp2(-rung) * STEPS)).astype(jnp.int32).astype(jnp.int16)


def lanes(rows=T):
    return lax.broadcasted_iota(jnp.int32, (rows, 128), 1)


def head_sum_matrix(first):
    row = lax.broadcasted_iota(jnp.int32, (128, 128), 0)
    col = lax.broadcasted_iota(jnp.int32, (128, 128), 1)
    return (col == first + row // P_SIZE).astype(BF16)


def lagged(u, tails, sel, off):
    led = mm(sel, tails.astype(BF16))
    out = []
    for k in (1, 2, 3):
        back = jnp.where(off >= k, pltpu.roll(u, k, axis=0), 0.0)
        out.append(back + led[(k - 1) * T : k * T])
    return out


def conv_forward(raw, tails, w, bias, sel, off):
    u = raw.astype(F32)
    l1, l2, l3 = lagged(u, tails, sel, off)
    a = bias + w[3:4] * u + w[2:3] * l1 + w[1:2] * l2 + w[0:1] * l3
    sig = sigmoid(a)
    return a * sig, sig * (1.0 + a * (1.0 - sig))


def conv_backward(dout, sp, raw, tails, w, selr, off):
    u = raw.astype(F32)
    da = dout * sp
    led = mm(selr, cat(split(da), 1))
    led = led[:, :128] + led[:, 128:]
    du = w[3:4] * da
    dt = jnp.zeros((16, 128), F32)
    sums = [jnp.sum(da * u, axis=0, keepdims=True), jnp.sum(da, axis=0, keepdims=True)]
    for k in (1, 2, 3):
        tap = w[3 - k : 4 - k]
        inside = off >= k
        own = led[16 * (k - 1) : 16 * k]
        dt = dt + tap * own
        back = jnp.where(inside, pltpu.roll(u, k, axis=0), 0.0)
        part = jnp.sum(da * back, axis=0, keepdims=True)
        sums.insert(0, part + jnp.sum(own * tails, axis=0, keepdims=True))
        du = du + pltpu.roll(jnp.where(inside, tap * da, 0.0), T - k, axis=0)
    sums.append(jnp.zeros((3, 128), F32))
    return du, cat(sums, 0), dt


def color(q):
    return (q & 1) ^ (2 * ((q >> 1) & 1)) ^ (3 * ((q >> 3) & 1))


def classes(devices):
    return [[q for q in range(devices) if color(q) == k] for k in range(4)]


def local_kernel(
    xr, br, cr, tx, tb, tc, wx, wb, wc, bx, bb, bc, off_ref, sel_ref,
    caus_ref, rel_ref, relt_ref, stept_ref, dsk_ref,
    x_o, b_o, c_o, spx_o, spb_o, spc_o, m0_o, lw_o, exr_o, cq_o, sc_o, score_o,
):
    off = off_ref[...]
    sel = sel_ref[...]
    b, spb = conv_forward(br[...], tb[...], wb[...], bb[...], sel, off)
    c, spc = conv_forward(cr[...], tc[...], wc[...], bc[...], sel, off)
    b_o[...] = b
    c_o[...] = c
    spb_o[...] = spb
    spc_o[...] = spc
    scores = mm3(c, b, NT)
    score_o[0] = scores
    rung = level(jnp.max(jnp.abs(c), axis=1, keepdims=True))
    cq = coded(c, rung)
    for h in range(4):
        cq_o[h] = cq
    sc_o[0] = jnp.broadcast_to(rung, (T, T)).T[:1]
    caus = caus_ref[...] > 0.0
    first = lanes() < P_SIZE
    for i in range(HG // 2):
        at = slice(128 * i, 128 * (i + 1))
        x, spx = conv_forward(xr[:, at], tx[:, at], wx[:, at], bx[:, at], sel, off)
        x_o[:, at] = x
        spx_o[:, at] = spx
        cols, weights = [], []
        for j in (2 * i, 2 * i + 1):
            col = jnp.broadcast_to(rel_ref[0, :, j : j + 1], (T, T))
            gap = jnp.where(caus, col - relt_ref[j : j + 1, :], -1e30)
            lw = jnp.exp(gap) * stept_ref[j : j + 1, :]
            lw_o[j] = lw
            cols.append(col)
            weights.append(lw * scores)
        exr_o[:, at] = jnp.exp(jnp.where(first, cols[0], cols[1]))
        wide = cat([jnp.where(first, x, 0.0), jnp.where(first, 0.0, x)], 0)
        m0_o[:, at] = mm3_wide(cat(weights, 1), wide) + dsk_ref[:, at] * x


def norm_kernel(
    st_ref, c_ref, m0_ref, exr_ref, z_ref, up_ref, gain_ref, tokw_ref, memb_ref, sc_ref,
    dz_o, dm_o, q_o, dg_o, rs_o,
    mix_s,
):
    memb = memb_ref[...]
    tokw = tokw_ref[...]
    for gg in range(2):
        cg = c_ref[:, 128 * gg : 128 * (gg + 1)]
        hi, lo = split(cat([cg * memb[:, d : d + 1] for d in range(DOCS)], 1))
        rhs = cat(
            [st_ref[HG * gg : HG * (gg + 1), d].reshape(GC, N) for d in range(DOCS)], 1
        )
        both = mm(cat([hi, lo], 0), rhs, NT)
        at = slice(GC * gg, GC * (gg + 1))
        mix_s[:, at] = m0_ref[:, at] + (both[:T] + both[T:]) * exr_ref[:, at]
    squares = jnp.zeros((T, 128), F32)
    crossed = jnp.zeros((T, 128), F32)
    for i in range(GS // 128):
        at = slice(128 * i, 128 * (i + 1))
        z = z_ref[:, at].astype(F32)
        v = mix_s[:, at] * (z * sigmoid(z))
        dn = up_ref[:, at].astype(F32) * tokw * gain_ref[:, at]
        squares = squares + v * v
        crossed = crossed + dn * v
    r = lax.rsqrt(jnp.sum(squares, axis=1, keepdims=True) * (1.0 / GS) + 1e-05)
    k = r * r * r * (jnp.sum(crossed, axis=1, keepdims=True) * (1.0 / GS))
    r = jnp.broadcast_to(r, (T, 128))
    k = jnp.broadcast_to(k, (T, 128))
    rs = jnp.zeros((2 * T, 128), F32)
    for i in range(GS // 128):
        at = slice(128 * i, 128 * (i + 1))
        z = z_ref[:, at].astype(F32)
        sig = sigmoid(z)
        sz = z * sig
        mixed = mix_s[:, at]
        v = mixed * sz
        go = up_ref[:, at].astype(F32) * tokw
        dg_o[:, at] = jnp.broadcast_to(jnp.sum(go * v * r, axis=0, keepdims=True), (8, 128))
        dv = r * (go * gain_ref[:, at]) - v * k
        dm = dv * sz
        dm_o[:, at] = dm
        dz_o[:, at] = (dv * mixed * (sig * (1.0 + z * (1.0 - sig)))).astype(BF16)
        hi, lo = split(dm * mixed)
        rs = rs + mm(cat([hi, lo], 0), head_sum_matrix(2 * i))
        turned = (dm * exr_ref[:, at]).T
        for j in range(2):
            h = 2 * i + j
            e = turned[P_SIZE * j : P_SIZE * (j + 1)]
            rung = level(jnp.max(jnp.abs(e), axis=0, keepdims=True))
            scaled = jnp.round(e * (jnp.exp2(-rung) * STEPS))
            both = jnp.broadcast_to(rung + sc_ref[h // HG], (Q_ROWS - P_SIZE, T))
            q_o[h] = cat([scaled, both], 0).astype(jnp.int32).astype(jnp.int16)
    rs_o[...] = (rs[:T] + rs[T:]).T[:32]


def back_kernel(
    st_ref, dm_ref, exr_ref, lw_ref, score_ref, x_ref, b_ref, c_ref,
    spx, spb, spc, xr, br, cr, tx, tb, tc, wx, wb, wc, off_ref, selr_ref,
    memb_ref, dsk_ref, caus_ref, rs_ref, stept_ref, sigt_ref, rate_ref, skip_ref, dgain_ref,
    gx_o, gb_o, gc_o, gdt_o, pay_o,
    acc_s, heads_s,
):
    group = pl.program_id(0)
    off = off_ref[...]
    selr = selr_ref[...]
    memb = memb_ref[...]
    b = b_ref[...]
    c = c_ref[...]
    scores = score_ref[0]

    def keep(first, sums, dt):
        first = pl.multiple_of(AHEAD + first, 128)
        acc_s[:16, pl.ds(first, 128)] = dt
        acc_s[16:, pl.ds(first, 128)] = sums

    hi, lo = split(dm_ref[...] * exr_ref[...])
    rhs = cat([st_ref[:, d].reshape(GC, N) for d in range(DOCS)], 1)
    both = mm(cat([hi, lo], 0), rhs)
    both = both[:T] + both[T:]
    dc = jnp.zeros((T, N), F32)
    for d in range(DOCS):
        dc = dc + both[:, N * d : N * (d + 1)] * memb[:, d : d + 1]
    first = lanes() < P_SIZE
    dscores = jnp.zeros((T, T), F32)
    rx = jnp.zeros((2 * T, 128), F32)
    col_q = []
    for i in range(HG // 2):
        at = slice(128 * i, 128 * (i + 1))
        dm = dm_ref[:, at]
        x = x_ref[:, at]
        wide = cat([jnp.where(first, dm, 0.0), jnp.where(first, 0.0, dm)], 0)
        dweights = mm3(wide, x, NT)
        weights = []
        for j in range(2):
            lw = lw_ref[2 * i + j]
            g1 = dweights[T * j : T * (j + 1)] * lw
            dscores = dscores + g1
            col_q.append(jnp.sum(g1 * scores, axis=0, keepdims=True))
            weights.append(lw * scores)
        dx = mm3_wide(wide_t(dm), cat(weights, 0)).T + dsk_ref[:, at] * dm
        hi, lo = split(dm * x)
        rx = rx + mm(cat([hi, lo], 0), head_sum_matrix(2 * i))
        du, sums, dt = conv_backward(dx, spx[:, at], xr[:, at], tx[:, at], wx[:, at], selr, off)
        gx_o[:, at] = du.astype(BF16)
        keep(group * GC + 128 * i, sums, dt)

    dc = dc + mm3(dscores, b)
    db = mm3(dscores.T, c)
    du, sums, dt = conv_backward(db, spb[...], br[...], tb[...], wb[...], selr, off)
    gb_o[...] = du.astype(BF16)
    keep(DI + group * N, sums, dt)
    du, sums, dt = conv_backward(dc, spc[...], cr[...], tc[...], wc[...], selr, off)
    gc_o[...] = du.astype(BF16)
    keep(DI + G * N + group * N, sums, dt)

    rx = (rx[:T] + rx[T:]).T[:HG]
    col_q = cat(col_q, 0)
    d_rel = rs_ref[...] - skip_ref[...] * rx - col_q
    d_decay = mm(cat(three_parts(d_rel), 0), caus_ref[...].astype(BF16))
    d_decay = d_decay[:HG] + (d_decay[HG : 2 * HG] + d_decay[2 * HG :])
    step = stept_ref[...]
    rate = rate_ref[...]
    d_dt = (col_q / step - rate * d_decay) * sigt_ref[...]
    gdt_o[...] = d_dt
    lane = lanes(HG)
    heads = jnp.where(lane == 0, jnp.sum(d_dt, axis=1, keepdims=True), 0.0)
    heads = jnp.where(lane == 1, -jnp.sum(step * rate * d_decay, axis=1, keepdims=True), heads)
    heads = jnp.where(lane == 2, jnp.sum(rx, axis=1, keepdims=True), heads)
    heads_s[pl.ds(pl.multiple_of(group * HG, HG), HG), :] = heads

    @pl.when(group == G - 1)
    def _():
        acc_s[:, :AHEAD] = jnp.zeros((24, AHEAD), F32)
        acc_s[:, AHEAD + CONV :] = jnp.zeros((24, 128), F32)
        pack_gradients(acc_s, heads_s, dgain_ref, pay_o)


def window(ref, rows, at):
    base, off = at // 128 * 128, at % 128
    if off == 0:
        return ref[rows, base : base + 128]
    return pltpu.roll(ref[rows, base : base + 256], 256 - off, axis=1)[:, :128]


def pack_gradients(acc, heads, dgain, out):
    row = lax.broadcasted_iota(jnp.int32, (8, 128), 0)
    lane = lax.broadcasted_iota(jnp.int32, (8, 128), 1)
    upper = row < 4
    taps = slice(16, 24)
    for f in range(32):
        at = AHEAD + 320 * f
        w0 = pltpu.roll(window(acc, taps, at), 4, axis=0)
        w1 = window(acc, taps, at + 128)
        w2 = pltpu.roll(window(acc, taps, at + 256), 4, axis=0)
        low = dgain[:, 256 * f : 256 * f + 128]
        high = dgain[:, 256 * f + 128 : 256 * f + 256]
        g = jnp.where(row < 6, jnp.where(row < 5, pltpu.roll(low, 64, axis=1), low),
                      jnp.where(row < 7, pltpu.roll(high, 64, axis=1), high))
        last = jnp.where(upper, w1, jnp.where(lane < 64, w2, g))
        extra = jnp.zeros((8, 128), F32)
        for k in range(7):
            piece = pltpu.roll(window(acc, taps, at + 48 * k - 80), (k - 4) % 8, axis=0)
            extra = jnp.where(row == k, piece, extra)
        tile = heads[8 * (f // 2) : 8 * (f // 2) + 8, :]
        for i in range(4):
            moved = pltpu.roll(tile, 80 + 3 * i, axis=1)
            moved = pltpu.roll(moved, (7 - 4 * (f % 2) - i) % 8, axis=0)
            here = (row == 7) & (lane >= 80 + 3 * i) & (lane < 83 + 3 * i)
            extra = jnp.where(here, moved, extra)
        for p in range(4):
            m = 32 * p + f
            at = AHEAD + 80 * m
            out[m, 0:8, :] = jnp.where(lane < 80, window(acc, slice(0, 8), at), extra)
            out[m, 8:16, :] = jnp.where(upper, window(acc, slice(8, 16), at), w0)
            out[m, 16:24, :] = last


def finish_kernel(back_ref, member_ref, tails_o, w_o, b_o, g_o, heads_o):
    for j in range(3):
        rows = cat([back_ref[:, 3 * d + j, :] for d in range(DOCS)], 0)
        got = mm(member_ref[...], cat(three_parts(rows), 1))
        got = got[:, :128] + (got[:, 128:256] + got[:, 256:])
        tails_o[:, j, :] = got[:, :80]
    total = jnp.sum(back_ref[...], axis=0)
    w_o[...] = cat([total[12:16], total[16:20], total[20:24, :64]], 1)
    lane = lax.broadcasted_iota(jnp.int32, (1, 128), 1)
    turned = pltpu.roll(total[16:24], 64, axis=1)
    lo = jnp.where(lane < 64, turned[4:5], total[21:22])
    hi = jnp.where(lane < 64, turned[6:7], total[23:24])
    g_o[...] = cat([lo, hi], 1)
    row = lax.broadcasted_iota(jnp.int32, (8, 384), 0)
    wide = lax.broadcasted_iota(jnp.int32, (8, 384), 1)
    spread = cat([total[:8], jnp.zeros((8, 256), F32)], 1)
    bias = jnp.zeros((8, 384), F32)
    for k in range(7):
        here = (row == k) & (wide >= 48 * k) & (wide < 48 * k + 48)
        bias = jnp.where(here, pltpu.roll(spread, (48 * k - 80) % 384, axis=1), bias)
    b_o[...] = jnp.sum(bias, axis=0, keepdims=True)[:, :320]
    heads_o[...] = pltpu.roll(total[:8], 48, axis=1)[7:8]


def three_parts(a):
    hi, lo = split(a)
    return hi, lo, (a - hi.astype(F32) - lo.astype(F32)).astype(BF16)


def wide_t(dm):
    t = dm.T
    z = jnp.zeros((P_SIZE, T), F32)
    return cat([cat([t[:P_SIZE], z], 1), cat([z, t[P_SIZE:]], 1)], 0)


def gather_kernel(prompt_ref, table_ref, out_ref):
    step = pl.program_id(0)
    for i in range(32):
        out_ref[i] = table_ref[prompt_ref[step * 32 + i]]


def state_kernel(order_ref, prompt_ref, q_ref, c0_ref, c1_ref, c2_ref, c3_ref, mask_ref, out_ref):
    out_ref[...] = jnp.zeros_like(out_ref)

    def place(s, carry):
        for kind, c_ref in enumerate((c0_ref, c1_ref, c2_ref, c3_ref)):
            source = order_ref[kind, s]
            q = q_ref[source].astype(jnp.int32).astype(F32)
            scale = jnp.exp2(q[P_SIZE : P_SIZE + 1]) * (1.0 / STEPS**2)
            hi, lo = split(q[:P_SIZE] * scale)
            ci = c_ref[s].astype(jnp.int32)
            low = ci & 255
            high = (ci - low).astype(F32).astype(BF16)
            low = low.astype(F32).astype(BF16)
            rhs = cat([cat([high, low], 1)] * 2, 0)
            rows = []
            for d in range(DOCS):
                m = jnp.broadcast_to(mask_ref[source, d : d + 1, :], (P_SIZE, T)).astype(BF16)
                rows.append(cat([hi * m, lo * m], 1))
            got = mm(cat(rows, 0), rhs)
            got = got[:, :N] + got[:, N:]
            for d in range(DOCS):
                p = prompt_ref[source * DOCS + d]
                out_ref[p] = out_ref[p] + got[P_SIZE * d : P_SIZE * (d + 1)]
        return carry

    lax.fori_loop(0, c0_ref.shape[0], place, 0)


def whole(shape):
    return pl.BlockSpec(shape, lambda g, *_: (0,) * len(shape))


def cols(rows, width, first=0):
    return pl.BlockSpec((rows, width), lambda g, *_: (0, first + g))


def lead(*shape):
    return pl.BlockSpec(shape, lambda g, *_: (g,) + (0,) * (len(shape) - 1))


def shape(dims, dtype=F32):
    return jax.ShapeDtypeStruct(dims, dtype)


def call(body, grid, in_specs, out_specs, out_shape, name, flops, nbytes, scratch=()):
    return pl.pallas_call(
        body,
        grid=grid,
        in_specs=in_specs,
        out_specs=out_specs,
        out_shape=out_shape,
        scratch_shapes=list(scratch),
        compiler_params=pltpu.CompilerParams(vmem_limit_bytes=56 * 1024 * 1024),
        cost_estimate=pl.CostEstimate(flops=flops, bytes_accessed=nbytes, transcendentals=0),
        name=name,
    )


def three(a):
    parts = []
    for _ in range(3):
        part = lax.reduce_precision(a, 8, 7)
        parts.append(part.astype(BF16))
        a = a - part
    return parts


def advantages(rewards, resp_prompt, prompt_count):
    member = (resp_prompt[:, None] == jnp.arange(prompt_count, dtype=jnp.int32)[None, :]).astype(F32)
    group_mean = jnp.dot(rewards, member, precision=lax.Precision.HIGHEST) / GROUP
    centred = rewards - jnp.dot(member, group_mean, precision=lax.Precision.HIGHEST)
    spread = jnp.sqrt(jnp.dot(centred * centred, member, precision=lax.Precision.HIGHEST) / GROUP)
    return centred / jnp.dot(member, jnp.maximum(spread, 0.8), precision=lax.Precision.HIGHEST)


def shards(
    xbc, zgate, dt_raw, prompt_states, conv_tails, resp_prompt, resp_lengths, rewards, upstream,
    conv_weight, conv_bias, dt_bias, a_log, d_skip, norm_gain,
):
    devices = lax.axis_size("dp") * lax.axis_size("fsdp")
    n_dp, n_fsdp = lax.axis_size("dp"), lax.axis_size("fsdp")
    dp = lax.axis_index("dp")
    holder = lax.axis_index(AXES)
    exchange = functools.partial(
        lax.all_to_all, axis_name=AXES, split_axis=0, concat_axis=0, tiled=True
    )

    weights = cat(
        [conv_weight.reshape(-1), conv_bias, dt_bias, a_log, d_skip, norm_gain], 0
    )
    count = weights.shape[0]
    weights = jnp.pad(weights, (0, 2048 - count))
    quarter = lax.dynamic_slice_in_dim(weights, dp * 512, 512)
    quarter = cat(three(quarter), 0)
    onehot = resp_prompt[:, None] == jnp.arange(PROMPTS, dtype=jnp.int32)[None, :]
    tails_sent = jnp.dot(
        onehot.astype(BF16), conv_tails.reshape(PROMPTS, 240), preferred_element_type=F32
    ).astype(BF16)
    lengths_f = jnp.broadcast_to(resp_lengths.astype(BF16), (devices, DOCS))
    sent = cat(
        [
            tails_sent.reshape(devices, 960),
            lengths_f,
            jnp.zeros((devices, 60), BF16),
            jnp.broadcast_to(quarter[None], (devices, 1536)),
            jnp.zeros((devices, 512), BF16),
        ],
        1,
    )
    got = exchange(sent.reshape(devices, 24, 128)).reshape(devices, 3072)
    states = pl.pallas_call(
        gather_kernel,
        grid_spec=pltpu.PrefetchScalarGridSpec(
            num_scalar_prefetch=1,
            grid=(devices * DOCS // 32,),
            in_specs=[whole((PROMPTS, P_SIZE, N))],
            out_specs=lead(32, P_SIZE, N),
        ),
        out_shape=shape((devices * DOCS, P_SIZE, N), BF16),
        compiler_params=pltpu.CompilerParams(vmem_limit_bytes=56 * 1024 * 1024),
        cost_estimate=pl.CostEstimate(flops=0, bytes_accessed=16 * 10**6, transcendentals=0),
        name="gather_states",
    )(resp_prompt, prompt_states.reshape(PROMPTS, P_SIZE, N))
    states = exchange(states.reshape(devices, DOCS, P_SIZE, N))

    lengths, got = lax.optimization_barrier((resp_lengths[0], got))
    tails = got[:, :960].reshape(devices, 12, 80).transpose(1, 0, 2).reshape(12, CONV)
    tails = jnp.pad(tails, ((0, 4), (0, 0)))
    all_lengths = got[:, 960:964].astype(jnp.int32)
    full = sum(got[:, i : i + 512].astype(F32) for i in (2048, 1536, 1024))
    full = full.reshape(n_dp, n_fsdp, 512).transpose(1, 0, 2).reshape(n_fsdp, 2048)
    conv_w = full[:, :1280].reshape(n_fsdp, 4, 320).transpose(1, 0, 2).reshape(4, CONV)
    conv_b = full[:, 1280:1600].reshape(1, CONV)
    bias_dt = full[:, 1600:1604].reshape(1, H)
    rate = jnp.exp(full[:, 1604:1608].reshape(1, H))
    skip = full[:, 1608:1612].reshape(1, H)
    gain = full[:, 1612:1868].reshape(1, DI)

    places = jnp.arange(T, dtype=jnp.int32)
    ends = jnp.cumsum(lengths)
    starts = ends - lengths
    member = (places[:, None] >= starts[None, :]) & (places[:, None] < ends[None, :])
    start = jnp.sum(jnp.where(member, starts[None, :], 0), axis=1)
    offset = (places - start)[:, None]
    causal = ((start[:, None] == start[None, :]) & (places[:, None] >= places[None, :])).astype(F32)
    member_f = member.astype(F32)
    lag = jnp.arange(1, 4, dtype=jnp.int32)[:, None, None, None]
    row = jnp.arange(3, dtype=jnp.int32)[None, None, None, :]
    sel = member[None, :, :, None] & (offset[None, :, :, None] - lag + 3 == row)
    sel = jnp.pad(sel.reshape(3 * T, 12).astype(BF16), ((0, 0), (0, 4)))
    sel_rows = sel.reshape(3, T, 16).transpose(0, 2, 1).reshape(48, T)
    by_doc = resp_prompt.reshape(devices, DOCS).T.reshape(1, -1)
    members = (jnp.arange(PROMPTS, dtype=jnp.int32)[:, None] == by_doc).astype(BF16)
    all_ends = jnp.cumsum(all_lengths, axis=1)
    all_starts = all_ends - all_lengths
    mask_rows = (
        (places[None, None, :] >= all_starts[:, :, None])
        & (places[None, None, :] < all_ends[:, :, None])
    ).astype(F32)
    advantage = advantages(rewards, resp_prompt, PROMPTS)
    doc_weight = lax.dynamic_slice_in_dim(advantage, holder * DOCS, DOCS) * (
        T / (DOCS * lengths.astype(F32))
    )
    tokw = jnp.sum(jnp.where(member, doc_weight[None, :], 0.0), axis=1)[:, None]

    raw_step = dt_raw + bias_dt
    step = jax.nn.softplus(raw_step)
    decay = -step * rate
    rel = jnp.dot(causal, decay, precision=lax.Precision.HIGHEST)
    step_t = step.T
    rel_g = rel.reshape(T, G, HG).transpose(1, 0, 2)
    skip_wide = jnp.repeat(skip, P_SIZE, axis=1)

    groups = classes(devices)
    order = jnp.asarray(groups, jnp.int32)[color(holder) ^ jnp.arange(4, dtype=jnp.int32)]
    rate_t, skip_t, sig_t = rate.T, skip.T, jax.nn.sigmoid(raw_step).T
    (offset, sel, sel_rows, causal, member_f, members, mask_rows, tokw, order, rate_t, skip_t, sig_t, step_t,
     conv_b) = lax.optimization_barrier(
        (offset, sel, sel_rows, causal, member_f, members, mask_rows, tokw, order, rate_t, skip_t, sig_t,
         step_t, conv_b)
    )

    conv_specs = [cols(T, GC), cols(T, N, 64), cols(T, N, 72)]
    tail_specs = [cols(16, GC), cols(16, N, 64), cols(16, N, 72)]
    tap_specs = [cols(4, GC), cols(4, N, 64), cols(4, N, 72)]
    bias_specs = [cols(1, GC), cols(1, N, 64), cols(1, N, 72)]
    x, b, c, spx, spb, spc, mixed0, lw, exr, cq, sc, scores = call(
        local_kernel,
        (G,),
        conv_specs + tail_specs + tap_specs + bias_specs
        + [whole((T, 1)), whole((3 * T, 16)), whole((T, T)), lead(1, T, HG), lead(HG, T), lead(HG, T),
           cols(1, GC)],
        [cols(T, GC), cols(T, N), cols(T, N), cols(T, GC), cols(T, N), cols(T, N), cols(T, GC),
         lead(HG, T, T), cols(T, GC), lead(4, T, N), lead(1, 1, T), lead(1, T, T)],
        [shape((T, DI)), shape((T, G * N)), shape((T, G * N)), shape((T, DI)), shape((T, G * N)),
         shape((T, G * N)), shape((T, DI)), shape((H, T, T)), shape((T, DI)),
         shape((4 * G, T, N), jnp.int16), shape((G, 1, T)), shape((G, T, T))],
        "local_forward", 0, 95 * 10**6,
    )(xbc, xbc, xbc, tails, tails, tails, conv_w, conv_w, conv_w, conv_b, conv_b, conv_b,
      offset, sel, causal, rel_g, rel.T, step_t, skip_wide)

    states, cq = lax.optimization_barrier((states, cq))
    near = [lax.all_to_all(cq, AXES, 0, 0, axis_index_groups=groups, tiled=True)]
    grad_z, dm, q, d_gain, rs = call(
        norm_kernel,
        (4,),
        [lead(32, DOCS, P_SIZE, N), cols(T, 2 * N), cols(T, GS), cols(T, GS), cols(T, GS), cols(T, GS),
         cols(1, GS), whole((T, 1)), whole((T, DOCS)), lead(2, 1, T)],
        [cols(T, GS), cols(T, GS), lead(32, Q_ROWS, T), cols(8, GS), lead(32, T)],
        [shape((T, DI), BF16), shape((T, DI)), shape((H, Q_ROWS, T), jnp.int16),
         shape((8, DI)), shape((H, T))],
        "norm_both_ways", 0, 52 * 10**6,
        [pltpu.VMEM((T, GS), F32)],
    )(states, c, mixed0, exr, zgate, upstream, gain, tokw, member_f, sc)
    q, dm, near[0] = lax.optimization_barrier((q, dm, near[0]))
    for bit in (1, 2, 8):
        near.append(lax.ppermute(near[0], AXES, [(d, d ^ bit) for d in range(devices)]))
    got_q = exchange(q)

    gx, gb, gc, grad_dt, back = call(
        back_kernel,
        (G,),
        [lead(HG, DOCS, P_SIZE, N), cols(T, GC), cols(T, GC), lead(HG, T, T), lead(1, T, T),
         cols(T, GC), cols(T, N), cols(T, N), cols(T, GC), cols(T, N), cols(T, N)]
        + conv_specs + tail_specs + tap_specs
        + [whole((T, 1)), whole((48, T)), whole((T, DOCS)), cols(1, GC), whole((T, T)), lead(HG, T),
           lead(HG, T), lead(HG, T), lead(HG, 1), lead(HG, 1), whole((8, DI))],
        [cols(T, GC), cols(T, N), cols(T, N), lead(HG, T), whole((devices, 24, 128))],
        [shape((T, DI), BF16), shape((T, G * N), BF16), shape((T, G * N), BF16), shape((H, T)),
         shape((devices, 24, 128))],
        "local_backward", 0, 133 * 10**6,
        [pltpu.VMEM((24, AHEAD + CONV + 128), F32), pltpu.VMEM((H, 128), F32)],
    )(states, dm, exr, lw, scores, x, b, c, spx, spb, spc, xbc, xbc, xbc, tails, tails, tails,
      conv_w, conv_w, conv_w, offset, sel_rows, member_f, skip_wide, causal, rs, step_t,
      sig_t, rate_t, skip_t, d_gain)

    gx, gb, gc, grad_dt, back, got_q, *near = lax.optimization_barrier(
        (gx, gb, gc, grad_dt, back, got_q, *near)
    )
    grad_x = cat([gx, gb, gc], 1)
    back = exchange(back)

    grad_states = pl.pallas_call(
        state_kernel,
        grid_spec=pltpu.PrefetchScalarGridSpec(
            num_scalar_prefetch=2,
            grid=(1,),
            in_specs=[whole((devices, Q_ROWS, T))] + [whole((devices // 4, T, N))] * 4
            + [whole((devices, DOCS, T))],
            out_specs=whole((PROMPTS, P_SIZE, N)),
        ),
        out_shape=shape((PROMPTS, P_SIZE, N)),
        compiler_params=pltpu.CompilerParams(vmem_limit_bytes=56 * 1024 * 1024),
        cost_estimate=pl.CostEstimate(flops=0, bytes_accessed=60 * 10**6, transcendentals=0),
        name="state_gradients",
    )(order, resp_prompt, got_q, *near, mask_rows)

    share = CONV // n_fsdp
    grad_tails, grad_w, grad_b, grad_gain, heads = call(
        finish_kernel,
        (1,),
        [whole((devices, 24, 128)), whole((PROMPTS, devices * DOCS))],
        [whole((PROMPTS, 3, 80)), whole((4, share)), whole((1, share)), whole((1, 256)), whole((1, 128))],
        [shape((PROMPTS, 3, 80)), shape((4, share)), shape((1, share)), shape((1, 256)), shape((1, 128))],
        "finish", 0, 10 * 10**6,
    )(back, members)
    heads = heads[0, :12].reshape(4, 3)
    return (
        grad_x,
        grad_z,
        grad_dt.T,
        grad_states.reshape(PROMPTS, 1, P_SIZE, N),
        grad_tails,
        grad_w,
        grad_b.reshape(share),
        heads[:, 0],
        heads[:, 1],
        heads[:, 2],
        grad_gain.reshape(256),
    )


def solution(mesh):
    whole_axis = P(AXES, None)
    weight = P("fsdp")
    return jax.shard_map(
        shards,
        mesh=mesh,
        in_specs=(
            whole_axis, whole_axis, whole_axis, P(None, AXES, None, None), P(None, None, AXES),
            P(), whole_axis, P(), whole_axis, P(None, "fsdp"), weight, weight, weight, weight, weight,
        ),
        out_specs=(
            whole_axis, whole_axis, whole_axis, P(None, AXES, None, None), P(None, None, AXES),
            P(None, "fsdp"), weight, weight, weight, weight, weight,
        ),
        check_vma=False,
    )
```

time: 362 us -> 271 us (0.75)
  blocking collectives: 67.7 us -> 0 us
  local copies, waits for them, and re-layouts: 40.4 us -> 20.2 us
  starting transfers between devices: 29.6 us -> 44.6 us
  waiting for transfers between devices: 113 us -> 103 us
  other arithmetic: 13.6 us -> 8.91 us
    all_to_all x2 -> x0, blocking collectives: 67.7 us -> none  [the longest x1 35.1 us: shards(): got_q = exchange(q)]
    all_to_all x4 -> x5, waiting for transfers between devices: 113 us -> 88.8 us  [the longest x1 71.8 us: shards(): states = exchange(states.reshape(devices, DOCS, P_SIZE, N))]
    ppermute x0 -> x3, waiting for transfers between devices: none -> 14 us  [shards(): lax.ppermute(near[0], AXES, [(d, d ^ bit) for d in range(devices)])]
    gather x1, local copies, waits for them, and re-layouts: 13.5 us -> 1.13 us  [shards(): jnp.asarray(groups, jnp.int32)]
    pallas_call x0 -> x2, Pallas kernels: none -> 11.4 us  [the longest x1 8.7 us: shards(): pl.pallas_call(gather_kernel, grid_spec=pltpu.PrefetchScalarGridSpec(num_...]
    all_to_all x4 -> x5, starting transfers between devices: 29.6 us -> 40.5 us  [the longest x1 11.5 us: shards(): got = exchange(sent.reshape(devices, 24, 128)).reshape(devices, 3072)]
    pallas_call x1, Pallas kernels: 25.6 us -> 18.5 us  [shards(): call(local_kernel, (G,), conv_specs + tail_specs + tap_specs + bias_specs...]
    pallas_call x1, Pallas kernels: 36 us -> 30.8 us  [shards(): call(back_kernel, (G,), [lead(HG, DOCS, P_SIZE, N), cols(T, GC), cols(T,...]
  transfers between devices with their start and end apart: 4 -> 8, of which waited for: 4 -> 6; matrix products, arithmetic and copies ran while one was open for 14% -> 8% of each run, Pallas kernels for 7% -> 32%
where the time goes in v2:
time: 271 us; the launch traced here: 270 us
  waiting for transfers between devices  103 us (38%)
  Pallas kernels  89.7 us (33%)
  starting transfers between devices  44.6 us (16%)
  local copies, waits for them, and re-layouts  20.2 us (7%)
  other arithmetic  8.91 us (3%)
    all_to_all x1, waiting for transfers between devices, shards(): states = exchange(states.reshape(devices, DOCS, P_SIZE, N))  71.8 us
    pallas_call x1, Pallas kernels, shards(): call(back_kernel, (G,), [lead(HG, DOCS, P_SIZE, N), cols(T, GC), cols(T,...  30.8 us
    pallas_call x1, Pallas kernels, shards(): call(local_kernel, (G,), conv_specs + tail_specs + tap_specs + bias_specs...  18.5 us
    pallas_call x1, Pallas kernels, shards(): pl.pallas_call(state_kernel, grid_spec=pltpu.PrefetchScalarGridSpec(num_s...  15 us
    ppermute x3, waiting for transfers between devices, shards(): lax.ppermute(near[0], AXES, [(d, d ^ bit) for d in range(devices)])  14 us
    pallas_call x1, Pallas kernels, shards(): call(norm_kernel, (4,), [lead(32, DOCS, P_SIZE, N), cols(T, 2 * N), cols(...  13.9 us
    all_to_all x1, starting transfers between devices, shards(): got = exchange(sent.reshape(devices, 24, 128)).reshape(devices, 3072)  11.5 us
    all_to_all x1, starting transfers between devices, shards(): back = exchange(back)  9.42 us
  transfers between devices with their start and end apart: 8, of which 6 were waited for; matrix products, arithmetic and copies ran while one was open for 8% of the time, Pallas kernels for 32%

profile of v2, /device:TPU:1, one launch (start us, length us, event | category | flops | bytes accessed | tf_op | source)
XLA Modules:
  0.0 269.8 jit_solution(4673529465467193410)
XLA Ops:
  0.6 0.8 reshape.282
  1.4 0.8 copy.103
  2.3 1.0 convolution_convert_fusion
  3.8 0.7 convert_bitcast_fusion
  4.5 0.8 concatenate.12
  5.8 1.0 copy.126
  6.8 11.5 %all-to-all-start.1 = ((bf16[128,24,128]{2,1,0:T(8,128)(2,1)}), bf16[128,24,128]{2,1,0:T(8,128)(2,1)S(1)}, u32[]{:S(2)}, u32[]{:S(2)}) async-start(bf16[128,24,128]{2,1,0:T(8,128)(2,1)} %bitcast.44), calls=%async_computation.1 | async-start | bytes 1572864 | tf_op jit(solution)/shard_map/all_to_all | solution.py:499
  18.3 8.7 %gather_states.1 = bf16[512,64,128]{2,1,0:T(8,128)(2,1)} custom-call(s32[512]{0:T(512)} %prompt_ref.3, bf16[32,64,128]{2,1,0:T(8,128)(2,1)} %bitcast.99), custom_call_target="tpu_custom_call" | custom-call | bytes 16000000 | tf_op jit(solution)/shard_map/gather_states/pallas_call | solution.py:500
  27.0 7.8 %all-to-all-done.1 = bf16[128,24,128]{2,1,0:T(8,128)(2,1)S(1)} async-done(((bf16[128,24,128]{2,1,0:T(8,128)(2,1)}), bf16[128,24,128]{2,1,0:T(8,128)(2,1)S(1)}, u32[]{:S(2)}, u32[]{:S(2)}) %all-to-all-start.1) | async-done | bytes 786464 | tf_op jit(solution)/shard_map/all_to_all | solution.py:499
  34.8 5.8 %all-to-all-start = ((bf16[128,4,64,128]{3,2,1,0:T(8,128)(2,1)}), bf16[128,4,64,128]{3,2,1,0:T(8,128)(2,1)}, u32[]{:S(2)}, u32[]{:S(2)}) async-start(bf16[128,4,64,128]{3,2,1,0:T(8,128)(2,1)} %bitcast.83), calls=%async_computation | async-start | bytes 16777216 | tf_op jit(solution)/shard_map/all_to_all | solution.py:513
  42.2 1.1 gather_fusion
  45.5 0.7 fusion.32
  46.7 0.7 copy.113
  47.9 0.7 reshape.296.bx.bb.bc
  48.8 0.7 fusion.22.caus_ref
  50.2 0.8 fusion.26
  50.9 1.0 fusion.9.mask_ref
  52.2 1.0 copy.118
  53.3 0.7 broadcast_in_dim.48.dsk_ref
  54.2 0.8 reshape.290.wx.wb.wc
  55.3 0.7 reshape.286
  55.9 0.8 pad.16.tx.tb.tc
  56.7 18.5 %local_forward.1 = (f32[128,8192]{1,0:T(8,128)}, f32[128,1024]{1,0:T(8,128)}, f32[128,1024]{1,0:T(8,128)}, f32[128,8192]{1,0:T(8,128)}, f32[128,1024]{1,0:T(8,12...) custom-call(bf16[128,10240]{1,0:T(8,128)(2,1)} %cr.3, ...), custom_call_target="tpu_custom_call" | custom-call | bytes 95000000 | tf_op jit(solution)/shard_map/local_forward/pallas_call | solution.py:576
  75.2 71.8 %all-to-all-done.st_ref = bf16[128,4,64,128]{3,2,1,0:T(8,128)(2,1)} async-done(((bf16[128,4,64,128]{3,2,1,0:T(8,128)(2,1)}), bf16[128,4,64,128]{3,2,1,0:T(8,128)(2,1)}, u32[]{:S(2)}, u32[]{:S(2)}) %all-to-all-start) | async-done | bytes 8388640 | tf_op jit(solution)/shard_map/all_to_all | solution.py:513
  146.9 5.9 %all-to-all-start.2 = ((s16[32,128,128]{2,1,0:T(8,128)(2,1)}), s16[32,128,128]{2,1,0:T(8,128)(2,1)S(1)}, u32[]{:S(2)}, u32[]{:S(2)}) async-start(s16[32,128,128]{2,1,0:T(8,128)(2,1)} %get-tuple-element.86), calls=%async_computation.2 | async-start | bytes 2097152 | tf_op jit(solution)/shard_map/all_to_all | solution.py:592
  152.8 0.7 copy.119.tokw_ref
  153.7 0.7 copy.128
  154.3 13.9 %norm_both_ways.1 = (bf16[128,8192]{1,0:T(8,128)(2,1)}, f32[128,8192]{1,0:T(8,128)}, s16[128,72,128]{2,1,0:T(8,128)(2,1)}, f32[8,8192]{1,0:T(8,128)}, f32[128,128]{1,0:T(8,128)}) custom-call(bf16[128,4,64,128]{3,2,1,0:T(8,128)(2,1)} %all-to-all-done.st_ref, f32[128,1024]{1,0:T(8,128)} %get-tuple-element.78.c_ref, f32[128,8192]{1,0:T(8,128)} %get-tuple-element.79.m0_ref, ...), custom_call_target="tpu_custom_call" | custom-call | bytes 52000000 | tf_op jit(solution)/shard_map/norm_both_ways/pallas_call | solution.py:593
  168.3 2.1 all-to-all-done.2.c0_ref
  170.3 8.0 %all-to-all-start.3 = ((s16[128,72,128]{2,1,0:T(8,128)(2,1)}), s16[128,72,128]{2,1,0:T(8,128)(2,1)S(1)}, u32[]{:S(2)}, u32[]{:S(2)}) async-start(s16[128,72,128]{2,1,0:T(8,128)(2,1)} %get-tuple-element.106), calls=%async_computation.3 | async-start | bytes 4718592 | tf_op jit(solution)/shard_map/all_to_all | solution.py:607
  178.3 1.5 collective-permute-start
  179.8 1.2 collective-permute-start.1
  181.0 1.4 collective-permute-start.2
  182.3 0.7 copy.120.rate_ref
  183.1 0.7 copy.121.skip_ref
  183.8 30.8 %local_backward.1 = (bf16[128,8192]{1,0:T(8,128)(2,1)}, bf16[128,1024]{1,0:T(8,128)(2,1)}, bf16[128,1024]{1,0:T(8,128)(2,1)}, f32[128,128]{1,0:T(8,128)}, f32[128,24,128]{2,1,0:T(8,128)}) custom-call(bf16[128,4,64,128]{3,2,1,0:T(8,128)(2,1)} %all-to-all-done.st_ref, f32[128,8192]{1,0:T(8,128)} %get-tuple-element.87.dm_ref, ...), custom_call_target="tpu_custom_call" | custom-call | bytes 133000000 | tf_op jit(solution)/shard_map/local_backward/pallas_call | solution.py:609
  214.6 13.0 %collective-permute-done.c1_ref = s16[32,128,128]{2,1,0:T(8,128)(2,1)} collective-permute-done((s16[32,128,128]{2,1,0:T(8,128)(2,1)S(1)}, s16[32,128,128]{2,1,0:T(8,128)(2,1)}, u32[]{:S(2)}, u32[]{:S(2)}) %collective-permute-start) | collective-permute-done | bytes 1048608 | tf_op jit(solution)/shard_map/ppermute | solution.py:606
  227.7 1.0 collective-permute-done.2.c3_ref
  228.7 9.4 %all-to-all-start.4 = ((f32[128,24,128]{2,1,0:T(8,128)}), f32[128,24,128]{2,1,0:T(8,128)}, u32[]{:S(2)}, u32[]{:S(2)}) async-start(f32[128,24,128]{2,1,0:T(8,128)} %get-tuple-element.120), calls=%async_computation.4 | async-start | bytes 3145728 | tf_op jit(solution)/shard_map/all_to_all | solution.py:630
  238.1 0.7 copy.122
  238.9 15.0 %state_gradients.1 = f32[32,64,128]{2,1,0:T(8,128)} custom-call(s32[4,32]{1,0:T(4,128)} %gather_fusion, s32[512]{0:T(512)} %prompt_ref.3, s16[128,72,128]{2,1,0:T(8,128)(2,1)} %copy-done, s16[32,128,128]{2,1,0:T(8,128)(2,1)} %copy-done.1, s16[32,128,128]{2,1,0:T(8,128)(2,1)} %collective-permute-done.c1_ref, ...), custom_call_target="tpu_custom_call" | custom-call | bytes 60000000 | tf_op jit(solution)/shard_map/state_gradients/pallas_call | solution.py:632
  253.9 1.7 pad_maximum_fusion
  255.6 7.2 %all-to-all-done.4.back_ref = f32[128,24,128]{2,1,0:T(8,128)} async-done(((f32[128,24,128]{2,1,0:T(8,128)}), f32[128,24,128]{2,1,0:T(8,128)}, u32[]{:S(2)}, u32[]{:S(2)}) %all-to-all-start.4) | async-done | bytes 1572896 | tf_op jit(solution)/shard_map/all_to_all | solution.py:630
  262.8 2.7 %finish.1 = (f32[32,3,80]{2,1,0:T(4,128)}, f32[4,320]{1,0:T(4,128)}, f32[1,320]{1,0:T(1,128)}, f32[1,256]{1,0:T(1,128)}, f32[1,128]{1,0:T(1,128)}) custom-call(f32[128,24,128]{2,1,0:T(8,128)} %all-to-all-done.4.back_ref, bf16[32,512]{1,0:T(8,128)(2,1)} %fusion.20.member_ref), custom_call_target="tpu_custom_call" | custom-call | bytes 10000000 | tf_op jit(solution)/shard_map/finish/pallas_call | solution.py:648
  265.5 1.5 copy.124
  267.0 0.7 slice_reduce_fusion.3
  267.8 0.7 slice_reduce_fusion
  268.5 1.3 reduce
  (92 shorter events, 7.5 us)
Async XLA Ops:
  6.8 28.0 %all-to-all-start.1 = ((bf16[128,24,128]{2,1,0:T(8,128)(2,1)}), bf16[128,24,128]{2,1,0:T(8,128)(2,1)S(1)}, u32[]{:S(2)}, u32[]{:S(2)}) async-start(bf16[128,24,128]{2,1,0:T(8,128)(2,1)} %bitcast.44), calls=%async_computation.1 | async-start | bytes 1572864 | tf_op jit(solution)/shard_map/all_to_all | solution.py:499
  34.8 5.8 %copy-start.10 = (s32[512]{0:T(512)S(1)}, s32[512]{0:T(512)}, u32[]{:S(2)}) copy-start(s32[512]{0:T(512)} %prompt_ref.3) | copy-start | bytes 6148
  34.8 5.9 %copy-start.8 = (f32[128,128]{1,0:T(8,128)S(1)}, f32[128,128]{1,0:T(8,128)}, u32[]{:S(2)}) copy-start(f32[128,128]{1,0:T(8,128)} %param.18) | copy-start | bytes 196612
  34.8 6.1 %copy-start.11 = (f32[512]{0:T(512)S(1)}, f32[512]{0:T(512)}, u32[]{:S(2)}) copy-start(f32[512]{0:T(512)} %param.23) | copy-start | bytes 6148
  34.8 7.4 %copy-start.7 = (s32[4,32]{1,0:T(4,128)S(1)}, s32[4,32]{1,0:T(4,128)}, u32[]{:S(2)}) copy-start(s32[4,32]{1,0:T(4,128)} %constant.60.clone) | copy-start | bytes 1540
  34.8 112.1 %all-to-all-start = ((bf16[128,4,64,128]{3,2,1,0:T(8,128)(2,1)}), bf16[128,4,64,128]{3,2,1,0:T(8,128)(2,1)}, u32[]{:S(2)}, u32[]{:S(2)}) async-start(bf16[128,4,64,128]{3,2,1,0:T(8,128)(2,1)} %bitcast.83), calls=%async_computation | async-start | bytes 16777216 | tf_op jit(solution)/shard_map/all_to_all | solution.py:513
  40.6 4.7 %copy-start.12 = (s32[1,4]{1,0:T(1,128)S(1)}, s32[1,4]{1,0:T(1,128)}, u32[]{:S(2)}) copy-start(s32[1,4]{1,0:T(1,128)} %param.22) | copy-start | bytes 52
  46.7 10.0 %copy-start.3 = (bf16[384,16]{1,0:T(8,128)(2,1)}, bf16[384,16]{1,0:T(8,128)(2,1)S(1)}, u32[]{:S(2)}) copy-start(bf16[384,16]{1,0:T(8,128)(2,1)S(1)} %pad_convert_fusion.sel_ref) | copy-start | bytes 36868
  52.2 4.5 %copy-start.4 = (f32[128,128]{0,1:T(8,128)}, f32[128,128]{0,1:T(8,128)S(1)}, u32[]{:S(2)}) copy-start(f32[128,128]{0,1:T(8,128)S(1)} %fusion.15) | copy-start | bytes 196612
  146.9 23.4 %all-to-all-start.2 = ((s16[32,128,128]{2,1,0:T(8,128)(2,1)}), s16[32,128,128]{2,1,0:T(8,128)(2,1)S(1)}, u32[]{:S(2)}, u32[]{:S(2)}) async-start(s16[32,128,128]{2,1,0:T(8,128)(2,1)} %get-tuple-element.86), calls=%async_computation.2 | async-start | bytes 2097152 | tf_op jit(solution)/shard_map/all_to_all | solution.py:592
  170.3 44.3 %copy-start.1 = (s16[32,128,128]{2,1,0:T(8,128)(2,1)}, s16[32,128,128]{2,1,0:T(8,128)(2,1)S(1)}, u32[]{:S(2)}) copy-start(s16[32,128,128]{2,1,0:T(8,128)(2,1)S(1)} %all-to-all-done.2.c0_ref) | copy-start | bytes 3145732
  170.3 58.3 %all-to-all-start.3 = ((s16[128,72,128]{2,1,0:T(8,128)(2,1)}), s16[128,72,128]{2,1,0:T(8,128)(2,1)S(1)}, u32[]{:S(2)}, u32[]{:S(2)}) async-start(s16[128,72,128]{2,1,0:T(8,128)(2,1)} %get-tuple-element.106), calls=%async_computation.3 | async-start | bytes 4718592 | tf_op jit(solution)/shard_map/all_to_all | solution.py:607
  178.3 49.3 %collective-permute-start = (s16[32,128,128]{2,1,0:T(8,128)(2,1)S(1)}, s16[32,128,128]{2,1,0:T(8,128)(2,1)}, u32[]{:S(2)}, u32[]{:S(2)}) collective-permute-start(s16[32,128,128]{2,1,0:T(8,128)(2,1)S(1)} %all-to-all-done.2.c0_ref), channel_id=1, source_target_pairs={{0,1},{1,0},{2,3},{3,2},{4,5},{5,4},{6,7},{7,6},{8,9},{9,8},{10,11... | collective-permute-start | bytes 3145736 | tf_op jit(solution)/shard_map/ppermute | solution.py:606
  179.8 47.9 %collective-permute-start.1 = (s16[32,128,128]{2,1,0:T(8,128)(2,1)S(1)}, s16[32,128,128]{2,1,0:T(8,128)(2,1)}, u32[]{:S(2)}, u32[]{:S(2)}) collective-permute-start(s16[32,128,128]{2,1,0:T(8,128)(2,1)S(1)} %all-to-all-done.2.c0_ref), channel_id=1, source_target_pairs={{0,2},{1,3},{2,0},{3,1},{4,6},{5,7},{6,4},{7,5},{8,10},{9,11},{10,... | collective-permute-start | bytes 3145736 | tf_op jit(solution)/shard_map/ppermute | solution.py:606
  181.0 47.7 %collective-permute-start.2 = (s16[32,128,128]{2,1,0:T(8,128)(2,1)S(1)}, s16[32,128,128]{2,1,0:T(8,128)(2,1)}, u32[]{:S(2)}, u32[]{:S(2)}) collective-permute-start(s16[32,128,128]{2,1,0:T(8,128)(2,1)S(1)} %all-to-all-done.2.c0_ref), channel_id=1, source_target_pairs={{0,8},{1,9},{2,10},{3,11},{4,12},{5,13},{6,14},{7,15},{8,0},{9,1},... | collective-permute-start | bytes 3145736 | tf_op jit(solution)/shard_map/ppermute | solution.py:606
  214.6 23.5 %copy-start.9 = (f32[128,128]{1,0:T(8,128)S(1)}, f32[128,128]{1,0:T(8,128)}, u32[]{:S(2)}) copy-start(f32[128,128]{1,0:T(8,128)} %get-tuple-element.112) | copy-start | bytes 196612
  228.7 10.2 %copy-start = (s16[128,72,128]{2,1,0:T(8,128)(2,1)}, s16[128,72,128]{2,1,0:T(8,128)(2,1)S(1)}, u32[]{:S(2)}) copy-start(s16[128,72,128]{2,1,0:T(8,128)(2,1)S(1)} %all-to-all-done.3.q_ref) | copy-start | bytes 7077892
  228.7 34.1 %all-to-all-start.4 = ((f32[128,24,128]{2,1,0:T(8,128)}), f32[128,24,128]{2,1,0:T(8,128)}, u32[]{:S(2)}, u32[]{:S(2)}) async-start(f32[128,24,128]{2,1,0:T(8,128)} %get-tuple-element.120), calls=%async_computation.4 | async-start | bytes 3145728 | tf_op jit(solution)/shard_map/all_to_all | solution.py:630
  238.8 15.0 %copy-start.2 = (bf16[128,8192]{1,0:T(8,128)(2,1)S(1)}, bf16[128,8192]{1,0:T(8,128)(2,1)}, u32[]{:S(2)}) copy-start(bf16[128,8192]{1,0:T(8,128)(2,1)} %get-tuple-element.108) | copy-start | bytes 6291460
  238.8 15.0 %copy-start.5 = (bf16[128,1024]{1,0:T(8,128)(2,1)S(1)}, bf16[128,1024]{1,0:T(8,128)(2,1)}, u32[]{:S(2)}) copy-start(bf16[128,1024]{1,0:T(8,128)(2,1)} %get-tuple-element.109) | copy-start | bytes 786436
  238.8 15.0 %copy-start.6 = (bf16[128,1024]{1,0:T(8,128)(2,1)S(1)}, bf16[128,1024]{1,0:T(8,128)(2,1)}, u32[]{:S(2)}) copy-start(bf16[128,1024]{1,0:T(8,128)(2,1)} %get-tuple-element.110) | copy-start | bytes 786436

commit v3 on v2

--- a/solution.py
+++ b/solution.py
@@ -295,8 +295,8 @@
     gdt_o[...] = d_dt
     lane = lanes(HG)
     heads = jnp.where(lane == 0, jnp.sum(d_dt, axis=1, keepdims=True), 0.0)
-    heads = jnp.where(lane == 1, -jnp.sum(step * rate * d_decay, axis=1, keepdims=True), heads)
-    heads = jnp.where(lane == 2, jnp.sum(rx, axis=1, keepdims=True), heads)
+    heads = jnp.where(lane == 4, -jnp.sum(step * rate * d_decay, axis=1, keepdims=True), heads)
+    heads = jnp.where(lane == 8, jnp.sum(rx, axis=1, keepdims=True), heads)
     heads_s[pl.ds(pl.multiple_of(group * HG, HG), HG), :] = heads
 
     @pl.when(group == G - 1)
@@ -334,9 +334,9 @@
             extra = jnp.where(row == k, piece, extra)
         tile = heads[8 * (f // 2) : 8 * (f // 2) + 8, :]
         for i in range(4):
-            moved = pltpu.roll(tile, 80 + 3 * i, axis=1)
+            moved = pltpu.roll(tile, 80 + i, axis=1)
             moved = pltpu.roll(moved, (7 - 4 * (f % 2) - i) % 8, axis=0)
-            here = (row == 7) & (lane >= 80 + 3 * i) & (lane < 83 + 3 * i)
+            here = (row == 7) & (lane >= 80) & (lane < 92) & (lane % 4 == i)
             extra = jnp.where(here, moved, extra)
         for p in range(4):
             m = 32 * p + f
@@ -346,12 +346,12 @@
             out[m, 16:24, :] = last
 
 
-def finish_kernel(back_ref, member_ref, tails_o, w_o, b_o, g_o, heads_o):
+def finish_kernel(back_ref, member_ref, tails_o, w_o, b_o, g_o, *heads_o):
     for j in range(3):
         rows = cat([back_ref[:, 3 * d + j, :] for d in range(DOCS)], 0)
         got = mm(member_ref[...], cat(three_parts(rows), 1))
         got = got[:, :128] + (got[:, 128:256] + got[:, 256:])
-        tails_o[:, j, :] = got[:, :80]
+        tails_o[j] = got[:, :80]
     total = jnp.sum(back_ref[...], axis=0)
     w_o[...] = cat([total[12:16], total[16:20], total[20:24, :64]], 1)
     lane = lax.broadcasted_iota(jnp.int32, (1, 128), 1)
@@ -366,8 +366,9 @@
     for k in range(7):
         here = (row == k) & (wide >= 48 * k) & (wide < 48 * k + 48)
         bias = jnp.where(here, pltpu.roll(spread, (48 * k - 80) % 384, axis=1), bias)
-    b_o[...] = jnp.sum(bias, axis=0, keepdims=True)[:, :320]
-    heads_o[...] = pltpu.roll(total[:8], 48, axis=1)[7:8]
+    b_o[...] = jnp.sum(bias, axis=0)[:320]
+    for i in range(3):
+        heads_o[i][...] = pltpu.roll(total[:8], 48 - 4 * i, axis=1)[7:8, :4]
 
 
 def three_parts(a):
@@ -480,7 +481,8 @@
     count = weights.shape[0]
     weights = jnp.pad(weights, (0, 2048 - count))
     quarter = lax.dynamic_slice_in_dim(weights, dp * 512, 512)
-    quarter = cat(three(quarter), 0)
+    parts = three(quarter)
+    quarter = cat(parts[:2], 0)
     onehot = resp_prompt[:, None] == jnp.arange(PROMPTS, dtype=jnp.int32)[None, :]
     tails_sent = jnp.dot(
         onehot.astype(BF16), conv_tails.reshape(PROMPTS, 240), preferred_element_type=F32
@@ -490,13 +492,12 @@
         [
             tails_sent.reshape(devices, 960),
             lengths_f,
-            jnp.zeros((devices, 60), BF16),
-            jnp.broadcast_to(quarter[None], (devices, 1536)),
-            jnp.zeros((devices, 512), BF16),
+            jnp.broadcast_to(jnp.pad(parts[2][64:80], (0, 44))[None], (devices, 60)),
+            jnp.broadcast_to(quarter[None], (devices, 1024)),
         ],
         1,
     )
-    got = exchange(sent.reshape(devices, 24, 128)).reshape(devices, 3072)
+    got = exchange(sent.reshape(devices, 16, 128)).reshape(devices, 2048)
     states = pl.pallas_call(
         gather_kernel,
         grid_spec=pltpu.PrefetchScalarGridSpec(
@@ -516,7 +517,8 @@
     tails = got[:, :960].reshape(devices, 12, 80).transpose(1, 0, 2).reshape(12, CONV)
     tails = jnp.pad(tails, ((0, 4), (0, 0)))
     all_lengths = got[:, 960:964].astype(jnp.int32)
-    full = sum(got[:, i : i + 512].astype(F32) for i in (2048, 1536, 1024))
+    third = jnp.pad(got[:, 964:980].astype(F32), ((0, 0), (64, 432)))
+    full = third + got[:, 1536:].astype(F32) + got[:, 1024:1536].astype(F32)
     full = full.reshape(n_dp, n_fsdp, 512).transpose(1, 0, 2).reshape(n_fsdp, 2048)
     conv_w = full[:, :1280].reshape(n_fsdp, 4, 320).transpose(1, 0, 2).reshape(4, CONV)
     conv_b = full[:, 1280:1600].reshape(1, CONV)
@@ -562,7 +564,10 @@
 
     groups = classes(devices)
     order = jnp.asarray(groups, jnp.int32)[color(holder) ^ jnp.arange(4, dtype=jnp.int32)]
-    rate_t, skip_t, sig_t = rate.T, skip.T, jax.nn.sigmoid(raw_step).T
+    sig_t = jax.nn.sigmoid(raw_step).T
+    rate_t, skip_t = jnp.broadcast_to(rate.T, (H, 128)), jnp.broadcast_to(skip.T, (H, 128))
+    tokw = jnp.broadcast_to(tokw, (T, 128))
+    member_f = jnp.pad(member_f, ((0, 0), (0, 128 - DOCS)))
     (offset, sel, sel_rows, causal, member_f, members, mask_rows, tokw, order, rate_t, skip_t, sig_t, step_t,
      conv_b) = lax.optimization_barrier(
         (offset, sel, sel_rows, causal, member_f, members, mask_rows, tokw, order, rate_t, skip_t, sig_t,
@@ -594,7 +599,7 @@
         norm_kernel,
         (4,),
         [lead(32, DOCS, P_SIZE, N), cols(T, 2 * N), cols(T, GS), cols(T, GS), cols(T, GS), cols(T, GS),
-         cols(1, GS), whole((T, 1)), whole((T, DOCS)), lead(2, 1, T)],
+         cols(1, GS), whole((T, 128)), whole((T, 128)), lead(2, 1, T)],
         [cols(T, GS), cols(T, GS), lead(32, Q_ROWS, T), cols(8, GS), lead(32, T)],
         [shape((T, DI), BF16), shape((T, DI)), shape((H, Q_ROWS, T), jnp.int16),
          shape((8, DI)), shape((H, T))],
@@ -612,8 +617,8 @@
         [lead(HG, DOCS, P_SIZE, N), cols(T, GC), cols(T, GC), lead(HG, T, T), lead(1, T, T),
          cols(T, GC), cols(T, N), cols(T, N), cols(T, GC), cols(T, N), cols(T, N)]
         + conv_specs + tail_specs + tap_specs
-        + [whole((T, 1)), whole((48, T)), whole((T, DOCS)), cols(1, GC), whole((T, T)), lead(HG, T),
-           lead(HG, T), lead(HG, T), lead(HG, 1), lead(HG, 1), whole((8, DI))],
+        + [whole((T, 1)), whole((48, T)), whole((T, 128)), cols(1, GC), whole((T, T)), lead(HG, T),
+           lead(HG, T), lead(HG, T), lead(HG, 128), lead(HG, 128), whole((8, DI))],
         [cols(T, GC), cols(T, N), cols(T, N), lead(HG, T), whole((devices, 24, 128))],
         [shape((T, DI), BF16), shape((T, G * N), BF16), shape((T, G * N), BF16), shape((H, T)),
          shape((devices, 24, 128))],
@@ -623,9 +628,7 @@
       conv_w, conv_w, conv_w, offset, sel_rows, member_f, skip_wide, causal, rs, step_t,
       sig_t, rate_t, skip_t, d_gain)
 
-    gx, gb, gc, grad_dt, back, got_q, *near = lax.optimization_barrier(
-        (gx, gb, gc, grad_dt, back, got_q, *near)
-    )
+    gx, gb, gc, grad_dt, back, got_q = lax.optimization_barrier((gx, gb, gc, grad_dt, back, got_q))
     grad_x = cat([gx, gb, gc], 1)
     back = exchange(back)
 
@@ -645,26 +648,25 @@
     )(order, resp_prompt, got_q, *near, mask_rows)
 
     share = CONV // n_fsdp
-    grad_tails, grad_w, grad_b, grad_gain, heads = call(
+    grad_tails, grad_w, grad_b, grad_gain, *heads = call(
         finish_kernel,
         (1,),
         [whole((devices, 24, 128)), whole((PROMPTS, devices * DOCS))],
-        [whole((PROMPTS, 3, 80)), whole((4, share)), whole((1, share)), whole((1, 256)), whole((1, 128))],
-        [shape((PROMPTS, 3, 80)), shape((4, share)), shape((1, share)), shape((1, 256)), shape((1, 128))],
+        [whole((3, PROMPTS, 80)), whole((4, share)), whole((share,)), whole((1, 256))] + [whole((1, 4))] * 3,
+        [shape((3, PROMPTS, 80)), shape((4, share)), shape((share,)), shape((1, 256))] + [shape((1, 4))] * 3,
         "finish", 0, 10 * 10**6,
     )(back, members)
-    heads = heads[0, :12].reshape(4, 3)
     return (
         grad_x,
         grad_z,
         grad_dt.T,
         grad_states.reshape(PROMPTS, 1, P_SIZE, N),
-        grad_tails,
+        grad_tails.transpose(1, 0, 2),
         grad_w,
-        grad_b.reshape(share),
-        heads[:, 0],
-        heads[:, 1],
-        heads[:, 2],
+        grad_b,
+        heads[0].reshape(4),
+        heads[1].reshape(4),
+        heads[2].reshape(4),
         grad_gain.reshape(256),
     )
 

time: 271 us -> 256 us (0.945)
  the two profiles are of different devices: /device:TPU:1 before, /device:TPU:90 now
where the time goes in v3:
time: 256 us; the launch traced here: 255 us
  Pallas kernels  89.7 us (35%)
  waiting for transfers between devices  81.9 us (32%)
  starting transfers between devices  56.3 us (22%)
  local copies, waits for them, and re-layouts  16.7 us (7%)
  other arithmetic  7 us (3%)
    all_to_all x1, waiting for transfers between devices, shards(): states = exchange(states.reshape(devices, DOCS, P_SIZE, N))  63.5 us
    pallas_call x1, Pallas kernels, shards(): call(back_kernel, (G,), [lead(HG, DOCS, P_SIZE, N), cols(T, GC), cols(T,...  30.9 us
    pallas_call x1, Pallas kernels, shards(): call(local_kernel, (G,), conv_specs + tail_specs + tap_specs + bias_specs...  18.6 us
    ppermute x3, waiting for transfers between devices, shards(): lax.ppermute(near[0], AXES, [(d, d ^ bit) for d in range(devices)])  16.9 us
    pallas_call x1, Pallas kernels, shards(): pl.pallas_call(state_kernel, grid_spec=pltpu.PrefetchScalarGridSpec(num_s...  14.9 us
    pallas_call x1, Pallas kernels, shards(): call(norm_kernel, (4,), [lead(32, DOCS, P_SIZE, N), cols(T, 2 * N), cols(...  13.9 us
    all_to_all x1, starting transfers between devices, shards(): lax.all_to_all(cq, AXES, 0, 0, axis_index_groups=groups, tiled=True)  11.3 us
    all_to_all x1, starting transfers between devices, shards(): back = exchange(back)  11.3 us
  transfers between devices with their start and end apart: 8, of which 3 were waited for; matrix products, arithmetic and copies ran while one was open for 8% of the time, Pallas kernels for 34%

profile of v3, /device:TPU:90, one launch (start us, length us, event | category | flops | bytes accessed | tf_op | source)
XLA Modules:
  0.0 255.2 jit_solution(9920815101853716183)
XLA Ops:
  0.6 0.7 convert_bitcast_fusion
  1.3 0.8 reshape.283
  2.1 0.8 concatenate.12
  3.1 0.8 copy.87
  3.9 1.0 convolution_convert_fusion
  5.1 0.4 reshape.282
  5.8 0.9 copy.106
  6.7 9.9 %all-to-all-start.1 = ((bf16[128,16,128]{2,1,0:T(8,128)(2,1)}), bf16[128,16,128]{2,1,0:T(8,128)(2,1)S(1)}, u32[]{:S(2)}, u32[]{:S(2)}) async-start(bf16[128,16,128]{2,1,0:T(8,128)(2,1)} %bitcast.47), calls=%async_computation.1 | async-start | bytes 1048576 | tf_op jit(solution)/shard_map/all_to_all | solution.py:500
  16.6 8.6 %gather_states.1 = bf16[512,64,128]{2,1,0:T(8,128)(2,1)} custom-call(s32[512]{0:T(512)} %prompt_ref.3, bf16[32,64,128]{2,1,0:T(8,128)(2,1)} %bitcast.103), custom_call_target="tpu_custom_call" | custom-call | bytes 16000000 | tf_op jit(solution)/shard_map/gather_states/pallas_call | solution.py:501
  25.3 10.9 %all-to-all-start = ((bf16[128,4,64,128]{3,2,1,0:T(8,128)(2,1)}), bf16[128,4,64,128]{3,2,1,0:T(8,128)(2,1)}, u32[]{:S(2)}, u32[]{:S(2)}) async-start(bf16[128,4,64,128]{3,2,1,0:T(8,128)(2,1)} %bitcast.86), calls=%async_computation | async-start | bytes 16777216 | tf_op jit(solution)/shard_map/all_to_all | solution.py:514
  36.5 0.3 fusion.1
  36.8 0.3 fusion.7
  37.2 0.3 fusion.5
  37.5 0.3 fusion.6
  37.8 1.1 gather_fusion
  39.0 0.6 fusion.20.member_ref
  39.6 0.5 copy.89
  41.2 0.7 copy.97
  42.2 0.7 reshape.297.bx.bb.bc
  43.5 0.8 reshape.291.wx.wb.wc
  44.4 0.7 broadcast_in_dim.54.dsk_ref
  45.3 0.6 iota_subtract_fusion.off_ref
  45.9 0.7 pad_convert_fusion.1
  46.6 0.8 fusion.26
  47.4 1.0 fusion.9.mask_ref
  48.5 0.7 broadcast_in_dim.45.tokw_ref
  49.1 0.7 broadcast_in_dim.50.rate_ref
  49.8 0.7 broadcast_in_dim.52.skip_ref
  50.8 0.7 reshape.287
  51.4 0.8 pad.35.tx.tb.tc
  52.5 1.0 copy.102
  53.5 18.6 %local_forward.1 = (f32[128,8192]{1,0:T(8,128)}, f32[128,1024]{1,0:T(8,128)}, f32[128,1024]{1,0:T(8,128)}, f32[128,8192]{1,0:T(8,128)}, f32[128,1024]{1,0:T(8,12...) custom-call(bf16[128,10240]{1,0:T(8,128)(2,1)} %cr.3, ...), custom_call_target="tpu_custom_call" | custom-call | bytes 95000000 | tf_op jit(solution)/shard_map/local_forward/pallas_call | solution.py:581
  72.1 63.5 %all-to-all-done.st_ref = bf16[128,4,64,128]{3,2,1,0:T(8,128)(2,1)} async-done(((bf16[128,4,64,128]{3,2,1,0:T(8,128)(2,1)}), bf16[128,4,64,128]{3,2,1,0:T(8,128)(2,1)}, u32[]{:S(2)}, u32[]{:S(2)}) %all-to-all-start) | async-done | bytes 8388640 | tf_op jit(solution)/shard_map/all_to_all | solution.py:514
  135.5 11.3 %all-to-all-start.2 = ((s16[32,128,128]{2,1,0:T(8,128)(2,1)}), s16[32,128,128]{2,1,0:T(8,128)(2,1)S(1)}, u32[]{:S(2)}, u32[]{:S(2)}) async-start(s16[32,128,128]{2,1,0:T(8,128)(2,1)} %get-tuple-element.84), calls=%async_computation.2 | async-start | bytes 2097152 | tf_op jit(solution)/shard_map/all_to_all | solution.py:597
  147.0 0.7 copy.108
  147.6 13.9 %norm_both_ways.1 = (bf16[128,8192]{1,0:T(8,128)(2,1)}, f32[128,8192]{1,0:T(8,128)}, s16[128,72,128]{2,1,0:T(8,128)(2,1)}, f32[8,8192]{1,0:T(8,128)}, f32[128,128]{1,0:T(8,128)}) custom-call(bf16[128,4,64,128]{3,2,1,0:T(8,128)(2,1)} %all-to-all-done.st_ref, f32[128,1024]{1,0:T(8,128)} %get-tuple-element.76.c_ref, f32[128,8192]{1,0:T(8,128)} %get-tuple-element.77.m0_ref, ...), custom_call_target="tpu_custom_call" | custom-call | bytes 52000000 | tf_op jit(solution)/shard_map/norm_both_ways/pallas_call | solution.py:598
  161.5 1.5 all-to-all-done.2.c0_ref
  163.0 10.0 %all-to-all-start.3 = ((s16[128,72,128]{2,1,0:T(8,128)(2,1)}), s16[128,72,128]{2,1,0:T(8,128)(2,1)S(1)}, u32[]{:S(2)}, u32[]{:S(2)}) async-start(s16[128,72,128]{2,1,0:T(8,128)(2,1)} %get-tuple-element.104), calls=%async_computation.3 | async-start | bytes 4718592 | tf_op jit(solution)/shard_map/all_to_all | solution.py:612
  173.1 1.5 collective-permute-start.2
  174.6 0.8 collective-permute-start.1
  175.4 0.5 collective-permute-start
  175.9 30.9 %local_backward.1 = (bf16[128,8192]{1,0:T(8,128)(2,1)}, bf16[128,1024]{1,0:T(8,128)(2,1)}, bf16[128,1024]{1,0:T(8,128)(2,1)}, f32[128,128]{1,0:T(8,128)}, f32[128,24,128]{2,1,0:T(8,128)}) custom-call(bf16[128,4,64,128]{3,2,1,0:T(8,128)(2,1)} %all-to-all-done.st_ref, f32[128,8192]{1,0:T(8,128)} %get-tuple-element.85.dm_ref, ...), custom_call_target="tpu_custom_call" | custom-call | bytes 133000000 | tf_op jit(solution)/shard_map/local_backward/pallas_call | solution.py:614
  206.9 11.3 %all-to-all-start.4 = ((f32[128,24,128]{2,1,0:T(8,128)}), f32[128,24,128]{2,1,0:T(8,128)}, u32[]{:S(2)}, u32[]{:S(2)}) async-start(f32[128,24,128]{2,1,0:T(8,128)} %get-tuple-element.114), calls=%async_computation.4 | async-start | bytes 3145728 | tf_op jit(solution)/shard_map/all_to_all | solution.py:633
  218.1 0.7 copy.103
  218.9 16.9 %collective-permute-done.2.c3_ref = s16[32,128,128]{2,1,0:T(8,128)(2,1)} collective-permute-done((s16[32,128,128]{2,1,0:T(8,128)(2,1)S(1)}, s16[32,128,128]{2,1,0:T(8,128)(2,1)}, u32[]{:S(2)}, u32[]{:S(2)}) %collective-permute-start.2) | collective-permute-done | bytes 1048608 | tf_op jit(solution)/shard_map/ppermute | solution.py:611
  235.8 14.9 %state_gradients.1 = f32[32,64,128]{2,1,0:T(8,128)} custom-call(s32[4,32]{1,0:T(4,128)} %gather_fusion, s32[512]{0:T(512)} %prompt_ref.3, s16[128,72,128]{2,1,0:T(8,128)(2,1)} %copy-done, s16[32,128,128]{2,1,0:T(8,128)(2,1)} %copy-done.1, s16[32,128,128]{2,1,0:T(8,128)(2,1)} %collective-permute-done.c1_ref, ...), custom_call_target="tpu_custom_call" | custom-call | bytes 60000000 | tf_op jit(solution)/shard_map/state_gradients/pallas_call | solution.py:635
  250.7 1.7 pad_maximum_fusion
  252.4 2.7 %finish.1 = (f32[3,32,80]{2,1,0:T(8,128)}, f32[4,320]{1,0:T(4,128)}, f32[320]{0:T(512)}, f32[1,256]{1,0:T(1,128)}, f32[1,4]{1,0:T(1,128)}, /*index=5*/f32[1,4]{1,0:T(1,128)}, f32[1,4]{1,0:T(1,128)}) custom-call(f32[128,24,128]{2,1,0:T(8,128)} %all-to-all-done.4.back_ref, bf16[32,512]{1,0:T(8,128)(2,1)} %fusion.20.member_ref), custom_call_target="tpu_custom_call" | custom-call | bytes 10000000 | tf_op jit(solution)/shard_map/finish/pallas_call | solution.py:651
  (87 shorter events, 3.8 us)
Async XLA Ops:
  6.7 18.5 %all-to-all-start.1 = ((bf16[128,16,128]{2,1,0:T(8,128)(2,1)}), bf16[128,16,128]{2,1,0:T(8,128)(2,1)S(1)}, u32[]{:S(2)}, u32[]{:S(2)}) async-start(bf16[128,16,128]{2,1,0:T(8,128)(2,1)} %bitcast.47), calls=%async_computation.1 | async-start | bytes 1048576 | tf_op jit(solution)/shard_map/all_to_all | solution.py:500
  25.3 10.9 %copy-start.10 = (s32[512]{0:T(512)S(1)}, s32[512]{0:T(512)}, u32[]{:S(2)}) copy-start(s32[512]{0:T(512)} %prompt_ref.3) | copy-start | bytes 6148
  25.3 11.1 %copy-start.8 = (f32[128,128]{1,0:T(8,128)S(1)}, f32[128,128]{1,0:T(8,128)}, u32[]{:S(2)}) copy-start(f32[128,128]{1,0:T(8,128)} %param.18) | copy-start | bytes 196612
  25.3 11.2 %copy-start.11 = (f32[512]{0:T(512)S(1)}, f32[512]{0:T(512)}, u32[]{:S(2)}) copy-start(f32[512]{0:T(512)} %param.23) | copy-start | bytes 6148
  25.3 12.5 %copy-start.7 = (s32[4,32]{1,0:T(4,128)S(1)}, s32[4,32]{1,0:T(4,128)}, u32[]{:S(2)}) copy-start(s32[4,32]{1,0:T(4,128)} %constant.60.clone) | copy-start | bytes 1540
  25.3 110.2 %all-to-all-start = ((bf16[128,4,64,128]{3,2,1,0:T(8,128)(2,1)}), bf16[128,4,64,128]{3,2,1,0:T(8,128)(2,1)}, u32[]{:S(2)}, u32[]{:S(2)}) async-start(bf16[128,4,64,128]{3,2,1,0:T(8,128)(2,1)} %bitcast.86), calls=%async_computation | async-start | bytes 16777216 | tf_op jit(solution)/shard_map/all_to_all | solution.py:514
  36.2 4.1 %copy-start.12 = (s32[1,4]{1,0:T(1,128)S(1)}, s32[1,4]{1,0:T(1,128)}, u32[]{:S(2)}) copy-start(s32[1,4]{1,0:T(1,128)} %param.22) | copy-start | bytes 52
  41.2 12.3 %copy-start.3 = (bf16[384,16]{1,0:T(8,128)(2,1)}, bf16[384,16]{1,0:T(8,128)(2,1)S(1)}, u32[]{:S(2)}) copy-start(bf16[384,16]{1,0:T(8,128)(2,1)S(1)} %pad_convert_fusion.sel_ref) | copy-start | bytes 36868
  52.5 1.0 copy-start.4
  135.5 27.5 %all-to-all-start.2 = ((s16[32,128,128]{2,1,0:T(8,128)(2,1)}), s16[32,128,128]{2,1,0:T(8,128)(2,1)S(1)}, u32[]{:S(2)}, u32[]{:S(2)}) async-start(s16[32,128,128]{2,1,0:T(8,128)(2,1)} %get-tuple-element.84), calls=%async_computation.2 | async-start | bytes 2097152 | tf_op jit(solution)/shard_map/all_to_all | solution.py:597
  163.0 43.8 %copy-start.1 = (s16[32,128,128]{2,1,0:T(8,128)(2,1)}, s16[32,128,128]{2,1,0:T(8,128)(2,1)S(1)}, u32[]{:S(2)}) copy-start(s16[32,128,128]{2,1,0:T(8,128)(2,1)S(1)} %all-to-all-done.2.c0_ref) | copy-start | bytes 3145732
  163.0 43.8 %all-to-all-start.3 = ((s16[128,72,128]{2,1,0:T(8,128)(2,1)}), s16[128,72,128]{2,1,0:T(8,128)(2,1)S(1)}, u32[]{:S(2)}, u32[]{:S(2)}) async-start(s16[128,72,128]{2,1,0:T(8,128)(2,1)} %get-tuple-element.104), calls=%async_computation.3 | async-start | bytes 4718592 | tf_op jit(solution)/shard_map/all_to_all | solution.py:612
  173.1 62.7 %collective-permute-start.2 = (s16[32,128,128]{2,1,0:T(8,128)(2,1)S(1)}, s16[32,128,128]{2,1,0:T(8,128)(2,1)}, u32[]{:S(2)}, u32[]{:S(2)}) collective-permute-start(s16[32,128,128]{2,1,0:T(8,128)(2,1)S(1)} %all-to-all-done.2.c0_ref), channel_id=1, source_target_pairs={{0,8},{1,9},{2,10},{3,11},{4,12},{5,13},{6,14},{7,15},{8,0},{9,1},... | collective-permute-start | bytes 3145736 | tf_op jit(solution)/shard_map/ppermute | solution.py:611
  174.6 61.2 %collective-permute-start.1 = (s16[32,128,128]{2,1,0:T(8,128)(2,1)S(1)}, s16[32,128,128]{2,1,0:T(8,128)(2,1)}, u32[]{:S(2)}, u32[]{:S(2)}) collective-permute-start(s16[32,128,128]{2,1,0:T(8,128)(2,1)S(1)} %all-to-all-done.2.c0_ref), channel_id=1, source_target_pairs={{0,2},{1,3},{2,0},{3,1},{4,6},{5,7},{6,4},{7,5},{8,10},{9,11},{10,... | collective-permute-start | bytes 3145736 | tf_op jit(solution)/shard_map/ppermute | solution.py:611
  175.4 60.4 %collective-permute-start = (s16[32,128,128]{2,1,0:T(8,128)(2,1)S(1)}, s16[32,128,128]{2,1,0:T(8,128)(2,1)}, u32[]{:S(2)}, u32[]{:S(2)}) collective-permute-start(s16[32,128,128]{2,1,0:T(8,128)(2,1)S(1)} %all-to-all-done.2.c0_ref), channel_id=1, source_target_pairs={{0,1},{1,0},{2,3},{3,2},{4,5},{5,4},{6,7},{7,6},{8,9},{9,8},{10,11... | collective-permute-start | bytes 3145736 | tf_op jit(solution)/shard_map/ppermute | solution.py:611
  206.8 11.3 %copy-start.9 = (f32[128,128]{1,0:T(8,128)S(1)}, f32[128,128]{1,0:T(8,128)}, u32[]{:S(2)}) copy-start(f32[128,128]{1,0:T(8,128)} %get-tuple-element.109) | copy-start | bytes 196612
  206.9 28.9 %copy-start = (s16[128,72,128]{2,1,0:T(8,128)(2,1)}, s16[128,72,128]{2,1,0:T(8,128)(2,1)S(1)}, u32[]{:S(2)}) copy-start(s16[128,72,128]{2,1,0:T(8,128)(2,1)S(1)} %all-to-all-done.3.q_ref) | copy-start | bytes 7077892
  206.9 45.6 %all-to-all-start.4 = ((f32[128,24,128]{2,1,0:T(8,128)}), f32[128,24,128]{2,1,0:T(8,128)}, u32[]{:S(2)}, u32[]{:S(2)}) async-start(f32[128,24,128]{2,1,0:T(8,128)} %get-tuple-element.114), calls=%async_computation.4 | async-start | bytes 3145728 | tf_op jit(solution)/shard_map/all_to_all | solution.py:633
  218.9 31.8 %copy-start.2 = (bf16[128,8192]{1,0:T(8,128)(2,1)S(1)}, bf16[128,8192]{1,0:T(8,128)(2,1)}, u32[]{:S(2)}) copy-start(bf16[128,8192]{1,0:T(8,128)(2,1)} %get-tuple-element.105) | copy-start | bytes 6291460
  218.9 31.8 %copy-start.5 = (bf16[128,1024]{1,0:T(8,128)(2,1)S(1)}, bf16[128,1024]{1,0:T(8,128)(2,1)}, u32[]{:S(2)}) copy-start(bf16[128,1024]{1,0:T(8,128)(2,1)} %get-tuple-element.106) | copy-start | bytes 786436
  218.9 31.8 %copy-start.6 = (bf16[128,1024]{1,0:T(8,128)(2,1)S(1)}, bf16[128,1024]{1,0:T(8,128)(2,1)}, u32[]{:S(2)}) copy-start(bf16[128,1024]{1,0:T(8,128)(2,1)} %get-tuple-element.107) | copy-start | bytes 786436

commit v4 on v3

--- a/solution.py
+++ b/solution.py
@@ -21,6 +21,7 @@
 CONV = 10240
 PROMPTS = 32
 AHEAD = 128
+AT_ONCE = 8
 STEPS = 32752.0
 Q_ROWS = 72
 
@@ -388,32 +389,41 @@
         out_ref[i] = table_ref[prompt_ref[step * 32 + i]]
 
 
-def state_kernel(order_ref, prompt_ref, q_ref, c0_ref, c1_ref, c2_ref, c3_ref, mask_ref, out_ref):
-    out_ref[...] = jnp.zeros_like(out_ref)
-
-    def place(s, carry):
-        for kind, c_ref in enumerate((c0_ref, c1_ref, c2_ref, c3_ref)):
-            source = order_ref[kind, s]
-            q = q_ref[source].astype(jnp.int32).astype(F32)
-            scale = jnp.exp2(q[P_SIZE : P_SIZE + 1]) * (1.0 / STEPS**2)
-            hi, lo = split(q[:P_SIZE] * scale)
-            ci = c_ref[s].astype(jnp.int32)
-            low = ci & 255
-            high = (ci - low).astype(F32).astype(BF16)
-            low = low.astype(F32).astype(BF16)
-            rhs = cat([cat([high, low], 1)] * 2, 0)
-            rows = []
-            for d in range(DOCS):
-                m = jnp.broadcast_to(mask_ref[source, d : d + 1, :], (P_SIZE, T)).astype(BF16)
-                rows.append(cat([hi * m, lo * m], 1))
-            got = mm(cat(rows, 0), rhs)
-            got = got[:, :N] + got[:, N:]
+def state_kernel(kinds, order_ref, prompt_ref, q_ref, *refs):
+    c_refs, mask_ref, rest = refs[: len(kinds)], refs[len(kinds)], refs[len(kinds) + 1 :]
+    out_ref = rest[-1]
+    out_ref[...] = rest[0][...] if len(rest) > 1 else jnp.zeros_like(out_ref)
+
+    def product(source, c):
+        q = q_ref[source].astype(jnp.int32).astype(F32)
+        scale = jnp.exp2(q[P_SIZE : P_SIZE + 1]) * (1.0 / STEPS**2)
+        hi, lo = split(q[:P_SIZE] * scale)
+        ci = c.astype(jnp.int32)
+        low = ci & 255
+        high = (ci - low).astype(F32).astype(BF16)
+        low = low.astype(F32).astype(BF16)
+        rhs = cat([cat([high, low], 1)] * 2, 0)
+        rows = []
+        for d in range(DOCS):
+            m = jnp.broadcast_to(mask_ref[source, d : d + 1, :], (P_SIZE, T)).astype(BF16)
+            rows.append(cat([hi * m, lo * m], 1))
+        got = mm(cat(rows, 0), rhs)
+        return got[:, :N] + got[:, N:]
+
+    def place(step, carry):
+        done = []
+        for i in range(AT_ONCE):
+            s = step * AT_ONCE + i
+            for kind, c_ref in zip(kinds, c_refs):
+                source = order_ref[kind, s]
+                done.append((source, product(source, c_ref[s])))
+        for source, got in done:
             for d in range(DOCS):
                 p = prompt_ref[source * DOCS + d]
                 out_ref[p] = out_ref[p] + got[P_SIZE * d : P_SIZE * (d + 1)]
         return carry
 
-    lax.fori_loop(0, c0_ref.shape[0], place, 0)
+    lax.fori_loop(0, c_refs[0].shape[0] // AT_ONCE, place, 0)
 
 
 def whole(shape):
@@ -632,20 +642,26 @@
     grad_x = cat([gx, gb, gc], 1)
     back = exchange(back)
 
-    grad_states = pl.pallas_call(
-        state_kernel,
-        grid_spec=pltpu.PrefetchScalarGridSpec(
-            num_scalar_prefetch=2,
-            grid=(1,),
-            in_specs=[whole((devices, Q_ROWS, T))] + [whole((devices // 4, T, N))] * 4
-            + [whole((devices, DOCS, T))],
-            out_specs=whole((PROMPTS, P_SIZE, N)),
-        ),
-        out_shape=shape((PROMPTS, P_SIZE, N)),
-        compiler_params=pltpu.CompilerParams(vmem_limit_bytes=56 * 1024 * 1024),
-        cost_estimate=pl.CostEstimate(flops=0, bytes_accessed=60 * 10**6, transcendentals=0),
-        name="state_gradients",
-    )(order, resp_prompt, got_q, *near, mask_rows)
+    def add_states(kinds, *before):
+        return pl.pallas_call(
+            functools.partial(state_kernel, kinds),
+            grid_spec=pltpu.PrefetchScalarGridSpec(
+                num_scalar_prefetch=2,
+                grid=(1,),
+                in_specs=[whole((devices, Q_ROWS, T))] + [whole((devices // 4, T, N))] * len(kinds)
+                + [whole((devices, DOCS, T))] + [whole((PROMPTS, P_SIZE, N))] * len(before),
+                out_specs=whole((PROMPTS, P_SIZE, N)),
+            ),
+            out_shape=shape((PROMPTS, P_SIZE, N)),
+            compiler_params=pltpu.CompilerParams(vmem_limit_bytes=56 * 1024 * 1024),
+            cost_estimate=pl.CostEstimate(
+                flops=0, bytes_accessed=15 * 10**6 * len(kinds), transcendentals=0
+            ),
+            name="state_gradients_%d" % len(kinds),
+        )(order, resp_prompt, got_q, *[near[k] for k in kinds], mask_rows, *before)
+
+    grad_states = add_states((0,))
+    grad_states = add_states((1, 2, 3), grad_states)
 
     share = CONV // n_fsdp
     grad_tails, grad_w, grad_b, grad_gain, *heads = call(

time: 256 us -> 251 us (0.980)
  the two profiles are of different devices: /device:TPU:90 before, /device:TPU:1 now
where the time goes in v4:
time: 251 us; the launch traced here: 250 us
  Pallas kernels  89.6 us (36%)
  waiting for transfers between devices  89 us (35%)
  starting transfers between devices  44.3 us (18%)
  local copies, waits for them, and re-layouts  16.7 us (7%)
  other arithmetic  7.01 us (3%)
  matrix products  2.53 us (1%)
    all_to_all x1, waiting for transfers between devices, shards(): states = exchange(states.reshape(devices, DOCS, P_SIZE, N))  70.4 us
    pallas_call x1, Pallas kernels, shards(): call(back_kernel, (G,), [lead(HG, DOCS, P_SIZE, N), cols(T, GC), cols(T,...  30.9 us
    pallas_call x1, Pallas kernels, shards(): call(local_kernel, (G,), conv_specs + tail_specs + tap_specs + bias_specs...  18.6 us
    pallas_call x2, Pallas kernels, add_states(): pl.pallas_call(functools.partial(state_kernel, kinds), grid_spec=pltpu.Pr...  14.8 us
    pallas_call x1, Pallas kernels, shards(): call(norm_kernel, (4,), [lead(32, DOCS, P_SIZE, N), cols(T, 2 * N), cols(...  13.9 us
    all_to_all x1, starting transfers between devices, shards(): got = exchange(sent.reshape(devices, 16, 128)).reshape(devices, 2048)  11.5 us
    all_to_all x1, waiting for transfers between devices, shards(): back = exchange(back)  10.5 us
    all_to_all x1, starting transfers between devices, shards(): back = exchange(back)  10.1 us
  transfers between devices with their start and end apart: 8, of which 4 were waited for; matrix products, arithmetic and copies ran while one was open for 8% of the time, Pallas kernels for 35%

profile of v4, /device:TPU:1, one launch (start us, length us, event | category | flops | bytes accessed | tf_op | source)
XLA Modules:
  0.0 250.2 jit_solution(16190591194316452255)
XLA Ops:
  0.6 0.7 convert_bitcast_fusion
  1.3 0.8 reshape.283
  2.1 0.8 concatenate.12
  3.1 0.8 copy.87
  3.9 1.0 convolution_convert_fusion
  5.1 0.4 reshape.282
  5.8 0.9 copy.106
  6.7 11.5 %all-to-all-start.1 = ((bf16[128,16,128]{2,1,0:T(8,128)(2,1)}), bf16[128,16,128]{2,1,0:T(8,128)(2,1)S(1)}, u32[]{:S(2)}, u32[]{:S(2)}) async-start(bf16[128,16,128]{2,1,0:T(8,128)(2,1)} %bitcast.47), calls=%async_computation.1 | async-start | bytes 1048576 | tf_op jit(solution)/shard_map/all_to_all | solution.py:510
  18.2 8.6 %gather_states.1 = bf16[512,64,128]{2,1,0:T(8,128)(2,1)} custom-call(s32[512]{0:T(512)} %prompt_ref.5, bf16[32,64,128]{2,1,0:T(8,128)(2,1)} %bitcast.103), custom_call_target="tpu_custom_call" | custom-call | bytes 16000000 | tf_op jit(solution)/shard_map/gather_states/pallas_call | solution.py:511
  26.9 5.2 %all-to-all-done.1 = bf16[128,16,128]{2,1,0:T(8,128)(2,1)S(1)} async-done(((bf16[128,16,128]{2,1,0:T(8,128)(2,1)}), bf16[128,16,128]{2,1,0:T(8,128)(2,1)S(1)}, u32[]{:S(2)}, u32[]{:S(2)}) %all-to-all-start.1) | async-done | bytes 524320 | tf_op jit(solution)/shard_map/all_to_all | solution.py:510
  32.1 5.6 %all-to-all-start = ((bf16[128,4,64,128]{3,2,1,0:T(8,128)(2,1)}), bf16[128,4,64,128]{3,2,1,0:T(8,128)(2,1)}, u32[]{:S(2)}, u32[]{:S(2)}) async-start(bf16[128,4,64,128]{3,2,1,0:T(8,128)(2,1)} %bitcast.86), calls=%async_computation | async-start | bytes 16777216 | tf_op jit(solution)/shard_map/all_to_all | solution.py:524
  38.3 0.3 fusion.7
  38.9 0.3 fusion.6
  39.3 1.1 gather_fusion
  40.4 0.6 fusion.20.member_ref
  41.1 0.5 copy.89
  42.7 0.7 copy.97
  43.7 0.7 reshape.297.bx.bb.bc
  45.0 0.8 reshape.291.wx.wb.wc
  45.9 0.7 broadcast_in_dim.54.dsk_ref
  46.8 0.6 iota_subtract_fusion.off_ref
  47.4 0.7 pad_convert_fusion.1
  48.1 0.8 fusion.26
  48.9 1.0 fusion.9.refs_1_.refs_3_
  49.9 0.7 broadcast_in_dim.45.tokw_ref
  50.6 0.7 broadcast_in_dim.50.rate_ref
  51.3 0.7 broadcast_in_dim.52.skip_ref
  52.3 0.7 reshape.287
  52.9 0.8 pad.35.tx.tb.tc
  54.0 1.0 copy.102
  55.0 18.6 %local_forward.1 = (f32[128,8192]{1,0:T(8,128)}, f32[128,1024]{1,0:T(8,128)}, f32[128,1024]{1,0:T(8,128)}, f32[128,8192]{1,0:T(8,128)}, f32[128,1024]{1,0:T(8,12...) custom-call(bf16[128,10240]{1,0:T(8,128)(2,1)} %cr.3, ...), custom_call_target="tpu_custom_call" | custom-call | bytes 95000000 | tf_op jit(solution)/shard_map/local_forward/pallas_call | solution.py:591
  73.6 70.4 %all-to-all-done.st_ref = bf16[128,4,64,128]{3,2,1,0:T(8,128)(2,1)} async-done(((bf16[128,4,64,128]{3,2,1,0:T(8,128)(2,1)}), bf16[128,4,64,128]{3,2,1,0:T(8,128)(2,1)}, u32[]{:S(2)}, u32[]{:S(2)}) %all-to-all-start) | async-done | bytes 8388640 | tf_op jit(solution)/shard_map/all_to_all | solution.py:524
  144.0 5.9 %all-to-all-start.2 = ((s16[32,128,128]{2,1,0:T(8,128)(2,1)}), s16[32,128,128]{2,1,0:T(8,128)(2,1)S(1)}, u32[]{:S(2)}, u32[]{:S(2)}) async-start(s16[32,128,128]{2,1,0:T(8,128)(2,1)} %get-tuple-element.84), calls=%async_computation.2 | async-start | bytes 2097152 | tf_op jit(solution)/shard_map/all_to_all | solution.py:607
  150.0 0.7 copy.108
  150.7 13.9 %norm_both_ways.1 = (bf16[128,8192]{1,0:T(8,128)(2,1)}, f32[128,8192]{1,0:T(8,128)}, s16[128,72,128]{2,1,0:T(8,128)(2,1)}, f32[8,8192]{1,0:T(8,128)}, f32[128,128]{1,0:T(8,128)}) custom-call(bf16[128,4,64,128]{3,2,1,0:T(8,128)(2,1)} %all-to-all-done.st_ref, f32[128,1024]{1,0:T(8,128)} %get-tuple-element.76.c_ref, f32[128,8192]{1,0:T(8,128)} %get-tuple-element.77.m0_ref, ...), custom_call_target="tpu_custom_call" | custom-call | bytes 52000000 | tf_op jit(solution)/shard_map/norm_both_ways/pallas_call | solution.py:608
  164.6 2.8 %all-to-all-done.2.refs_0_ = s16[32,128,128]{2,1,0:T(8,128)(2,1)S(1)} async-done(((s16[32,128,128]{2,1,0:T(8,128)(2,1)}), s16[32,128,128]{2,1,0:T(8,128)(2,1)S(1)}, u32[]{:S(2)}, u32[]{:S(2)}) %all-to-all-start.2) | async-done | bytes 1048608 | tf_op jit(solution)/shard_map/all_to_all | solution.py:607
  167.4 7.2 %all-to-all-start.3 = ((s16[128,72,128]{2,1,0:T(8,128)(2,1)}), s16[128,72,128]{2,1,0:T(8,128)(2,1)S(1)}, u32[]{:S(2)}, u32[]{:S(2)}) async-start(s16[128,72,128]{2,1,0:T(8,128)(2,1)} %get-tuple-element.104), calls=%async_computation.3 | async-start | bytes 4718592 | tf_op jit(solution)/shard_map/all_to_all | solution.py:622
  174.7 1.6 collective-permute-start.2
  176.2 1.2 collective-permute-start.1
  177.5 1.2 collective-permute-start
  178.7 30.9 %local_backward.1 = (bf16[128,8192]{1,0:T(8,128)(2,1)}, bf16[128,1024]{1,0:T(8,128)(2,1)}, bf16[128,1024]{1,0:T(8,128)(2,1)}, f32[128,128]{1,0:T(8,128)}, f32[128,24,128]{2,1,0:T(8,128)}) custom-call(bf16[128,4,64,128]{3,2,1,0:T(8,128)(2,1)} %all-to-all-done.st_ref, f32[128,8192]{1,0:T(8,128)} %get-tuple-element.85.dm_ref, ...), custom_call_target="tpu_custom_call" | custom-call | bytes 133000000 | tf_op jit(solution)/shard_map/local_backward/pallas_call | solution.py:624
  209.7 10.1 %all-to-all-start.4 = ((f32[128,24,128]{2,1,0:T(8,128)}), f32[128,24,128]{2,1,0:T(8,128)}, u32[]{:S(2)}, u32[]{:S(2)}) async-start(f32[128,24,128]{2,1,0:T(8,128)} %get-tuple-element.114), calls=%async_computation.4 | async-start | bytes 3145728 | tf_op jit(solution)/shard_map/all_to_all | solution.py:643
  219.7 0.7 copy.103
  220.5 5.7 %state_gradients_1.1.refs_4_ = f32[32,64,128]{2,1,0:T(8,128)} custom-call(s32[4,32]{1,0:T(4,128)} %gather_fusion, s32[512]{0:T(512)} %prompt_ref.5, s16[128,72,128]{2,1,0:T(8,128)(2,1)} %copy-done, s16[32,128,128]{2,1,0:T(8,128)(2,1)} %copy-done.1, f32[128,4,128]{2,1,0:T(4,128)} %fusion.9.refs_1_.refs_3_), custom_call_target="tpu_custom_call" | custom-call | bytes 15000000 | tf_op jit(solution)/shard_map/state_gradients_1/pallas_call | solution.py:646
  226.2 9.1 %state_gradients_3.1 = f32[32,64,128]{2,1,0:T(8,128)} custom-call(s32[4,32]{1,0:T(4,128)} %gather_fusion, s32[512]{0:T(512)} %prompt_ref.5, s16[128,72,128]{2,1,0:T(8,128)(2,1)} %copy-done, s16[32,128,128]{2,1,0:T(8,128)(2,1)} %collective-permute-done.refs_0_, s16[32,128,128]{2,1,0:T(8,128)(2,1)} %collective-permute-done.1.refs_1_, ...), custom_call_target="tpu_custom_call" | custom-call | bytes 45000000 | tf_op jit(solution)/shard_map/state_gradients_3/pallas_call | solution.py:646
  235.3 1.7 pad_maximum_fusion
  237.1 10.5 %all-to-all-done.4.back_ref = f32[128,24,128]{2,1,0:T(8,128)} async-done(((f32[128,24,128]{2,1,0:T(8,128)}), f32[128,24,128]{2,1,0:T(8,128)}, u32[]{:S(2)}, u32[]{:S(2)}) %all-to-all-start.4) | async-done | bytes 1572896 | tf_op jit(solution)/shard_map/all_to_all | solution.py:643
  247.5 2.7 %finish.1 = (f32[3,32,80]{2,1,0:T(8,128)}, f32[4,320]{1,0:T(4,128)}, f32[320]{0:T(512)}, f32[1,256]{1,0:T(1,128)}, f32[1,4]{1,0:T(1,128)}, /*index=5*/f32[1,4]{1,0:T(1,128)}, f32[1,4]{1,0:T(1,128)}) custom-call(f32[128,24,128]{2,1,0:T(8,128)} %all-to-all-done.4.back_ref, bf16[32,512]{1,0:T(8,128)(2,1)} %fusion.20.member_ref), custom_call_target="tpu_custom_call" | custom-call | bytes 10000000 | tf_op jit(solution)/shard_map/finish/pallas_call | solution.py:667
  (88 shorter events, 4.4 us)
Async XLA Ops:
  6.7 25.4 %all-to-all-start.1 = ((bf16[128,16,128]{2,1,0:T(8,128)(2,1)}), bf16[128,16,128]{2,1,0:T(8,128)(2,1)S(1)}, u32[]{:S(2)}, u32[]{:S(2)}) async-start(bf16[128,16,128]{2,1,0:T(8,128)(2,1)} %bitcast.47), calls=%async_computation.1 | async-start | bytes 1048576 | tf_op jit(solution)/shard_map/all_to_all | solution.py:510
  32.1 5.6 %copy-start.10 = (s32[512]{0:T(512)S(1)}, s32[512]{0:T(512)}, u32[]{:S(2)}) copy-start(s32[512]{0:T(512)} %prompt_ref.5) | copy-start | bytes 6148
  32.1 5.7 %copy-start.8 = (f32[128,128]{1,0:T(8,128)S(1)}, f32[128,128]{1,0:T(8,128)}, u32[]{:S(2)}) copy-start(f32[128,128]{1,0:T(8,128)} %param.18) | copy-start | bytes 196612
  32.1 5.9 %copy-start.11 = (f32[512]{0:T(512)S(1)}, f32[512]{0:T(512)}, u32[]{:S(2)}) copy-start(f32[512]{0:T(512)} %param.23) | copy-start | bytes 6148
  32.1 7.2 %copy-start.7 = (s32[4,32]{1,0:T(4,128)S(1)}, s32[4,32]{1,0:T(4,128)}, u32[]{:S(2)}) copy-start(s32[4,32]{1,0:T(4,128)} %constant.60.clone) | copy-start | bytes 1540
  32.1 111.9 %all-to-all-start = ((bf16[128,4,64,128]{3,2,1,0:T(8,128)(2,1)}), bf16[128,4,64,128]{3,2,1,0:T(8,128)(2,1)}, u32[]{:S(2)}, u32[]{:S(2)}) async-start(bf16[128,4,64,128]{3,2,1,0:T(8,128)(2,1)} %bitcast.86), calls=%async_computation | async-start | bytes 16777216 | tf_op jit(solution)/shard_map/all_to_all | solution.py:524
  37.7 4.1 %copy-start.12 = (s32[1,4]{1,0:T(1,128)S(1)}, s32[1,4]{1,0:T(1,128)}, u32[]{:S(2)}) copy-start(s32[1,4]{1,0:T(1,128)} %param.22) | copy-start | bytes 52
  42.6 12.4 %copy-start.3 = (bf16[384,16]{1,0:T(8,128)(2,1)}, bf16[384,16]{1,0:T(8,128)(2,1)S(1)}, u32[]{:S(2)}) copy-start(bf16[384,16]{1,0:T(8,128)(2,1)S(1)} %pad_convert_fusion.sel_ref) | copy-start | bytes 36868
  54.0 1.0 copy-start.4
  144.0 23.4 %all-to-all-start.2 = ((s16[32,128,128]{2,1,0:T(8,128)(2,1)}), s16[32,128,128]{2,1,0:T(8,128)(2,1)S(1)}, u32[]{:S(2)}, u32[]{:S(2)}) async-start(s16[32,128,128]{2,1,0:T(8,128)(2,1)} %get-tuple-element.84), calls=%async_computation.2 | async-start | bytes 2097152 | tf_op jit(solution)/shard_map/all_to_all | solution.py:607
  167.4 42.2 %copy-start.1 = (s16[32,128,128]{2,1,0:T(8,128)(2,1)}, s16[32,128,128]{2,1,0:T(8,128)(2,1)S(1)}, u32[]{:S(2)}) copy-start(s16[32,128,128]{2,1,0:T(8,128)(2,1)S(1)} %all-to-all-done.2.refs_0_) | copy-start | bytes 3145732
  167.4 42.2 %all-to-all-start.3 = ((s16[128,72,128]{2,1,0:T(8,128)(2,1)}), s16[128,72,128]{2,1,0:T(8,128)(2,1)S(1)}, u32[]{:S(2)}, u32[]{:S(2)}) async-start(s16[128,72,128]{2,1,0:T(8,128)(2,1)} %get-tuple-element.104), calls=%async_computation.3 | async-start | bytes 4718592 | tf_op jit(solution)/shard_map/all_to_all | solution.py:622
  174.7 51.5 %collective-permute-start.2 = (s16[32,128,128]{2,1,0:T(8,128)(2,1)S(1)}, s16[32,128,128]{2,1,0:T(8,128)(2,1)}, u32[]{:S(2)}, u32[]{:S(2)}) collective-permute-start(s16[32,128,128]{2,1,0:T(8,128)(2,1)S(1)} %all-to-all-done.2.refs_0_), channel_id=1, source_target_pairs={{0,8},{1,9},{2,10},{3,11},{4,12},{5,13},{6,14},{7,15},{8,0},{9,1},... | collective-permute-start | bytes 3145736 | tf_op jit(solution)/shard_map/ppermute | solution.py:621
  176.2 49.9 %collective-permute-start.1 = (s16[32,128,128]{2,1,0:T(8,128)(2,1)S(1)}, s16[32,128,128]{2,1,0:T(8,128)(2,1)}, u32[]{:S(2)}, u32[]{:S(2)}) collective-permute-start(s16[32,128,128]{2,1,0:T(8,128)(2,1)S(1)} %all-to-all-done.2.refs_0_), channel_id=1, source_target_pairs={{0,2},{1,3},{2,0},{3,1},{4,6},{5,7},{6,4},{7,5},{8,10},{9,11},{10,... | collective-permute-start | bytes 3145736 | tf_op jit(solution)/shard_map/ppermute | solution.py:621
  177.5 48.7 %collective-permute-start = (s16[32,128,128]{2,1,0:T(8,128)(2,1)S(1)}, s16[32,128,128]{2,1,0:T(8,128)(2,1)}, u32[]{:S(2)}, u32[]{:S(2)}) collective-permute-start(s16[32,128,128]{2,1,0:T(8,128)(2,1)S(1)} %all-to-all-done.2.refs_0_), channel_id=1, source_target_pairs={{0,1},{1,0},{2,3},{3,2},{4,5},{5,4},{6,7},{7,6},{8,9},{9,8},{10,11... | collective-permute-start | bytes 3145736 | tf_op jit(solution)/shard_map/ppermute | solution.py:621
  209.6 10.1 %copy-start.9 = (f32[128,128]{1,0:T(8,128)S(1)}, f32[128,128]{1,0:T(8,128)}, u32[]{:S(2)}) copy-start(f32[128,128]{1,0:T(8,128)} %get-tuple-element.109) | copy-start | bytes 196612
  209.6 10.8 %copy-start = (s16[128,72,128]{2,1,0:T(8,128)(2,1)}, s16[128,72,128]{2,1,0:T(8,128)(2,1)S(1)}, u32[]{:S(2)}) copy-start(s16[128,72,128]{2,1,0:T(8,128)(2,1)S(1)} %all-to-all-done.3.q_ref) | copy-start | bytes 7077892
  209.7 37.8 %all-to-all-start.4 = ((f32[128,24,128]{2,1,0:T(8,128)}), f32[128,24,128]{2,1,0:T(8,128)}, u32[]{:S(2)}, u32[]{:S(2)}) async-start(f32[128,24,128]{2,1,0:T(8,128)} %get-tuple-element.114), calls=%async_computation.4 | async-start | bytes 3145728 | tf_op jit(solution)/shard_map/all_to_all | solution.py:643
  226.2 9.2 %copy-start.2 = (bf16[128,8192]{1,0:T(8,128)(2,1)S(1)}, bf16[128,8192]{1,0:T(8,128)(2,1)}, u32[]{:S(2)}) copy-start(bf16[128,8192]{1,0:T(8,128)(2,1)} %get-tuple-element.105) | copy-start | bytes 6291460
  226.2 9.2 %copy-start.5 = (bf16[128,1024]{1,0:T(8,128)(2,1)S(1)}, bf16[128,1024]{1,0:T(8,128)(2,1)}, u32[]{:S(2)}) copy-start(bf16[128,1024]{1,0:T(8,128)(2,1)} %get-tuple-element.106) | copy-start | bytes 786436
  226.2 9.2 %copy-start.6 = (bf16[128,1024]{1,0:T(8,128)(2,1)S(1)}, bf16[128,1024]{1,0:T(8,128)(2,1)}, u32[]{:S(2)}) copy-start(bf16[128,1024]{1,0:T(8,128)(2,1)} %get-tuple-element.107) | copy-start | bytes 786436

commit v5 on v4

--- a/solution.py
+++ b/solution.py
@@ -21,7 +21,7 @@
 CONV = 10240
 PROMPTS = 32
 AHEAD = 128
-AT_ONCE = 8
+AT_ONCE = 16
 STEPS = 32752.0
 Q_ROWS = 72
 

time: 251 us -> 251 us (level)
  transfers between devices with their start and end apart: 8 -> 8, of which waited for: 4 -> 4; matrix products, arithmetic and copies ran while one was open for 8% -> 8% of each run, Pallas kernels for 35% -> 34%
where the time goes in v5:
time: 251 us; the launch traced here: 250 us
  waiting for transfers between devices  89.6 us (36%)
  Pallas kernels  88.9 us (35%)
  starting transfers between devices  44.3 us (18%)
  local copies, waits for them, and re-layouts  16.7 us (7%)
  other arithmetic  7.01 us (3%)
  matrix products  2.53 us (1%)
    all_to_all x1, waiting for transfers between devices, shards(): states = exchange(states.reshape(devices, DOCS, P_SIZE, N))  70.4 us
    pallas_call x1, Pallas kernels, shards(): call(back_kernel, (G,), [lead(HG, DOCS, P_SIZE, N), cols(T, GC), cols(T,...  30.9 us
    pallas_call x1, Pallas kernels, shards(): call(local_kernel, (G,), conv_specs + tail_specs + tap_specs + bias_specs...  18.6 us
    pallas_call x2, Pallas kernels, add_states(): pl.pallas_call(functools.partial(state_kernel, kinds), grid_spec=pltpu.Pr...  14.2 us
    pallas_call x1, Pallas kernels, shards(): call(norm_kernel, (4,), [lead(32, DOCS, P_SIZE, N), cols(T, 2 * N), cols(...  13.9 us
    all_to_all x1, starting transfers between devices, shards(): got = exchange(sent.reshape(devices, 16, 128)).reshape(devices, 2048)  11.5 us
    all_to_all x1, waiting for transfers between devices, shards(): back = exchange(back)  11.1 us
    all_to_all x1, starting transfers between devices, shards(): back = exchange(back)  10.1 us
  transfers between devices with their start and end apart: 8, of which 4 were waited for; matrix products, arithmetic and copies ran while one was open for 8% of the time, Pallas kernels for 34%

profile of v5, /device:TPU:1, one launch (start us, length us, event | category | flops | bytes accessed | tf_op | source)
XLA Modules:
  0.0 250.2 jit_solution(7587547719399320624)
XLA Ops:
  0.6 0.7 convert_bitcast_fusion
  1.3 0.8 reshape.283
  2.1 0.8 concatenate.12
  3.1 0.8 copy.87
  3.9 1.0 convolution_convert_fusion
  5.1 0.4 reshape.282
  5.8 0.9 copy.106
  6.7 11.5 %all-to-all-start.1 = ((bf16[128,16,128]{2,1,0:T(8,128)(2,1)}), bf16[128,16,128]{2,1,0:T(8,128)(2,1)S(1)}, u32[]{:S(2)}, u32[]{:S(2)}) async-start(bf16[128,16,128]{2,1,0:T(8,128)(2,1)} %bitcast.47), calls=%async_computation.1 | async-start | bytes 1048576 | tf_op jit(solution)/shard_map/all_to_all | solution.py:510
  18.2 8.6 %gather_states.1 = bf16[512,64,128]{2,1,0:T(8,128)(2,1)} custom-call(s32[512]{0:T(512)} %prompt_ref.5, bf16[32,64,128]{2,1,0:T(8,128)(2,1)} %bitcast.103), custom_call_target="tpu_custom_call" | custom-call | bytes 16000000 | tf_op jit(solution)/shard_map/gather_states/pallas_call | solution.py:511
  26.9 5.2 %all-to-all-done.1 = bf16[128,16,128]{2,1,0:T(8,128)(2,1)S(1)} async-done(((bf16[128,16,128]{2,1,0:T(8,128)(2,1)}), bf16[128,16,128]{2,1,0:T(8,128)(2,1)S(1)}, u32[]{:S(2)}, u32[]{:S(2)}) %all-to-all-start.1) | async-done | bytes 524320 | tf_op jit(solution)/shard_map/all_to_all | solution.py:510
  32.1 5.6 %all-to-all-start = ((bf16[128,4,64,128]{3,2,1,0:T(8,128)(2,1)}), bf16[128,4,64,128]{3,2,1,0:T(8,128)(2,1)}, u32[]{:S(2)}, u32[]{:S(2)}) async-start(bf16[128,4,64,128]{3,2,1,0:T(8,128)(2,1)} %bitcast.86), calls=%async_computation | async-start | bytes 16777216 | tf_op jit(solution)/shard_map/all_to_all | solution.py:524
  38.3 0.3 fusion.7
  38.9 0.3 fusion.6
  39.3 1.1 gather_fusion
  40.4 0.6 fusion.20.member_ref
  41.1 0.5 copy.89
  42.7 0.7 copy.97
  43.7 0.7 reshape.297.bx.bb.bc
  45.0 0.8 reshape.291.wx.wb.wc
  45.9 0.7 broadcast_in_dim.54.dsk_ref
  46.8 0.6 iota_subtract_fusion.off_ref
  47.4 0.7 pad_convert_fusion.1
  48.1 0.8 fusion.26
  48.9 1.0 fusion.9.refs_1_.refs_3_
  49.9 0.7 broadcast_in_dim.45.tokw_ref
  50.6 0.7 broadcast_in_dim.50.rate_ref
  51.3 0.7 broadcast_in_dim.52.skip_ref
  52.3 0.7 reshape.287
  52.9 0.8 pad.35.tx.tb.tc
  54.0 1.0 copy.102
  55.0 18.6 %local_forward.1 = (f32[128,8192]{1,0:T(8,128)}, f32[128,1024]{1,0:T(8,128)}, f32[128,1024]{1,0:T(8,128)}, f32[128,8192]{1,0:T(8,128)}, f32[128,1024]{1,0:T(8,12...) custom-call(bf16[128,10240]{1,0:T(8,128)(2,1)} %cr.3, ...), custom_call_target="tpu_custom_call" | custom-call | bytes 95000000 | tf_op jit(solution)/shard_map/local_forward/pallas_call | solution.py:591
  73.6 70.4 %all-to-all-done.st_ref = bf16[128,4,64,128]{3,2,1,0:T(8,128)(2,1)} async-done(((bf16[128,4,64,128]{3,2,1,0:T(8,128)(2,1)}), bf16[128,4,64,128]{3,2,1,0:T(8,128)(2,1)}, u32[]{:S(2)}, u32[]{:S(2)}) %all-to-all-start) | async-done | bytes 8388640 | tf_op jit(solution)/shard_map/all_to_all | solution.py:524
  144.0 5.9 %all-to-all-start.2 = ((s16[32,128,128]{2,1,0:T(8,128)(2,1)}), s16[32,128,128]{2,1,0:T(8,128)(2,1)S(1)}, u32[]{:S(2)}, u32[]{:S(2)}) async-start(s16[32,128,128]{2,1,0:T(8,128)(2,1)} %get-tuple-element.84), calls=%async_computation.2 | async-start | bytes 2097152 | tf_op jit(solution)/shard_map/all_to_all | solution.py:607
  150.0 0.7 copy.108
  150.7 13.9 %norm_both_ways.1 = (bf16[128,8192]{1,0:T(8,128)(2,1)}, f32[128,8192]{1,0:T(8,128)}, s16[128,72,128]{2,1,0:T(8,128)(2,1)}, f32[8,8192]{1,0:T(8,128)}, f32[128,128]{1,0:T(8,128)}) custom-call(bf16[128,4,64,128]{3,2,1,0:T(8,128)(2,1)} %all-to-all-done.st_ref, f32[128,1024]{1,0:T(8,128)} %get-tuple-element.76.c_ref, f32[128,8192]{1,0:T(8,128)} %get-tuple-element.77.m0_ref, ...), custom_call_target="tpu_custom_call" | custom-call | bytes 52000000 | tf_op jit(solution)/shard_map/norm_both_ways/pallas_call | solution.py:608
  164.6 2.8 %all-to-all-done.2.refs_0_ = s16[32,128,128]{2,1,0:T(8,128)(2,1)S(1)} async-done(((s16[32,128,128]{2,1,0:T(8,128)(2,1)}), s16[32,128,128]{2,1,0:T(8,128)(2,1)S(1)}, u32[]{:S(2)}, u32[]{:S(2)}) %all-to-all-start.2) | async-done | bytes 1048608 | tf_op jit(solution)/shard_map/all_to_all | solution.py:607
  167.4 7.2 %all-to-all-start.3 = ((s16[128,72,128]{2,1,0:T(8,128)(2,1)}), s16[128,72,128]{2,1,0:T(8,128)(2,1)S(1)}, u32[]{:S(2)}, u32[]{:S(2)}) async-start(s16[128,72,128]{2,1,0:T(8,128)(2,1)} %get-tuple-element.104), calls=%async_computation.3 | async-start | bytes 4718592 | tf_op jit(solution)/shard_map/all_to_all | solution.py:622
  174.7 1.6 collective-permute-start.2
  176.2 1.2 collective-permute-start.1
  177.5 1.2 collective-permute-start
  178.7 30.9 %local_backward.1 = (bf16[128,8192]{1,0:T(8,128)(2,1)}, bf16[128,1024]{1,0:T(8,128)(2,1)}, bf16[128,1024]{1,0:T(8,128)(2,1)}, f32[128,128]{1,0:T(8,128)}, f32[128,24,128]{2,1,0:T(8,128)}) custom-call(bf16[128,4,64,128]{3,2,1,0:T(8,128)(2,1)} %all-to-all-done.st_ref, f32[128,8192]{1,0:T(8,128)} %get-tuple-element.85.dm_ref, ...), custom_call_target="tpu_custom_call" | custom-call | bytes 133000000 | tf_op jit(solution)/shard_map/local_backward/pallas_call | solution.py:624
  209.7 10.1 %all-to-all-start.4 = ((f32[128,24,128]{2,1,0:T(8,128)}), f32[128,24,128]{2,1,0:T(8,128)}, u32[]{:S(2)}, u32[]{:S(2)}) async-start(f32[128,24,128]{2,1,0:T(8,128)} %get-tuple-element.114), calls=%async_computation.4 | async-start | bytes 3145728 | tf_op jit(solution)/shard_map/all_to_all | solution.py:643
  219.7 0.7 copy.103
  220.5 5.3 %state_gradients_1.1.refs_4_ = f32[32,64,128]{2,1,0:T(8,128)} custom-call(s32[4,32]{1,0:T(4,128)} %gather_fusion, s32[512]{0:T(512)} %prompt_ref.5, s16[128,72,128]{2,1,0:T(8,128)(2,1)} %copy-done, s16[32,128,128]{2,1,0:T(8,128)(2,1)} %copy-done.1, f32[128,4,128]{2,1,0:T(4,128)} %fusion.9.refs_1_.refs_3_), custom_call_target="tpu_custom_call" | custom-call | bytes 15000000 | tf_op jit(solution)/shard_map/state_gradients_1/pallas_call | solution.py:646
  225.9 8.8 %state_gradients_3.1 = f32[32,64,128]{2,1,0:T(8,128)} custom-call(s32[4,32]{1,0:T(4,128)} %gather_fusion, s32[512]{0:T(512)} %prompt_ref.5, s16[128,72,128]{2,1,0:T(8,128)(2,1)} %copy-done, s16[32,128,128]{2,1,0:T(8,128)(2,1)} %collective-permute-done.refs_0_, s16[32,128,128]{2,1,0:T(8,128)(2,1)} %collective-permute-done.1.refs_1_, ...), custom_call_target="tpu_custom_call" | custom-call | bytes 45000000 | tf_op jit(solution)/shard_map/state_gradients_3/pallas_call | solution.py:646
  234.7 1.7 pad_maximum_fusion
  236.4 11.1 %all-to-all-done.4.back_ref = f32[128,24,128]{2,1,0:T(8,128)} async-done(((f32[128,24,128]{2,1,0:T(8,128)}), f32[128,24,128]{2,1,0:T(8,128)}, u32[]{:S(2)}, u32[]{:S(2)}) %all-to-all-start.4) | async-done | bytes 1572896 | tf_op jit(solution)/shard_map/all_to_all | solution.py:643
  247.5 2.7 %finish.1 = (f32[3,32,80]{2,1,0:T(8,128)}, f32[4,320]{1,0:T(4,128)}, f32[320]{0:T(512)}, f32[1,256]{1,0:T(1,128)}, f32[1,4]{1,0:T(1,128)}, /*index=5*/f32[1,4]{1,0:T(1,128)}, f32[1,4]{1,0:T(1,128)}) custom-call(f32[128,24,128]{2,1,0:T(8,128)} %all-to-all-done.4.back_ref, bf16[32,512]{1,0:T(8,128)(2,1)} %fusion.20.member_ref), custom_call_target="tpu_custom_call" | custom-call | bytes 10000000 | tf_op jit(solution)/shard_map/finish/pallas_call | solution.py:667
  (88 shorter events, 4.4 us)
Async XLA Ops:
  6.7 25.4 %all-to-all-start.1 = ((bf16[128,16,128]{2,1,0:T(8,128)(2,1)}), bf16[128,16,128]{2,1,0:T(8,128)(2,1)S(1)}, u32[]{:S(2)}, u32[]{:S(2)}) async-start(bf16[128,16,128]{2,1,0:T(8,128)(2,1)} %bitcast.47), calls=%async_computation.1 | async-start | bytes 1048576 | tf_op jit(solution)/shard_map/all_to_all | solution.py:510
  32.1 5.6 %copy-start.10 = (s32[512]{0:T(512)S(1)}, s32[512]{0:T(512)}, u32[]{:S(2)}) copy-start(s32[512]{0:T(512)} %prompt_ref.5) | copy-start | bytes 6148
  32.1 5.7 %copy-start.8 = (f32[128,128]{1,0:T(8,128)S(1)}, f32[128,128]{1,0:T(8,128)}, u32[]{:S(2)}) copy-start(f32[128,128]{1,0:T(8,128)} %param.18) | copy-start | bytes 196612
  32.1 5.9 %copy-start.11 = (f32[512]{0:T(512)S(1)}, f32[512]{0:T(512)}, u32[]{:S(2)}) copy-start(f32[512]{0:T(512)} %param.23) | copy-start | bytes 6148
  32.1 7.2 %copy-start.7 = (s32[4,32]{1,0:T(4,128)S(1)}, s32[4,32]{1,0:T(4,128)}, u32[]{:S(2)}) copy-start(s32[4,32]{1,0:T(4,128)} %constant.60.clone) | copy-start | bytes 1540
  32.1 111.9 %all-to-all-start = ((bf16[128,4,64,128]{3,2,1,0:T(8,128)(2,1)}), bf16[128,4,64,128]{3,2,1,0:T(8,128)(2,1)}, u32[]{:S(2)}, u32[]{:S(2)}) async-start(bf16[128,4,64,128]{3,2,1,0:T(8,128)(2,1)} %bitcast.86), calls=%async_computation | async-start | bytes 16777216 | tf_op jit(solution)/shard_map/all_to_all | solution.py:524
  37.7 4.1 %copy-start.12 = (s32[1,4]{1,0:T(1,128)S(1)}, s32[1,4]{1,0:T(1,128)}, u32[]{:S(2)}) copy-start(s32[1,4]{1,0:T(1,128)} %param.22) | copy-start | bytes 52
  42.6 12.4 %copy-start.3 = (bf16[384,16]{1,0:T(8,128)(2,1)}, bf16[384,16]{1,0:T(8,128)(2,1)S(1)}, u32[]{:S(2)}) copy-start(bf16[384,16]{1,0:T(8,128)(2,1)S(1)} %pad_convert_fusion.sel_ref) | copy-start | bytes 36868
  54.0 1.0 copy-start.4
  144.0 23.4 %all-to-all-start.2 = ((s16[32,128,128]{2,1,0:T(8,128)(2,1)}), s16[32,128,128]{2,1,0:T(8,128)(2,1)S(1)}, u32[]{:S(2)}, u32[]{:S(2)}) async-start(s16[32,128,128]{2,1,0:T(8,128)(2,1)} %get-tuple-element.84), calls=%async_computation.2 | async-start | bytes 2097152 | tf_op jit(solution)/shard_map/all_to_all | solution.py:607
  167.4 42.2 %copy-start.1 = (s16[32,128,128]{2,1,0:T(8,128)(2,1)}, s16[32,128,128]{2,1,0:T(8,128)(2,1)S(1)}, u32[]{:S(2)}) copy-start(s16[32,128,128]{2,1,0:T(8,128)(2,1)S(1)} %all-to-all-done.2.refs_0_) | copy-start | bytes 3145732
  167.4 42.2 %all-to-all-start.3 = ((s16[128,72,128]{2,1,0:T(8,128)(2,1)}), s16[128,72,128]{2,1,0:T(8,128)(2,1)S(1)}, u32[]{:S(2)}, u32[]{:S(2)}) async-start(s16[128,72,128]{2,1,0:T(8,128)(2,1)} %get-tuple-element.104), calls=%async_computation.3 | async-start | bytes 4718592 | tf_op jit(solution)/shard_map/all_to_all | solution.py:622
  174.7 51.2 %collective-permute-start.2 = (s16[32,128,128]{2,1,0:T(8,128)(2,1)S(1)}, s16[32,128,128]{2,1,0:T(8,128)(2,1)}, u32[]{:S(2)}, u32[]{:S(2)}) collective-permute-start(s16[32,128,128]{2,1,0:T(8,128)(2,1)S(1)} %all-to-all-done.2.refs_0_), channel_id=1, source_target_pairs={{0,8},{1,9},{2,10},{3,11},{4,12},{5,13},{6,14},{7,15},{8,0},{9,1},... | collective-permute-start | bytes 3145736 | tf_op jit(solution)/shard_map/ppermute | solution.py:621
  176.2 49.6 %collective-permute-start.1 = (s16[32,128,128]{2,1,0:T(8,128)(2,1)S(1)}, s16[32,128,128]{2,1,0:T(8,128)(2,1)}, u32[]{:S(2)}, u32[]{:S(2)}) collective-permute-start(s16[32,128,128]{2,1,0:T(8,128)(2,1)S(1)} %all-to-all-done.2.refs_0_), channel_id=1, source_target_pairs={{0,2},{1,3},{2,0},{3,1},{4,6},{5,7},{6,4},{7,5},{8,10},{9,11},{10,... | collective-permute-start | bytes 3145736 | tf_op jit(solution)/shard_map/ppermute | solution.py:621
  177.5 48.4 %collective-permute-start = (s16[32,128,128]{2,1,0:T(8,128)(2,1)S(1)}, s16[32,128,128]{2,1,0:T(8,128)(2,1)}, u32[]{:S(2)}, u32[]{:S(2)}) collective-permute-start(s16[32,128,128]{2,1,0:T(8,128)(2,1)S(1)} %all-to-all-done.2.refs_0_), channel_id=1, source_target_pairs={{0,1},{1,0},{2,3},{3,2},{4,5},{5,4},{6,7},{7,6},{8,9},{9,8},{10,11... | collective-permute-start | bytes 3145736 | tf_op jit(solution)/shard_map/ppermute | solution.py:621
  209.6 10.1 %copy-start.9 = (f32[128,128]{1,0:T(8,128)S(1)}, f32[128,128]{1,0:T(8,128)}, u32[]{:S(2)}) copy-start(f32[128,128]{1,0:T(8,128)} %get-tuple-element.109) | copy-start | bytes 196612
  209.6 10.8 %copy-start = (s16[128,72,128]{2,1,0:T(8,128)(2,1)}, s16[128,72,128]{2,1,0:T(8,128)(2,1)S(1)}, u32[]{:S(2)}) copy-start(s16[128,72,128]{2,1,0:T(8,128)(2,1)S(1)} %all-to-all-done.3.q_ref) | copy-start | bytes 7077892
  209.7 37.8 %all-to-all-start.4 = ((f32[128,24,128]{2,1,0:T(8,128)}), f32[128,24,128]{2,1,0:T(8,128)}, u32[]{:S(2)}, u32[]{:S(2)}) async-start(f32[128,24,128]{2,1,0:T(8,128)} %get-tuple-element.114), calls=%async_computation.4 | async-start | bytes 3145728 | tf_op jit(solution)/shard_map/all_to_all | solution.py:643
  225.8 8.9 %copy-start.2 = (bf16[128,8192]{1,0:T(8,128)(2,1)S(1)}, bf16[128,8192]{1,0:T(8,128)(2,1)}, u32[]{:S(2)}) copy-start(bf16[128,8192]{1,0:T(8,128)(2,1)} %get-tuple-element.105) | copy-start | bytes 6291460
  225.8 8.9 %copy-start.5 = (bf16[128,1024]{1,0:T(8,128)(2,1)S(1)}, bf16[128,1024]{1,0:T(8,128)(2,1)}, u32[]{:S(2)}) copy-start(bf16[128,1024]{1,0:T(8,128)(2,1)} %get-tuple-element.106) | copy-start | bytes 786436
  225.8 8.9 %copy-start.6 = (bf16[128,1024]{1,0:T(8,128)(2,1)S(1)}, bf16[128,1024]{1,0:T(8,128)(2,1)}, u32[]{:S(2)}) copy-start(bf16[128,1024]{1,0:T(8,128)(2,1)} %get-tuple-element.107) | copy-start | bytes 786436
